TPU v7x, 256 devices: a whole 4x4x8 slice. The times are simulated.
256 devices in a mesh: seq: 8 (over z_hi, x), res: 32 (over z_lo, y, core).
Axes of the slice: x: 4, y: 4, z: 8 (z_hi: 2, z_lo: 4; z = z_hi * 4 + z_lo), core: 2. Of those that a mesh axis runs over, the one named last changes fastest.
Arguments:
- alignment_embeddings: bfloat16 [64, 1024, 768], P('seq', 'res'), may hold values from -6 to 6
- standardize_gain: float32 [768], replicated, may hold values from 0.5 to 1.5
- asking_projection: bfloat16 [768, 768], replicated
- lookup_projection: bfloat16 [768, 768], replicated, may hold values from -0.21875 to 0.21875
- content_projection: bfloat16 [768, 768], replicated, may hold values from -0.21875 to 0.21875
- final_projection: bfloat16 [768, 768], replicated, may hold values from -0.21875 to 0.21875
Outputs:
- updated: bfloat16 [64, 1024, 768], P('seq', 'res')
All inputs are finite; a program needn't handle non-finite values.
Results may differ from a plain program's by a relative error of at most 0.012.
The roundings to bfloat16 on the way count: a program that leaves them out, or rounds other values in their place, can miss the bound.
Values may be sent and summed in bfloat16 or wider, within the bound.
No kernel may reach another device: no remote copies, remote signals or barrier semaphores. Data moves between devices by JAX's collectives and lax.ppermute only.
A program may use at most 128 MiB of HBM per device.

v0:
```python
import jax
import jax.numpy as jnp
from jax import lax
from jax.sharding import PartitionSpec as P

HEADS = 12
HEAD_SIZE = 64


def per_device(
    alignment_embeddings,
    standardize_gain,
    asking_projection,
    lookup_projection,
    content_projection,
    final_projection,
):
    alignment_member, alignment_members, embed_dimension = alignment_embeddings.shape
    heads = HEADS
    size = HEAD_SIZE
    broad_arrangement = alignment_embeddings.astype(jnp.float32)
    mean = jnp.mean(broad_arrangement, axis=-1, keepdims=True)
    var = jnp.mean((broad_arrangement - mean) ** 2, axis=-1, keepdims=True)
    normed = ((broad_arrangement - mean) / jnp.sqrt(var + 1e-05) * standardize_gain).astype(
        jnp.bfloat16
    )
    flat = normed.reshape(alignment_member * alignment_members, embed_dimension)
    query = jnp.dot(flat, asking_projection, preferred_element_type=jnp.float32).astype(
        jnp.bfloat16
    )
    query = query.reshape(alignment_member, alignment_members, heads, size)
    key = (
        jnp.dot(flat, lookup_projection, preferred_element_type=jnp.float32)
        .astype(jnp.bfloat16)
        .reshape(alignment_member, alignment_members, embed_dimension)
    )
    value = (
        jnp.dot(flat, content_projection, preferred_element_type=jnp.float32)
        .astype(jnp.bfloat16)
        .reshape(alignment_member, alignment_members, embed_dimension)
    )
    scale = size ** (-0.5) / jnp.sqrt(jnp.float32(alignment_member * lax.axis_size("seq")))
    key_all, value_all = (
        lax.all_gather(key, "res", axis=1, tiled=True),
        lax.all_gather(value, "res", axis=1, tiled=True),
    )
    block = key_all.reshape(alignment_member, key_all.shape[1], heads, size)
    partial_value = jnp.einsum("sihd,sjhd->hij", query, block, preferred_element_type=jnp.float32)
    total = lax.psum(partial_value, "seq")
    probs = jax.nn.softmax(total * scale, axis=-1).astype(jnp.bfloat16)
    value_blocks = value_all.reshape(alignment_member, value_all.shape[1], heads, size)
    context = jnp.einsum("hij,sjhd->sihd", probs, value_blocks, preferred_element_type=jnp.float32)
    context = context.astype(jnp.bfloat16).reshape(
        alignment_member * alignment_members, embed_dimension
    )
    mixed = jnp.dot(context, final_projection, preferred_element_type=jnp.float32)
    return (
        broad_arrangement + mixed.reshape(alignment_member, alignment_members, embed_dimension)
    ).astype(jnp.bfloat16)


def solution(mesh):
    placed = (P("seq", "res", None), P(), P(), P(), P(), P())
    return jax.shard_map(
        per_device, mesh=mesh, in_specs=placed, out_specs=P("seq", "res", None), check_vma=False
    )
```

profile of v0, /device:TPU:6, one launch (start us, length us, event | category | flops | bytes accessed | tf_op | source)
XLA Modules:
  0.0 323.2 jit_solution(3761407535720846166)
XLA Ops:
  6.5 0.0 copy-start
  6.5 0.0 all-gather.5.cloned.1.call-start
  6.5 1.2 convert_reduce_fusion
  7.8 1.2 fusion.21
  9.0 1.2 fusion.23
  10.2 0.0 copy-done
  10.2 0.0 copy-start.2
  10.3 0.5 convolution_convert_fusion
  10.7 1.0 copy.16
  11.8 0.0 all-gather.5.cloned.1.call-update
  11.8 0.0 all-gather.3.cloned.1.call-start
  11.8 0.0 copy-done.2
  11.8 0.5 convolution_convert_fusion.2
  12.3 1.0 copy.14
  13.3 0.0 all-gather.3.cloned.1.call-update
  13.3 0.0 all-reduce.2.cloned.1.call-start
  13.4 1.7 convolution_convert_fusion.1
  15.1 0.6 reshape.40
  15.7 78.4 %all-gather.5.cloned.1.call-done = bf16[8,1024,768]{2,0,1:T(8,128)(2,1)} async-done(((bf16[8,32,768]{2,0,1:T(8,128)(2,1)}), bf16[8,1024,768]{2,0,1:T(8,128)(2,1)}) %all-gather.5.cloned.1.call-update) | async-done | bytes 12582928 | tf_op jit(solution)/shard_map/all_gather | solution.py:44
  94.1 16.7 %copy.17 = bf16[8,1024,768]{1,2,0:T(8,128)(2,1)} copy(bf16[8,1024,768]{2,0,1:T(8,128)(2,1)} %all-gather.5.cloned.1.call-done) | data formatting | bytes 25165824 | tf_op jit(solution)/shard_map/all_gather | solution.py:44
  110.8 8.3 %fusion.7 = f32[12,32,1024]{2,1,0:T(8,128)} fusion(bf16[8,1024,12,64]{1,3,2,0:T(8,128)(2,1)} %bitcast.26, bf16[8,32,12,64]{3,2,1,0:T(8,128)(2,1)S(1)} %reshape.40), kind=kOutput, calls=%fused_computation.8 | convolution fusion | flops 402653184 | bytes 14548992 | tf_op jit(solution)/shard_map/sihd,sjhd->hij/dot_general | solution.py:48
  119.1 0.0 all-reduce.2.cloned.1.call-update
  119.1 56.4 %all-gather.3.cloned.1.call-done = bf16[8,1024,768]{2,0,1:T(8,128)(2,1)} async-done(((bf16[8,32,768]{2,0,1:T(8,128)(2,1)}), bf16[8,1024,768]{2,0,1:T(8,128)(2,1)}) %all-gather.3.cloned.1.call-update) | async-done | bytes 12582928 | tf_op jit(solution)/shard_map/all_gather | solution.py:45
  175.5 16.5 %copy.15 = bf16[8,1024,768]{1,2,0:T(8,128)(2,1)} copy(bf16[8,1024,768]{2,0,1:T(8,128)(2,1)} %all-gather.3.cloned.1.call-done) | data formatting | bytes 25165824 | tf_op jit(solution)/shard_map/all_gather | solution.py:45
  192.1 109.6 %all-reduce.2.cloned.1.call-done = f32[12,32,1024]{2,1,0:T(8,128)} async-done(((f32[12,32,1024]{2,1,0:T(8,128)}), f32[12,32,1024]{2,1,0:T(8,128)}) %all-reduce.2.cloned.1.call-update) | async-done | bytes 1572880 | tf_op jit(solution)/shard_map/psum | solution.py:49
  301.6 1.9 fusion.35
  303.5 9.5 %fusion.14 = bf16[8,32,12,64]{3,1,0,2:T(8,128)(2,1)S(1)} fusion(bf16[8,1024,12,64]{1,3,2,0:T(8,128)(2,1)} %bitcast.25, f32[12,32]{1,0:T(8,128)S(1)} %fusion.35, f32[12,32,1024]{2,1,0:T(8,128)} %all-reduce.2.cloned.1.call-done), kind=kOutput, calls=%fused_computation.12 | convolution fusion | flops 404424064 | bytes 14550528 | tf_op jit(solution)/shard_map/hij,sjhd->sihd/dot_general | solution.py:52
  313.0 0.0 copy-start.1
  313.0 0.5 copy.21
  313.6 0.6 dot_general.25
  314.2 0.0 copy-done.1
  314.2 2.5 fusion.17
  (2 shorter events, 0.0 us)
Async XLA Ops:
  6.5 3.7 %copy-start = (bf16[768,768]{1,0:T(8,128)(2,1)S(1)}, bf16[768,768]{1,0:T(8,128)(2,1)}, u32[]{:S(2)}) copy-start(bf16[768,768]{1,0:T(8,128)(2,1)} %param.9) | copy-start | bytes 3538948
  6.5 87.6 %all-gather.5.cloned.1.call-start = ((), (), s32[]{:S(2)}) async-start(), calls=%async_computation.1 | async-start | bytes 12976128 | tf_op jit(solution)/shard_map/all_gather | solution.py:44
  10.2 1.6 copy-start.2
  11.8 163.7 %all-gather.3.cloned.1.call-start = ((), (), s32[]{:S(2)}) async-start(), calls=%async_computation | async-start | bytes 12976128 | tf_op jit(solution)/shard_map/all_gather | solution.py:45
  13.3 288.3 %all-reduce.2.cloned.1.call-start = ((), (), s32[]{:S(2)}) async-start(), calls=%async_computation.2 | async-start | bytes 3145728 | tf_op jit(solution)/shard_map/psum | solution.py:49
  313.0 1.2 copy-start.1
Sparse Core Ops, SparseCore 0:
  11.9 82.1 all-gather.4
  96.0 79.5 all-gather.2
  178.2 123.4 all-reduce.1
where the time goes:
time: 324 us; the launch traced here: 323 us
  waiting for transfers between devices  244 us (75%)
  local copies, waits for them, and re-layouts  37 us (11%)
  matrix products  23 us (7%)
  between operations  13.2 us (4%)
  other arithmetic  5.56 us (2%)
    psum x1, waiting for transfers between devices, per_device(): total = lax.psum(partial_value, 'seq')  110 us
    all_gather x1, waiting for transfers between devices, per_device(): lax.all_gather(key, 'res', axis=1, tiled=True)  78.4 us
    all_gather x1, waiting for transfers between devices, per_device(): lax.all_gather(value, 'res', axis=1, tiled=True)  56.4 us
    all_gather x1, local copies, waits for them, and re-layouts, per_device(): lax.all_gather(key, 'res', axis=1, tiled=True)  16.7 us
    all_gather x1, local copies, waits for them, and re-layouts, per_device(): lax.all_gather(value, 'res', axis=1, tiled=True)  16.5 us
    dot_general x1, matrix products, per_device(): jnp.einsum('hij,sjhd->sihd', probs, value_blocks, preferred_element_type=...  9.45 us
    dot_general x1, matrix products, per_device(): jnp.einsum('sihd,sjhd->hij', query, block, preferred_element_type=jnp.flo...  8.3 us
  transfers between devices with their start and end apart: 3, of which 3 were waited for; matrix products, arithmetic and copies ran while one was open for 14% of the time, Pallas kernels for 0%

commit v1 on v0

v1 whole, which is shorter than its diff:
```python
import functools

import jax
import jax.numpy as jnp
from jax import lax
from jax.experimental import pallas as pl
from jax.experimental.pallas import tpu as pltpu
from jax.sharding import Mesh
from jax.sharding import PartitionSpec as P

HEADS = 12
SIZE = 64
GROUPS = 4
OWN = HEADS // GROUPS
F32, BF16 = jnp.float32, jnp.bfloat16
LINE = [[(i, i ^ m) for i in range(4)] for m in range(4)]
RING = [[(i, (i + k) % 4) for i in range(4)] for k in range(4)]
VMEM = pl.BlockSpec(memory_space=pltpu.VMEM)
LIMIT = 48 * 1024 * 1024


def call(body, outs, scratch=(), flops=1000000, moved=1000000):
    def run(*args):
        return pl.pallas_call(
            body,
            out_shape=[jax.ShapeDtypeStruct(s, d) for s, d in outs],
            in_specs=[VMEM] * len(args),
            out_specs=[VMEM] * len(outs),
            scratch_shapes=list(scratch),
            compiler_params=pltpu.CompilerParams(vmem_limit_bytes=LIMIT),
            cost_estimate=pl.CostEstimate(
                flops=flops, bytes_accessed=moved, transcendentals=0
            ),
        )(*args)

    return run


def pack(full, store):
    parts = full.reshape(4, 2, 32, HEADS * SIZE)
    even, odd = parts[:, 0].reshape(128, -1), parts[:, 1].reshape(128, -1)
    for n in range(HEADS // 2):
        a, b = even[:, n * 128 : n * 128 + 128], odd[:, n * 128 : n * 128 + 128]
        store(2 * n, jnp.concatenate([a[:, :64], b[:, :64]], axis=1).astype(BF16))
        store(2 * n + 1, jnp.concatenate([a[:, 64:], b[:, 64:]], axis=1).astype(BF16))


def key_kernel(x_ref, gain_ref, w_ref, normed_ref, o0, o1, o2, o3, held):
    x = x_ref[...].astype(F32)
    mean = jnp.mean(x, axis=-1, keepdims=True)
    off = x - mean
    var = jnp.mean(off * off, axis=-1, keepdims=True)
    normed = (off / jnp.sqrt(var + 1e-05) * gain_ref[...]).astype(BF16)
    normed_ref[...] = normed
    full = jnp.dot(normed, w_ref[...], preferred_element_type=F32)

    def store(h, block):
        held[h // OWN, (h % OWN) * 128 : (h % OWN) * 128 + 128, :] = block

    pack(full, store)
    me = lax.axis_index("zl")
    for m, out in enumerate((o0, o1, o2, o3)):
        out[...] = held[jnp.bitwise_xor(me, m)]


def query_value_kernel(normed_ref, wq_ref, wv_ref, o0, o1, o2, o3, held):
    normed = normed_ref[...]
    for part, w_ref in enumerate((wq_ref, wv_ref)):
        full = jnp.dot(normed, w_ref[...], preferred_element_type=F32)

        def store(h, block, part=part):
            row = part * 384 + (h % OWN) * 128
            held[h // OWN, row : row + 128, :] = block

        pack(full, store)
    me = lax.axis_index("zl")
    for m, out in enumerate((o0, o1, o2, o3)):
        out[...] = held[jnp.bitwise_xor(me, m)]


def slab_kernel(base, p0, p1, p2, p3, slab):
    for m, piece in enumerate((p0, p1, p2, p3)):
        for h in range(OWN):
            for sp in range(4):
                row = base + h * 128 + sp * 32
                slab[h * 128 + m * 32 : h * 128 + m * 32 + 32, sp * 128 : sp * 128 + 128] = (
                    piece[row : row + 32, :]
                )


def logits_kernel(*refs):
    pieces, slabs = refs[:4], refs[4:12]
    own, others, held = refs[12], refs[13:16], refs[16]
    me = lax.axis_index("x")
    for m, piece in enumerate(pieces):
        at = lax.rem(m - me + 4, 4)
        for h in range(OWN):
            for sp in range(4):
                row = h * 128 + sp * 32
                held[h, at, :, sp * 128 : sp * 128 + 128] = piece[row : row + 32, :]
    for h in range(OWN):
        query = held[h].reshape(128, 512)
        for j, slab in enumerate(slabs):
            part = lax.dot_general(
                query,
                slab[h * 128 : h * 128 + 128, :],
                (((1,), (1,)), ((), ())),
                preferred_element_type=F32,
            )
            cols = slice(j * 128, j * 128 + 128)
            own[h * 32 : h * 32 + 32, cols] = part[:32]
            for k, out in enumerate(others):
                out[h * 32 : h * 32 + 32, cols] = part[k * 32 + 32 : k * 32 + 64].astype(BF16)


def sum_kernel(own, r1, r2, r3, total, sent):
    s = own[...] + r1[...].astype(F32) + r2[...].astype(F32) + r3[...].astype(F32)
    total[...] = s
    sent[...] = s.astype(BF16)


def softmax_kernel(scale, total, other, probs):
    logits = (total[...] + other[...].astype(F32)) * scale
    top = jnp.max(logits, axis=-1, keepdims=True)
    e = jnp.exp(logits - top)
    probs[...] = (e / jnp.sum(e, axis=-1, keepdims=True)).astype(BF16)


def context_kernel(*refs):
    probs, slabs, outs, held = refs[:4], refs[4:12], refs[12:16], refs[16]
    me = lax.axis_index("x")
    for k, piece in enumerate(probs):
        at = lax.rem(me - k + 4, 4)
        for h in range(OWN):
            held[h, at] = piece[h * 32 : h * 32 + 32, :]
    for h in range(OWN):
        p = held[h].reshape(128, 1024)
        total = None
        for j, slab in enumerate(slabs):
            part = jnp.dot(
                p[:, j * 128 : j * 128 + 128],
                slab[h * 128 : h * 128 + 128, :],
                preferred_element_type=F32,
            )
            total = part if total is None else total + part
        total = total.astype(BF16)
        for m, out in enumerate(outs):
            for sp in range(4):
                row = h * 128 + sp * 32
                out[row : row + 32, :] = total[
                    m * 32 : m * 32 + 32, sp * 128 : sp * 128 + 128
                ]


def out_kernel(c0, c1, c2, c3, x_ref, w_ref, out, held, context):
    me = lax.axis_index("zl")
    for m, piece in enumerate((c0, c1, c2, c3)):
        held[jnp.bitwise_xor(me, m)] = piece[...]

    def block(h):
        return held[h // OWN, (h % OWN) * 128 : (h % OWN) * 128 + 128, :].astype(F32)

    for n in range(HEADS // 2):
        a, b = block(2 * n), block(2 * n + 1)
        even = jnp.concatenate([a[:, :64], b[:, :64]], axis=1).astype(BF16)
        odd = jnp.concatenate([a[:, 64:], b[:, 64:]], axis=1).astype(BF16)
        for sp in range(4):
            rows = slice(sp * 32, sp * 32 + 32)
            cols = slice(n * 128, n * 128 + 128)
            context[sp * 64 : sp * 64 + 32, cols] = even[rows]
            context[sp * 64 + 32 : sp * 64 + 64, cols] = odd[rows]
    mixed = jnp.dot(context[...], w_ref[...], preferred_element_type=F32)
    out[...] = (x_ref[...].astype(F32) + mixed).astype(BF16)


def line(pieces):
    return (pieces[0], *(lax.ppermute(pieces[m], "zl", LINE[m]) for m in (1, 2, 3)))


def around(slab):
    ring = [slab] + [lax.ppermute(slab, "y", RING[k]) for k in (1, 3, 2)]
    return ring + [lax.ppermute(s, "c", [(0, 1), (1, 0)]) for s in ring]


def per_device(x, gain, wq, wk, wv, wf):
    flat = x.reshape(256, 768)
    piece = ((384, 128), BF16)
    both = ((768, 128), BF16)
    slab = [((384, 512), BF16)]
    part = ((96, 1024), BF16)
    normed, *keys = call(
        key_kernel, [((256, 768), BF16)] + [piece] * 4, [pltpu.VMEM((4, 384, 128), BF16)]
    )(flat, gain.reshape(1, 768), wk)
    pairs = call(query_value_kernel, [both] * 4, [pltpu.VMEM((4, 768, 128), BF16)])(
        normed, wq, wv
    )
    keys = line(keys)
    keys, pairs = lax.optimization_barrier((tuple(keys), tuple(pairs)))
    (key_slab,) = call(functools.partial(slab_kernel, 0), slab)(*keys)
    pairs = line(pairs)
    key_slabs = around(key_slab)
    own, *others = call(
        logits_kernel,
        [((96, 1024), F32)] + [part] * 3,
        [pltpu.VMEM((OWN, 4, 32, 512), BF16)],
    )(*pairs, *key_slabs)
    (value_slab,) = call(functools.partial(slab_kernel, 384), slab)(*pairs)
    value_slabs = around(value_slab)
    got = [lax.ppermute(others[k - 1], "x", RING[k]) for k in (1, 2, 3)]
    total, sent = call(sum_kernel, [((96, 1024), F32), part])(own, *got)
    other = lax.ppermute(sent, "zh", [(0, 1), (1, 0)])
    scale = SIZE ** (-0.5) / (64.0**0.5)
    (probs,) = call(functools.partial(softmax_kernel, scale), [part])(total, other)
    probs = [probs] + [lax.ppermute(probs, "x", RING[k]) for k in (1, 2, 3)]
    context = call(
        context_kernel, [piece] * 4, [pltpu.VMEM((OWN, 4, 32, 1024), BF16)]
    )(*probs, *value_slabs)
    context = line(context)
    (out,) = call(
        out_kernel,
        [((256, 768), BF16)],
        [pltpu.VMEM((4, 384, 128), BF16), pltpu.VMEM((256, 768), BF16)],
    )(*context, flat, wf)
    return out.reshape(8, 32, 768)


def solution(mesh):
    fine = Mesh(mesh.devices.reshape(2, 4, 4, 4, 2), ("zh", "x", "zl", "y", "c"))
    split = P(("zh", "x"), ("zl", "y", "c"), None)
    return jax.shard_map(
        per_device,
        mesh=fine,
        in_specs=(split, P(), P(), P(), P(), P()),
        out_specs=split,
        check_vma=False,
    )
```

time: 324 us -> 101 us (0.31)
  waiting for transfers between devices: 244 us -> 53.1 us
  starting transfers between devices: 0.09 us -> 37.8 us
  local copies, waits for them, and re-layouts: 37 us -> 4.24 us
  matrix products: 23 us -> 0 us
  between operations: 13.2 us -> 0.13 us
  Pallas kernels: 0 us -> 5.56 us
  other arithmetic: 5.56 us -> 0 us
    all_gather x2 -> x0, waiting for transfers between devices: 135 us -> none  [the longest x1 78.4 us: per_device(): lax.all_gather(key, 'res', axis=1, tiled=True)]
    psum x1 -> x0, waiting for transfers between devices: 110 us -> none  [per_device(): total = lax.psum(partial_value, 'seq')]
    ppermute x0 -> x30, waiting for transfers between devices: none -> 53.1 us  [the longest x9 22.8 us: line(): lax.ppermute(pieces[m], 'zl', LINE[m])]
    ppermute x0 -> x30, starting transfers between devices: none -> 37.8 us  [the longest x9 14.7 us: line(): lax.ppermute(pieces[m], 'zl', LINE[m])]
    all_gather x2 -> x0, local copies, waits for them, and re-layouts: 33.2 us -> none  [the longest x1 16.7 us: per_device(): lax.all_gather(key, 'res', axis=1, tiled=True)]
    dot_general x6 -> x0, matrix products: 23 us -> none  [the longest x1 9.45 us: per_device(): jnp.einsum('hij,sjhd->sihd', probs, value_blocks, preferred_element_type=...]
    pallas_call x0 -> x9, Pallas kernels: none -> 5.56 us  [run(): pl.pallas_call(body, out_shape=[jax.ShapeDtypeStruct(s, d) for s, d in ou...]
    unnamed x6 -> x12, local copies, waits for them, and re-layouts: 0.02 us -> 3.55 us
  transfers between devices with their start and end apart: 3 -> 30, of which waited for: 3 -> 12; matrix products, arithmetic and copies ran while one was open for 14% -> 0% of each run, Pallas kernels for 0% -> 2%
where the time goes in v1:
time: 101 us
  waiting for transfers between devices  53.1 us (53%)
  starting transfers between devices  37.8 us (37%)
  Pallas kernels  5.56 us (6%)
  local copies, waits for them, and re-layouts  4.24 us (4%)
    ppermute x9, waiting for transfers between devices, line(): lax.ppermute(pieces[m], 'zl', LINE[m])  22.8 us
    ppermute x9, starting transfers between devices, line(): lax.ppermute(pieces[m], 'zl', LINE[m])  14.7 us
    ppermute x6, waiting for transfers between devices, around(): ring = [slab] + [lax.ppermute(slab, 'y', RING[k]) for k in (1, 3, 2)]  13.1 us
    ppermute x6, starting transfers between devices, around(): ring = [slab] + [lax.ppermute(slab, 'y', RING[k]) for k in (1, 3, 2)]  9.06 us
    ppermute x3, waiting for transfers between devices, per_device(): probs = [probs] + [lax.ppermute(probs, 'x', RING[k]) for k in (1, 2, 3)]  8.31 us
    ppermute x1, starting transfers between devices, per_device(): other = lax.ppermute(sent, 'zh', [(0, 1), (1, 0)])  5.88 us
    pallas_call x9, Pallas kernels, run(): pl.pallas_call(body, out_shape=[jax.ShapeDtypeStruct(s, d) for s, d in ou...  5.56 us
    ppermute x3, waiting for transfers between devices, per_device(): got = [lax.ppermute(others[k - 1], 'x', RING[k]) for k in (1, 2, 3)]  5.54 us
  transfers between devices with their start and end apart: 30, of which 12 were waited for; matrix products, arithmetic and copies ran while one was open for 0% of the time, Pallas kernels for 2%

profile of v1, /device:TPU:6, one launch (start us, length us, event | category | flops | bytes accessed | tf_op | source)
XLA Modules:
  0.0 100.8 jit_solution(15313590510805735847)
XLA Ops:
  0.7 1.0 copy-done
  1.7 1.3 %copy-done.3 = bf16[768,768]{1,0:T(8,128)(2,1)S(1)} copy-done((bf16[768,768]{1,0:T(8,128)(2,1)S(1)}, bf16[768,768]{1,0:T(8,128)(2,1)}, u32[]{:S(2)}) %copy-start.3) | copy-done | bytes 1179672
  3.8 2.0 %collective-permute-start = (bf16[384,128]{1,0:T(8,128)(2,1)S(1)}, bf16[384,128]{1,0:T(8,128)(2,1)S(1)}, u32[]{:S(2)}, u32[]{:S(2)}) collective-permute-start(bf16[384,128]{1,0:T(8,128)(2,1)S(1)} %get-tuple-element.33), channel_id=1, source_target_pairs={{0,8},{8,0},{16,24},{24,16},{1,9},{9,1},{17,25},{25,17},{2,10},{10... | collective-permute-start | bytes 294920 | tf_op jit(solution)/shard_map/ppermute | solution.py:177
  5.8 3.3 %collective-permute-start.1 = (bf16[384,128]{1,0:T(8,128)(2,1)S(1)}, bf16[384,128]{1,0:T(8,128)(2,1)S(1)}, u32[]{:S(2)}, u32[]{:S(2)}) collective-permute-start(bf16[384,128]{1,0:T(8,128)(2,1)S(1)} %get-tuple-element.34), channel_id=1, source_target_pairs={{0,16},{8,24},{16,0},{24,8},{1,17},{9,25},{17,1},{25,9},{2,18},{10... | collective-permute-start | bytes 294920 | tf_op jit(solution)/shard_map/ppermute | solution.py:177
  9.1 1.3 %copy-done.5 = bf16[768,768]{1,0:T(8,128)(2,1)S(1)} copy-done((bf16[768,768]{1,0:T(8,128)(2,1)S(1)}, bf16[768,768]{1,0:T(8,128)(2,1)}, u32[]{:S(2)}) %copy-start.5) | copy-done | bytes 1179672
  10.4 0.9 shard_map.65
  11.3 5.5 %collective-permute-done.1.p2 = bf16[384,128]{1,0:T(8,128)(2,1)S(1)} collective-permute-done((bf16[384,128]{1,0:T(8,128)(2,1)S(1)}, bf16[384,128]{1,0:T(8,128)(2,1)S(1)}, u32[]{:S(2)}, u32[]{:S(2)}) %collective-permute-start.1) | collective-permute-done | bytes 98336 | tf_op jit(solution)/shard_map/ppermute | solution.py:177
  16.9 1.7 %collective-permute-start.6 = (bf16[384,512]{1,0:T(8,128)(2,1)S(1)}, bf16[384,512]{1,0:T(8,128)(2,1)S(1)}, u32[]{:S(2)}, u32[]{:S(2)}) collective-permute-start(bf16[384,512]{1,0:T(8,128)(2,1)S(1)} %shard_map.66.refs_4_), channel_id=1, source_target_pairs={{0,2},{2,4},{4,6},{6,0},{1,3},{3,5},{5,7},{7,1},{8,10},{10,12},{12... | collective-permute-start | bytes 1179656 | tf_op jit(solution)/shard_map/ppermute | solution.py:181
  18.6 1.7 %collective-permute-start.7 = (bf16[384,512]{1,0:T(8,128)(2,1)S(1)}, bf16[384,512]{1,0:T(8,128)(2,1)S(1)}, u32[]{:S(2)}, u32[]{:S(2)}) collective-permute-start(bf16[384,512]{1,0:T(8,128)(2,1)S(1)} %shard_map.66.refs_4_), channel_id=1, source_target_pairs={{0,6},{2,0},{4,2},{6,4},{1,7},{3,1},{5,3},{7,5},{8,14},{10,8},{12,... | collective-permute-start | bytes 1179656 | tf_op jit(solution)/shard_map/ppermute | solution.py:181
  20.2 2.0 %collective-permute-start.8 = (bf16[384,512]{1,0:T(8,128)(2,1)S(1)}, bf16[384,512]{1,0:T(8,128)(2,1)S(1)}, u32[]{:S(2)}, u32[]{:S(2)}) collective-permute-start(bf16[384,512]{1,0:T(8,128)(2,1)S(1)} %shard_map.66.refs_4_), channel_id=1, source_target_pairs={{0,4},{2,6},{4,0},{6,2},{1,5},{3,7},{5,1},{7,3},{8,12},{10,14},{12... | collective-permute-start | bytes 1179656 | tf_op jit(solution)/shard_map/ppermute | solution.py:181
  22.2 1.6 %collective-permute-start.3 = (bf16[768,128]{1,0:T(8,128)(2,1)S(1)}, bf16[768,128]{1,0:T(8,128)(2,1)S(1)}, u32[]{:S(2)}, u32[]{:S(2)}) collective-permute-start(bf16[768,128]{1,0:T(8,128)(2,1)S(1)} %get-tuple-element.42), channel_id=1, source_target_pairs={{0,8},{8,0},{16,24},{24,16},{1,9},{9,1},{17,25},{25,17},{2,10},{10... | collective-permute-start | bytes 589832 | tf_op jit(solution)/shard_map/ppermute | solution.py:177
  23.8 1.4 %collective-permute-start.4 = (bf16[768,128]{1,0:T(8,128)(2,1)S(1)}, bf16[768,128]{1,0:T(8,128)(2,1)S(1)}, u32[]{:S(2)}, u32[]{:S(2)}) collective-permute-start(bf16[768,128]{1,0:T(8,128)(2,1)S(1)} %get-tuple-element.43), channel_id=1, source_target_pairs={{0,16},{8,24},{16,0},{24,8},{1,17},{9,25},{17,1},{25,9},{2,18},{10... | collective-permute-start | bytes 589832 | tf_op jit(solution)/shard_map/ppermute | solution.py:177
  25.2 4.6 %collective-permute-done.3.refs_1_.p1 = bf16[768,128]{1,0:T(8,128)(2,1)S(1)} collective-permute-done((bf16[768,128]{1,0:T(8,128)(2,1)S(1)}, bf16[768,128]{1,0:T(8,128)(2,1)S(1)}, u32[]{:S(2)}, u32[]{:S(2)}) %collective-permute-start.3) | collective-permute-done | bytes 196640 | tf_op jit(solution)/shard_map/ppermute | solution.py:177
  29.9 1.9 %collective-permute-start.5 = (bf16[768,128]{1,0:T(8,128)(2,1)S(1)}, bf16[768,128]{1,0:T(8,128)(2,1)S(1)}, u32[]{:S(2)}, u32[]{:S(2)}) collective-permute-start(bf16[768,128]{1,0:T(8,128)(2,1)S(1)} %get-tuple-element.44), channel_id=1, source_target_pairs={{0,24},{8,16},{16,8},{24,0},{1,25},{9,17},{17,9},{25,1},{2,26},{10... | collective-permute-start | bytes 589832 | tf_op jit(solution)/shard_map/ppermute | solution.py:177
  31.8 8.0 %collective-permute-done.4.refs_2_.p2 = bf16[768,128]{1,0:T(8,128)(2,1)S(1)} collective-permute-done((bf16[768,128]{1,0:T(8,128)(2,1)S(1)}, bf16[768,128]{1,0:T(8,128)(2,1)S(1)}, u32[]{:S(2)}, u32[]{:S(2)}) %collective-permute-start.4) | collective-permute-done | bytes 196640 | tf_op jit(solution)/shard_map/ppermute | solution.py:177
  41.6 2.6 %collective-permute-start.21 = (bf16[384,512]{1,0:T(8,128)(2,1)S(1)}, bf16[384,512]{1,0:T(8,128)(2,1)S(1)}, u32[]{:S(2)}, u32[]{:S(2)}) collective-permute-start(bf16[384,512]{1,0:T(8,128)(2,1)S(1)} %shard_map.70.refs_4_), channel_id=1, source_target_pairs={{0,6},{2,0},{4,2},{6,4},{1,7},{3,1},{5,3},{7,5},{8,14},{10,8},{12,... | collective-permute-start | bytes 1179656 | tf_op jit(solution)/shard_map/ppermute | solution.py:181
  44.6 1.0 shard_map.67
  46.2 2.4 %collective-permute-start.14 = (bf16[96,1024]{1,0:T(8,128)(2,1)S(1)}, bf16[96,1024]{1,0:T(8,128)(2,1)S(1)}, u32[]{:S(2)}, u32[]{:S(2)}) collective-permute-start(bf16[96,1024]{1,0:T(8,128)(2,1)S(1)} %get-tuple-element.51), channel_id=1, source_target_pairs={{0,64},{32,96},{64,0},{96,32},{1,65},{33,97},{65,1},{97,33},{2,66}... | collective-permute-start | bytes 589832 | tf_op jit(solution)/shard_map/ppermute | solution.py:209
  48.6 13.1 %collective-permute-done.20.refs_5_ = bf16[384,512]{1,0:T(8,128)(2,1)S(1)} collective-permute-done((bf16[384,512]{1,0:T(8,128)(2,1)S(1)}, bf16[384,512]{1,0:T(8,128)(2,1)S(1)}, u32[]{:S(2)}, u32[]{:S(2)}) %collective-permute-start.20) | collective-permute-done | bytes 393248 | tf_op jit(solution)/shard_map/ppermute | solution.py:181
  63.0 5.5 %collective-permute-done.15.r3 = bf16[96,1024]{1,0:T(8,128)(2,1)S(1)} collective-permute-done((bf16[96,1024]{1,0:T(8,128)(2,1)S(1)}, bf16[96,1024]{1,0:T(8,128)(2,1)S(1)}, u32[]{:S(2)}, u32[]{:S(2)}) %collective-permute-start.15) | collective-permute-done | bytes 196640 | tf_op jit(solution)/shard_map/ppermute | solution.py:209
  68.7 5.9 %collective-permute-start.16 = (bf16[96,1024]{1,0:T(8,128)(2,1)S(1)}, bf16[96,1024]{1,0:T(8,128)(2,1)S(1)}, u32[]{:S(2)}, u32[]{:S(2)}) collective-permute-start(bf16[96,1024]{1,0:T(8,128)(2,1)S(1)} %get-tuple-element.54), channel_id=1, source_target_pairs={{0,128},{128,0},{1,129},{129,1},{2,130},{130,2},{3,131},{131,3},{4... | collective-permute-start | bytes 589832 | tf_op jit(solution)/shard_map/ppermute | solution.py:211
  75.1 3.4 %collective-permute-done.16.other = bf16[96,1024]{1,0:T(8,128)(2,1)S(1)} collective-permute-done((bf16[96,1024]{1,0:T(8,128)(2,1)S(1)}, bf16[96,1024]{1,0:T(8,128)(2,1)S(1)}, u32[]{:S(2)}, u32[]{:S(2)}) %collective-permute-start.16) | collective-permute-done | bytes 196640 | tf_op jit(solution)/shard_map/ppermute | solution.py:211
  78.7 1.3 %collective-permute-start.17 = (bf16[96,1024]{1,0:T(8,128)(2,1)S(1)}, bf16[96,1024]{1,0:T(8,128)(2,1)S(1)}, u32[]{:S(2)}, u32[]{:S(2)}) collective-permute-start(bf16[96,1024]{1,0:T(8,128)(2,1)S(1)} %shard_map.69.refs_0_), channel_id=1, source_target_pairs={{0,32},{32,64},{64,96},{96,0},{1,33},{33,65},{65,97},{97,1},{2,34}... | collective-permute-start | bytes 589832 | tf_op jit(solution)/shard_map/ppermute | solution.py:214
  81.0 3.5 %collective-permute-done.17.refs_1_ = bf16[96,1024]{1,0:T(8,128)(2,1)S(1)} collective-permute-done((bf16[96,1024]{1,0:T(8,128)(2,1)S(1)}, bf16[96,1024]{1,0:T(8,128)(2,1)S(1)}, u32[]{:S(2)}, u32[]{:S(2)}) %collective-permute-start.17) | collective-permute-done | bytes 196640 | tf_op jit(solution)/shard_map/ppermute | solution.py:214
  84.4 2.9 %collective-permute-done.18.refs_2_ = bf16[96,1024]{1,0:T(8,128)(2,1)S(1)} collective-permute-done((bf16[96,1024]{1,0:T(8,128)(2,1)S(1)}, bf16[96,1024]{1,0:T(8,128)(2,1)S(1)}, u32[]{:S(2)}, u32[]{:S(2)}) %collective-permute-start.18) | collective-permute-done | bytes 196640 | tf_op jit(solution)/shard_map/ppermute | solution.py:214
  87.3 2.0 %collective-permute-done.19.refs_3_ = bf16[96,1024]{1,0:T(8,128)(2,1)S(1)} collective-permute-done((bf16[96,1024]{1,0:T(8,128)(2,1)S(1)}, bf16[96,1024]{1,0:T(8,128)(2,1)S(1)}, u32[]{:S(2)}, u32[]{:S(2)}) %collective-permute-start.19) | collective-permute-done | bytes 196640 | tf_op jit(solution)/shard_map/ppermute | solution.py:214
  89.3 1.0 %shard_map.71 = (bf16[384,128]{1,0:T(8,128)(2,1)S(1)}, bf16[384,128]{1,0:T(8,128)(2,1)S(1)}, bf16[384,128]{1,0:T(8,128)(2,1)S(1)}, bf16[384,128]{1,0:T(8,128)(2,1)S(1)}) custom-call(bf16[96,1024]{1,0:T(8,128)(2,1)S(1)} %shard_map.69.refs_0_, bf16[96,1024]{1,0:T(8,128)(2,1)S(1)} %collective-permute-done.17.refs_1_, ...), custom_call_target="tpu_custom_call" | custom-call | flops 1000000 | bytes 1000000 | tf_op jit(solution)/shard_map/pallas_call | solution.py:24
  90.4 2.5 %collective-permute-start.28 = (bf16[384,128]{1,0:T(8,128)(2,1)S(1)}, bf16[384,128]{1,0:T(8,128)(2,1)S(1)}, u32[]{:S(2)}, u32[]{:S(2)}) collective-permute-start(bf16[384,128]{1,0:T(8,128)(2,1)S(1)} %get-tuple-element.57), channel_id=1, source_target_pairs={{0,16},{8,24},{16,0},{24,8},{1,17},{9,25},{17,1},{25,9},{2,18},{10... | collective-permute-start | bytes 294920 | tf_op jit(solution)/shard_map/ppermute | solution.py:177
  92.9 1.9 %collective-permute-start.29 = (bf16[384,128]{1,0:T(8,128)(2,1)S(1)}, bf16[384,128]{1,0:T(8,128)(2,1)S(1)}, u32[]{:S(2)}, u32[]{:S(2)}) collective-permute-start(bf16[384,128]{1,0:T(8,128)(2,1)S(1)} %get-tuple-element.58), channel_id=1, source_target_pairs={{0,24},{8,16},{16,8},{24,0},{1,25},{9,17},{17,9},{25,1},{2,26},{10... | collective-permute-start | bytes 294920 | tf_op jit(solution)/shard_map/ppermute | solution.py:177
  95.0 1.0 %collective-permute-done.28.c2 = bf16[384,128]{1,0:T(8,128)(2,1)S(1)} collective-permute-done((bf16[384,128]{1,0:T(8,128)(2,1)S(1)}, bf16[384,128]{1,0:T(8,128)(2,1)S(1)}, u32[]{:S(2)}, u32[]{:S(2)}) %collective-permute-start.28) | collective-permute-done | bytes 98336 | tf_op jit(solution)/shard_map/ppermute | solution.py:177
  96.1 3.3 %collective-permute-done.29.c3 = bf16[384,128]{1,0:T(8,128)(2,1)S(1)} collective-permute-done((bf16[384,128]{1,0:T(8,128)(2,1)S(1)}, bf16[384,128]{1,0:T(8,128)(2,1)S(1)}, u32[]{:S(2)}, u32[]{:S(2)}) %collective-permute-start.29) | collective-permute-done | bytes 98336 | tf_op jit(solution)/shard_map/ppermute | solution.py:177
  99.4 1.3 %shard_map.72 = bf16[256,768]{1,0:T(8,128)(2,1)} custom-call(bf16[384,128]{1,0:T(8,128)(2,1)S(1)} %get-tuple-element.55.c0, bf16[384,128]{1,0:T(8,128)(2,1)S(1)} %collective-permute-done.27.c1, bf16[384,128]{1,0:T(8,128)(2,1)S(1)} %collective-permute-done.28.c2, bf16[384,128]{1,0:T(8,128)(2,1)S(1)} %collective-permute-done.29.c3, ...), custom_call_target="tpu_custom_call" | custom-call | flops 1000000 | bytes 1000000 | tf_op jit(solution)/shard_map/pallas_call | solution.py:24
  (50 shorter events, 8.0 us)
Async XLA Ops:
  3.8 7.5 %collective-permute-start = (bf16[384,128]{1,0:T(8,128)(2,1)S(1)}, bf16[384,128]{1,0:T(8,128)(2,1)S(1)}, u32[]{:S(2)}, u32[]{:S(2)}) collective-permute-start(bf16[384,128]{1,0:T(8,128)(2,1)S(1)} %get-tuple-element.33), channel_id=1, source_target_pairs={{0,8},{8,0},{16,24},{24,16},{1,9},{9,1},{17,25},{25,17},{2,10},{10... | collective-permute-start | bytes 294920 | tf_op jit(solution)/shard_map/ppermute | solution.py:177
  5.8 11.0 %collective-permute-start.1 = (bf16[384,128]{1,0:T(8,128)(2,1)S(1)}, bf16[384,128]{1,0:T(8,128)(2,1)S(1)}, u32[]{:S(2)}, u32[]{:S(2)}) collective-permute-start(bf16[384,128]{1,0:T(8,128)(2,1)S(1)} %get-tuple-element.34), channel_id=1, source_target_pairs={{0,16},{8,24},{16,0},{24,8},{1,17},{9,25},{17,1},{25,9},{2,18},{10... | collective-permute-start | bytes 294920 | tf_op jit(solution)/shard_map/ppermute | solution.py:177
  9.1 7.7 %collective-permute-start.2 = (bf16[384,128]{1,0:T(8,128)(2,1)S(1)}, bf16[384,128]{1,0:T(8,128)(2,1)S(1)}, u32[]{:S(2)}, u32[]{:S(2)}) collective-permute-start(bf16[384,128]{1,0:T(8,128)(2,1)S(1)} %get-tuple-element.35), channel_id=1, source_target_pairs={{0,24},{8,16},{16,8},{24,0},{1,25},{9,17},{17,9},{25,1},{2,26},{10... | collective-permute-start | bytes 294920 | tf_op jit(solution)/shard_map/ppermute | solution.py:177
  16.9 22.9 %collective-permute-start.6 = (bf16[384,512]{1,0:T(8,128)(2,1)S(1)}, bf16[384,512]{1,0:T(8,128)(2,1)S(1)}, u32[]{:S(2)}, u32[]{:S(2)}) collective-permute-start(bf16[384,512]{1,0:T(8,128)(2,1)S(1)} %shard_map.66.refs_4_), channel_id=1, source_target_pairs={{0,2},{2,4},{4,6},{6,0},{1,3},{3,5},{5,7},{7,1},{8,10},{10,12},{12... | collective-permute-start | bytes 1179656 | tf_op jit(solution)/shard_map/ppermute | solution.py:181
  18.6 21.7 %collective-permute-start.7 = (bf16[384,512]{1,0:T(8,128)(2,1)S(1)}, bf16[384,512]{1,0:T(8,128)(2,1)S(1)}, u32[]{:S(2)}, u32[]{:S(2)}) collective-permute-start(bf16[384,512]{1,0:T(8,128)(2,1)S(1)} %shard_map.66.refs_4_), channel_id=1, source_target_pairs={{0,6},{2,0},{4,2},{6,4},{1,7},{3,1},{5,3},{7,5},{8,14},{10,8},{12,... | collective-permute-start | bytes 1179656 | tf_op jit(solution)/shard_map/ppermute | solution.py:181
  20.2 20.2 %collective-permute-start.8 = (bf16[384,512]{1,0:T(8,128)(2,1)S(1)}, bf16[384,512]{1,0:T(8,128)(2,1)S(1)}, u32[]{:S(2)}, u32[]{:S(2)}) collective-permute-start(bf16[384,512]{1,0:T(8,128)(2,1)S(1)} %shard_map.66.refs_4_), channel_id=1, source_target_pairs={{0,4},{2,6},{4,0},{6,2},{1,5},{3,7},{5,1},{7,3},{8,12},{10,14},{12... | collective-permute-start | bytes 1179656 | tf_op jit(solution)/shard_map/ppermute | solution.py:181
  22.2 7.7 %collective-permute-start.3 = (bf16[768,128]{1,0:T(8,128)(2,1)S(1)}, bf16[768,128]{1,0:T(8,128)(2,1)S(1)}, u32[]{:S(2)}, u32[]{:S(2)}) collective-permute-start(bf16[768,128]{1,0:T(8,128)(2,1)S(1)} %get-tuple-element.42), channel_id=1, source_target_pairs={{0,8},{8,0},{16,24},{24,16},{1,9},{9,1},{17,25},{25,17},{2,10},{10... | collective-permute-start | bytes 589832 | tf_op jit(solution)/shard_map/ppermute | solution.py:177
  23.8 15.9 %collective-permute-start.4 = (bf16[768,128]{1,0:T(8,128)(2,1)S(1)}, bf16[768,128]{1,0:T(8,128)(2,1)S(1)}, u32[]{:S(2)}, u32[]{:S(2)}) collective-permute-start(bf16[768,128]{1,0:T(8,128)(2,1)S(1)} %get-tuple-element.43), channel_id=1, source_target_pairs={{0,16},{8,24},{16,0},{24,8},{1,17},{9,25},{17,1},{25,9},{2,18},{10... | collective-permute-start | bytes 589832 | tf_op jit(solution)/shard_map/ppermute | solution.py:177
  29.9 10.9 %collective-permute-start.5 = (bf16[768,128]{1,0:T(8,128)(2,1)S(1)}, bf16[768,128]{1,0:T(8,128)(2,1)S(1)}, u32[]{:S(2)}, u32[]{:S(2)}) collective-permute-start(bf16[768,128]{1,0:T(8,128)(2,1)S(1)} %get-tuple-element.44), channel_id=1, source_target_pairs={{0,24},{8,16},{16,8},{24,0},{1,25},{9,17},{17,9},{25,1},{2,26},{10... | collective-permute-start | bytes 589832 | tf_op jit(solution)/shard_map/ppermute | solution.py:177
  39.8 1.9 %collective-permute-start.9 = (bf16[384,512]{1,0:T(8,128)(2,1)S(1)}, bf16[384,512]{1,0:T(8,128)(2,1)S(1)}, u32[]{:S(2)}, u32[]{:S(2)}) collective-permute-start(bf16[384,512]{1,0:T(8,128)(2,1)S(1)} %shard_map.66.refs_4_), channel_id=1, source_target_pairs={{0,1},{1,0},{2,3},{3,2},{4,5},{5,4},{6,7},{7,6},{8,9},{9,8},{10,11... | collective-permute-start | bytes 1179656 | tf_op jit(solution)/shard_map/ppermute | solution.py:182
  39.8 4.4 %collective-permute-start.10 = (bf16[384,512]{1,0:T(8,128)(2,1)S(1)}, bf16[384,512]{1,0:T(8,128)(2,1)S(1)}, u32[]{:S(2)}, u32[]{:S(2)}) collective-permute-start(bf16[384,512]{1,0:T(8,128)(2,1)S(1)} %collective-permute-done.6.refs_5_), channel_id=1, source_target_pairs={{0,1},{1,0},{2,3},{3,2},{4,5},{5,4},{6,7},{7,6},{8,9},{9,8},{10,11... | collective-permute-start | bytes 1179656 | tf_op jit(solution)/shard_map/ppermute | solution.py:182
  40.3 4.4 %collective-permute-start.11 = (bf16[384,512]{1,0:T(8,128)(2,1)S(1)}, bf16[384,512]{1,0:T(8,128)(2,1)S(1)}, u32[]{:S(2)}, u32[]{:S(2)}) collective-permute-start(bf16[384,512]{1,0:T(8,128)(2,1)S(1)} %collective-permute-done.7.refs_6_), channel_id=1, source_target_pairs={{0,1},{1,0},{2,3},{3,2},{4,5},{5,4},{6,7},{7,6},{8,9},{9,8},{10,11... | collective-permute-start | bytes 1179656 | tf_op jit(solution)/shard_map/ppermute | solution.py:182
  40.4 4.3 %collective-permute-start.12 = (bf16[384,512]{1,0:T(8,128)(2,1)S(1)}, bf16[384,512]{1,0:T(8,128)(2,1)S(1)}, u32[]{:S(2)}, u32[]{:S(2)}) collective-permute-start(bf16[384,512]{1,0:T(8,128)(2,1)S(1)} %collective-permute-done.8.refs_7_), channel_id=1, source_target_pairs={{0,1},{1,0},{2,3},{3,2},{4,5},{5,4},{6,7},{7,6},{8,9},{9,8},{10,11... | collective-permute-start | bytes 1179656 | tf_op jit(solution)/shard_map/ppermute | solution.py:182
  40.9 20.8 %collective-permute-start.20 = (bf16[384,512]{1,0:T(8,128)(2,1)S(1)}, bf16[384,512]{1,0:T(8,128)(2,1)S(1)}, u32[]{:S(2)}, u32[]{:S(2)}) collective-permute-start(bf16[384,512]{1,0:T(8,128)(2,1)S(1)} %shard_map.70.refs_4_), channel_id=1, source_target_pairs={{0,2},{2,4},{4,6},{6,0},{1,3},{3,5},{5,7},{7,1},{8,10},{10,12},{12... | collective-permute-start | bytes 1179656 | tf_op jit(solution)/shard_map/ppermute | solution.py:181
  41.6 32.9 %collective-permute-start.21 = (bf16[384,512]{1,0:T(8,128)(2,1)S(1)}, bf16[384,512]{1,0:T(8,128)(2,1)S(1)}, u32[]{:S(2)}, u32[]{:S(2)}) collective-permute-start(bf16[384,512]{1,0:T(8,128)(2,1)S(1)} %shard_map.70.refs_4_), channel_id=1, source_target_pairs={{0,6},{2,0},{4,2},{6,4},{1,7},{3,1},{5,3},{7,5},{8,14},{10,8},{12,... | collective-permute-start | bytes 1179656 | tf_op jit(solution)/shard_map/ppermute | solution.py:181
  44.2 30.4 %collective-permute-start.22 = (bf16[384,512]{1,0:T(8,128)(2,1)S(1)}, bf16[384,512]{1,0:T(8,128)(2,1)S(1)}, u32[]{:S(2)}, u32[]{:S(2)}) collective-permute-start(bf16[384,512]{1,0:T(8,128)(2,1)S(1)} %shard_map.70.refs_4_), channel_id=1, source_target_pairs={{0,4},{2,6},{4,0},{6,2},{1,5},{3,7},{5,1},{7,3},{8,12},{10,14},{12... | collective-permute-start | bytes 1179656 | tf_op jit(solution)/shard_map/ppermute | solution.py:181
  45.6 16.9 %collective-permute-start.13 = (bf16[96,1024]{1,0:T(8,128)(2,1)S(1)}, bf16[96,1024]{1,0:T(8,128)(2,1)S(1)}, u32[]{:S(2)}, u32[]{:S(2)}) collective-permute-start(bf16[96,1024]{1,0:T(8,128)(2,1)S(1)} %get-tuple-element.50), channel_id=1, source_target_pairs={{0,32},{32,64},{64,96},{96,0},{1,33},{33,65},{65,97},{97,1},{2,34}... | collective-permute-start | bytes 589832 | tf_op jit(solution)/shard_map/ppermute | solution.py:209
  46.2 16.3 %collective-permute-start.14 = (bf16[96,1024]{1,0:T(8,128)(2,1)S(1)}, bf16[96,1024]{1,0:T(8,128)(2,1)S(1)}, u32[]{:S(2)}, u32[]{:S(2)}) collective-permute-start(bf16[96,1024]{1,0:T(8,128)(2,1)S(1)} %get-tuple-element.51), channel_id=1, source_target_pairs={{0,64},{32,96},{64,0},{96,32},{1,65},{33,97},{65,1},{97,33},{2,66}... | collective-permute-start | bytes 589832 | tf_op jit(solution)/shard_map/ppermute | solution.py:209
  61.7 6.9 %collective-permute-start.15 = (bf16[96,1024]{1,0:T(8,128)(2,1)S(1)}, bf16[96,1024]{1,0:T(8,128)(2,1)S(1)}, u32[]{:S(2)}, u32[]{:S(2)}) collective-permute-start(bf16[96,1024]{1,0:T(8,128)(2,1)S(1)} %get-tuple-element.52), channel_id=1, source_target_pairs={{0,96},{32,0},{64,32},{96,64},{1,97},{33,1},{65,33},{97,65},{2,98}... | collective-permute-start | bytes 589832 | tf_op jit(solution)/shard_map/ppermute | solution.py:209
  62.5 17.5 %collective-permute-start.23 = (bf16[384,512]{1,0:T(8,128)(2,1)S(1)}, bf16[384,512]{1,0:T(8,128)(2,1)S(1)}, u32[]{:S(2)}, u32[]{:S(2)}) collective-permute-start(bf16[384,512]{1,0:T(8,128)(2,1)S(1)} %shard_map.70.refs_4_), channel_id=1, source_target_pairs={{0,1},{1,0},{2,3},{3,2},{4,5},{5,4},{6,7},{7,6},{8,9},{9,8},{10,11... | collective-permute-start | bytes 1179656 | tf_op jit(solution)/shard_map/ppermute | solution.py:182
  62.5 17.9 %collective-permute-start.24 = (bf16[384,512]{1,0:T(8,128)(2,1)S(1)}, bf16[384,512]{1,0:T(8,128)(2,1)S(1)}, u32[]{:S(2)}, u32[]{:S(2)}) collective-permute-start(bf16[384,512]{1,0:T(8,128)(2,1)S(1)} %collective-permute-done.20.refs_5_), channel_id=1, source_target_pairs={{0,1},{1,0},{2,3},{3,2},{4,5},{5,4},{6,7},{7,6},{8,9},{9,8},{10,11... | collective-permute-start | bytes 1179656 | tf_op jit(solution)/shard_map/ppermute | solution.py:182
  68.7 9.8 %collective-permute-start.16 = (bf16[96,1024]{1,0:T(8,128)(2,1)S(1)}, bf16[96,1024]{1,0:T(8,128)(2,1)S(1)}, u32[]{:S(2)}, u32[]{:S(2)}) collective-permute-start(bf16[96,1024]{1,0:T(8,128)(2,1)S(1)} %get-tuple-element.54), channel_id=1, source_target_pairs={{0,128},{128,0},{1,129},{129,1},{2,130},{130,2},{3,131},{131,3},{4... | collective-permute-start | bytes 589832 | tf_op jit(solution)/shard_map/ppermute | solution.py:211
  74.5 6.4 %collective-permute-start.25 = (bf16[384,512]{1,0:T(8,128)(2,1)S(1)}, bf16[384,512]{1,0:T(8,128)(2,1)S(1)}, u32[]{:S(2)}, u32[]{:S(2)}) collective-permute-start(bf16[384,512]{1,0:T(8,128)(2,1)S(1)} %collective-permute-done.21.refs_6_), channel_id=1, source_target_pairs={{0,1},{1,0},{2,3},{3,2},{4,5},{5,4},{6,7},{7,6},{8,9},{9,8},{10,11... | collective-permute-start | bytes 1179656 | tf_op jit(solution)/shard_map/ppermute | solution.py:182
  74.6 6.4 %collective-permute-start.26 = (bf16[384,512]{1,0:T(8,128)(2,1)S(1)}, bf16[384,512]{1,0:T(8,128)(2,1)S(1)}, u32[]{:S(2)}, u32[]{:S(2)}) collective-permute-start(bf16[384,512]{1,0:T(8,128)(2,1)S(1)} %collective-permute-done.22.refs_7_), channel_id=1, source_target_pairs={{0,1},{1,0},{2,3},{3,2},{4,5},{5,4},{6,7},{7,6},{8,9},{9,8},{10,11... | collective-permute-start | bytes 1179656 | tf_op jit(solution)/shard_map/ppermute | solution.py:182
  78.7 20.8 %copy-start.1 = (bf16[8,32,768]{2,1,0:T(8,128)(2,1)S(1)}, bf16[8,32,768]{2,1,0:T(8,128)(2,1)}, u32[]{:S(2)}) copy-start(bf16[8,32,768]{2,1,0:T(8,128)(2,1)} %param.6) | copy-start | bytes 1179652
  78.7 20.8 %copy-start.2 = (bf16[768,768]{1,0:T(8,128)(2,1)S(1)}, bf16[768,768]{1,0:T(8,128)(2,1)}, u32[]{:S(2)}) copy-start(bf16[768,768]{1,0:T(8,128)(2,1)} %w_ref.3) | copy-start | bytes 3538948
  78.7 5.7 %collective-permute-start.17 = (bf16[96,1024]{1,0:T(8,128)(2,1)S(1)}, bf16[96,1024]{1,0:T(8,128)(2,1)S(1)}, u32[]{:S(2)}, u32[]{:S(2)}) collective-permute-start(bf16[96,1024]{1,0:T(8,128)(2,1)S(1)} %shard_map.69.refs_0_), channel_id=1, source_target_pairs={{0,32},{32,64},{64,96},{96,0},{1,33},{33,65},{65,97},{97,1},{2,34}... | collective-permute-start | bytes 589832 | tf_op jit(solution)/shard_map/ppermute | solution.py:214
  80.0 7.3 %collective-permute-start.18 = (bf16[96,1024]{1,0:T(8,128)(2,1)S(1)}, bf16[96,1024]{1,0:T(8,128)(2,1)S(1)}, u32[]{:S(2)}, u32[]{:S(2)}) collective-permute-start(bf16[96,1024]{1,0:T(8,128)(2,1)S(1)} %shard_map.69.refs_0_), channel_id=1, source_target_pairs={{0,64},{32,96},{64,0},{96,32},{1,65},{33,97},{65,1},{97,33},{2,66}... | collective-permute-start | bytes 589832 | tf_op jit(solution)/shard_map/ppermute | solution.py:214
  80.5 8.8 %collective-permute-start.19 = (bf16[96,1024]{1,0:T(8,128)(2,1)S(1)}, bf16[96,1024]{1,0:T(8,128)(2,1)S(1)}, u32[]{:S(2)}, u32[]{:S(2)}) collective-permute-start(bf16[96,1024]{1,0:T(8,128)(2,1)S(1)} %shard_map.69.refs_0_), channel_id=1, source_target_pairs={{0,96},{32,0},{64,32},{96,64},{1,97},{33,1},{65,33},{97,65},{2,98}... | collective-permute-start | bytes 589832 | tf_op jit(solution)/shard_map/ppermute | solution.py:214
  90.3 4.7 %collective-permute-start.27 = (bf16[384,128]{1,0:T(8,128)(2,1)S(1)}, bf16[384,128]{1,0:T(8,128)(2,1)S(1)}, u32[]{:S(2)}, u32[]{:S(2)}) collective-permute-start(bf16[384,128]{1,0:T(8,128)(2,1)S(1)} %get-tuple-element.56), channel_id=1, source_target_pairs={{0,8},{8,0},{16,24},{24,16},{1,9},{9,1},{17,25},{25,17},{2,10},{10... | collective-permute-start | bytes 294920 | tf_op jit(solution)/shard_map/ppermute | solution.py:177
  90.4 5.7 %collective-permute-start.28 = (bf16[384,128]{1,0:T(8,128)(2,1)S(1)}, bf16[384,128]{1,0:T(8,128)(2,1)S(1)}, u32[]{:S(2)}, u32[]{:S(2)}) collective-permute-start(bf16[384,128]{1,0:T(8,128)(2,1)S(1)} %get-tuple-element.57), channel_id=1, source_target_pairs={{0,16},{8,24},{16,0},{24,8},{1,17},{9,25},{17,1},{25,9},{2,18},{10... | collective-permute-start | bytes 294920 | tf_op jit(solution)/shard_map/ppermute | solution.py:177
  92.9 6.5 %collective-permute-start.29 = (bf16[384,128]{1,0:T(8,128)(2,1)S(1)}, bf16[384,128]{1,0:T(8,128)(2,1)S(1)}, u32[]{:S(2)}, u32[]{:S(2)}) collective-permute-start(bf16[384,128]{1,0:T(8,128)(2,1)S(1)} %get-tuple-element.58), channel_id=1, source_target_pairs={{0,24},{8,16},{16,8},{24,0},{1,25},{9,17},{17,9},{25,1},{2,26},{10... | collective-permute-start | bytes 294920 | tf_op jit(solution)/shard_map/ppermute | solution.py:177
  (4 other events, 9.7 us)

commit v2 on v1

v2 whole, which is shorter than its diff:
```python
import functools

import jax
import jax.numpy as jnp
from jax import lax
from jax.experimental import pallas as pl
from jax.experimental.pallas import tpu as pltpu
from jax.sharding import Mesh
from jax.sharding import PartitionSpec as P

HEADS = 12
SIZE = 64
GROUPS = 4
OWN = HEADS // GROUPS
F32, BF16 = jnp.float32, jnp.bfloat16
LINE = [[(i, i ^ m) for i in range(4)] for m in range(4)]
RING = [[(i, (i + k) % 4) for i in range(4)] for k in range(4)]
VMEM = pl.BlockSpec(memory_space=pltpu.VMEM)
FAR = pl.BlockSpec(memory_space=pltpu.HBM)
LIMIT = 48 * 1024 * 1024
MOST = 60 * 1024 * 1024


def call(body, outs, scratch=(), flops=5000000000, moved=1000000, places=None, after=(), limit=LIMIT):
    def run(*args):
        count = len(args)

        def kernel(*refs):
            body(*refs[:count], *refs[count + len(after) :])

        specs = [places.get(i, VMEM) if places else VMEM for i in range(count)]
        return pl.pallas_call(
            kernel,
            out_shape=[jax.ShapeDtypeStruct(s, d) for s, d in outs],
            in_specs=specs + [FAR] * len(after),
            out_specs=[VMEM] * len(outs),
            scratch_shapes=list(scratch),
            compiler_params=pltpu.CompilerParams(vmem_limit_bytes=limit),
            cost_estimate=pl.CostEstimate(
                flops=flops, bytes_accessed=moved, transcendentals=0
            ),
        )(*args, *after)

    return run


def pack(full, store):
    parts = full.reshape(4, 2, 32, HEADS * SIZE)
    even, odd = parts[:, 0].reshape(128, -1), parts[:, 1].reshape(128, -1)
    for n in range(HEADS // 2):
        a, b = even[:, n * 128 : n * 128 + 128], odd[:, n * 128 : n * 128 + 128]
        store(2 * n, jnp.concatenate([a[:, :64], b[:, :64]], axis=1).astype(BF16))
        store(2 * n + 1, jnp.concatenate([a[:, 64:], b[:, 64:]], axis=1).astype(BF16))


def key_kernel(x_far, gain_far, w_far, normed_ref, o0, o1, o2, o3, held, x_ref, gain_ref, w_ref, sems):
    copies = [
        pltpu.make_async_copy(far, near, sems.at[i])
        for i, (far, near) in enumerate(
            ((x_far, x_ref), (gain_far, gain_ref), (w_far, w_ref))
        )
    ]
    for copy in copies:
        copy.start()
    copies[0].wait()
    x = x_ref[...].astype(F32)
    mean = jnp.mean(x, axis=-1, keepdims=True)
    off = x - mean
    var = jnp.mean(off * off, axis=-1, keepdims=True)
    copies[1].wait()
    gain = gain_ref[...].reshape(1, HEADS * SIZE)
    normed = (off / jnp.sqrt(var + 1e-05) * gain).astype(BF16)
    normed_ref[...] = normed
    copies[2].wait()
    spread(normed, w_ref, (o0, o1, o2, o3), held)


def spread(normed, w_ref, outs, held, row=0):
    full = jnp.dot(normed, w_ref[...], preferred_element_type=F32)

    def store(h, block):
        held[h // OWN, (h % OWN) * 128 : (h % OWN) * 128 + 128, :] = block

    pack(full, store)
    me = lax.axis_index("zl")
    for m, out in enumerate(outs):
        out[row : row + 384, :] = held[jnp.bitwise_xor(me, m)]


def projection_kernel(normed_ref, *refs):
    n = (len(refs) - 5)
    outs, held = refs[n:-1], refs[-1]
    for i, w_ref in enumerate(refs[:n]):
        spread(normed_ref[...], w_ref, outs, held, i * 384)


def slab_kernel(base, *refs):
    pieces, slab = refs[:-1], refs[-1]
    n = len(pieces)
    for m, piece in enumerate(pieces):
        for h in range(OWN):
            for sp in range(4):
                row, to = base + h * 128 + sp * 32, (h * n + m) * 32
                slab[to : to + 32, sp * 128 : sp * 128 + 128] = piece[row : row + 32, :]


def logits_kernel(*refs):
    pieces, slabs = refs[:4], refs[4:-5]
    own, others, held = refs[-5], refs[-4:-1], refs[-1]
    me = lax.axis_index("x")
    for m, piece in enumerate(pieces):
        at = lax.rem(m - me + 4, 4)
        for h in range(OWN):
            for sp in range(4):
                row = h * 128 + sp * 32
                held[h, at, :, sp * 128 : sp * 128 + 128] = piece[row : row + 32, :]
    for h in range(OWN):
        query = held[h].reshape(128, 512)
        for j in range(len(slabs) // 2):
            keys = jnp.concatenate(
                [slab[h * 128 : h * 128 + 128, :] for slab in slabs[2 * j : 2 * j + 2]], axis=0
            )
            part = lax.dot_general(
                query, keys, (((1,), (1,)), ((), ())), preferred_element_type=F32
            )
            cols = slice(j * 256, j * 256 + 256)
            own[h * 32 : h * 32 + 32, cols] = part[:32]
            for k, out in enumerate(others):
                out[h * 32 : h * 32 + 32, cols] = part[k * 32 + 32 : k * 32 + 64].astype(BF16)


def sum_kernel(own, r1, r2, r3, total, sent):
    s = own[...] + r1[...].astype(F32) + r2[...].astype(F32) + r3[...].astype(F32)
    total[...] = s
    sent[...] = s.astype(BF16)


def softmax_kernel(scale, total, other, probs):
    logits = (total[...] + other[...].astype(F32)) * scale
    top = jnp.max(logits, axis=-1, keepdims=True)
    e = jnp.exp(logits - top)
    probs[...] = (e / jnp.sum(e, axis=-1, keepdims=True)).astype(BF16)


def context_kernel(*refs):
    probs, slabs, outs, held = refs[:4], refs[4:-5], refs[-5:-1], refs[-1]
    me = lax.axis_index("x")
    for k, piece in enumerate(probs):
        at = lax.rem(me - k + 4, 4)
        for h in range(OWN):
            held[h, at] = piece[h * 32 : h * 32 + 32, :]
    for h in range(OWN):
        p = held[h].reshape(128, 1024)
        total = None
        for j in range(4):
            values = jnp.concatenate(
                [slab[h * 128 : h * 128 + 128, :] for slab in slabs[2 * j : 2 * j + 2]], axis=0
            )
            part = jnp.dot(
                p[:, j * 256 : j * 256 + 256], values, preferred_element_type=F32
            )
            total = part if total is None else total + part
        total = total.astype(BF16)
        for m, out in enumerate(outs):
            for sp in range(4):
                row = h * 128 + sp * 32
                out[row : row + 32, :] = total[
                    m * 32 : m * 32 + 32, sp * 128 : sp * 128 + 128
                ]


def out_kernel(c0, c1, c2, c3, x_ref, w_ref, out, held, context):
    me = lax.axis_index("zl")
    for m, piece in enumerate((c0, c1, c2, c3)):
        held[jnp.bitwise_xor(me, m)] = piece[...]

    def block(h):
        return held[h // OWN, (h % OWN) * 128 : (h % OWN) * 128 + 128, :].astype(F32)

    for n in range(HEADS // 2):
        a, b = block(2 * n), block(2 * n + 1)
        even = jnp.concatenate([a[:, :64], b[:, :64]], axis=1).astype(BF16)
        odd = jnp.concatenate([a[:, 64:], b[:, 64:]], axis=1).astype(BF16)
        for sp in range(4):
            rows = slice(sp * 32, sp * 32 + 32)
            cols = slice(n * 128, n * 128 + 128)
            context[sp * 64 : sp * 64 + 32, cols] = even[rows]
            context[sp * 64 + 32 : sp * 64 + 64, cols] = odd[rows]
    mixed = jnp.dot(context[...], w_ref[...], preferred_element_type=F32)
    out[...] = (x_ref[...].astype(F32) + mixed).astype(BF16)


def line(pieces):
    return (pieces[0], *(lax.ppermute(pieces[m], "zl", LINE[m]) for m in (1, 2, 3)))


def other_core(slabs):
    return [lax.ppermute(s, "c", [(0, 1), (1, 0)]) for s in slabs]


def over(axis, arrays, order=(1, 3, 2)):
    return [lax.ppermute(arrays[k], axis, RING[k]) for k in order]


def per_device(x, gain, wq, wk, wv, wf):
    flat = x.reshape(256, 768)
    piece = ((384, 128), BF16)
    part = ((96, 1024), BF16)
    whole = ((384, 512), BF16)
    weights = pltpu.VMEM((768, 768), BF16)
    pieces = pltpu.VMEM((4, 384, 128), BF16)
    normed, *keys = call(
        key_kernel,
        [((256, 768), BF16)] + [piece] * 4,
        [
            pieces,
            pltpu.VMEM((256, 768), BF16),
            pltpu.VMEM((768,), F32),
            weights,
            pltpu.SemaphoreType.DMA((3,)),
        ],
        places={0: FAR, 1: FAR, 2: FAR},
        limit=MOST,
    )(flat, gain, wk)
    keys = line(keys)

    def slab(parts, base, after=()):
        return call(functools.partial(slab_kernel, base), [whole], after=after)(*parts)[0]

    pairs = line(
        call(projection_kernel, [((768, 128), BF16)] * 4, [pieces])(normed, wq, wv)
    )
    first = slab(keys, 0)
    slabs = [first] + over("y", [first] * 4)
    slabs += other_core(slabs)
    own, *others = call(
        logits_kernel,
        [((96, 1024), F32)] + [part] * 3,
        [pltpu.VMEM((OWN, 4, 32, 512), BF16)],
    )(*pairs, *slabs)
    got = over("x", [own, *others])
    first = slab(pairs, 384)
    slabs = [first] + over("y", [first] * 4, (1, 3))
    swapped = other_core(slabs)
    last = over("y", [slab(pairs, 384, got)] * 4, (2,))
    slabs += last + swapped + other_core(last)
    total, sent = call(sum_kernel, [((96, 1024), F32), part])(own, *got)
    other = lax.ppermute(sent, "zh", [(0, 1), (1, 0)])
    scale = SIZE ** (-0.5) / (64.0**0.5)
    (probs,) = call(functools.partial(softmax_kernel, scale), [part], after=swapped)(
        total, other
    )
    probs = [probs] + over("x", [probs] * 4, (1, 2, 3))
    context = call(
        context_kernel, [piece] * 4, [pltpu.VMEM((OWN, 4, 32, 1024), BF16)]
    )(*probs, *slabs)
    (out,) = call(
        out_kernel, [((256, 768), BF16)], [pieces, pltpu.VMEM((256, 768), BF16)]
    )(*line(context), flat, wf)
    return out.reshape(8, 32, 768)


def solution(mesh):
    fine = Mesh(mesh.devices.reshape(2, 4, 4, 4, 2), ("zh", "x", "zl", "y", "c"))
    split = P(("zh", "x"), ("zl", "y", "c"), None)
    return jax.shard_map(
        per_device,
        mesh=fine,
        in_specs=(split, P(), P(), P(), P(), P()),
        out_specs=split,
        check_vma=False,
    )
```

time: 101 us -> 94.6 us (0.937)
  waiting for transfers between devices: 53.1 us -> 45.8 us
  local copies, waits for them, and re-layouts: 4.24 us -> 1.01 us
  starting transfers between devices: 37.8 us -> 40 us
  Pallas kernels: 5.56 us -> 7.46 us
    ppermute x20, waiting for transfers between devices: 26.9 us -> 20.1 us  [the longest x12 20 us: over(): return [lax.ppermute(arrays[k], axis, RING[k]) for k in order]]
    unnamed x12, local copies, waits for them, and re-layouts: 3.55 us -> 1.01 us
    pallas_call x9 -> x10, Pallas kernels: 5.56 us -> 7.46 us  [run(): pl.pallas_call(kernel, out_shape=[jax.ShapeDtypeStruct(s, d) for s, d in...]
    ppermute x20, starting transfers between devices: 17.2 us -> 18.7 us  [the longest x12 17.1 us: over(): return [lax.ppermute(arrays[k], axis, RING[k]) for k in order]]
  transfers between devices with their start and end apart: 30 -> 30, of which waited for: 12 -> 12; matrix products, arithmetic and copies ran while one was open for 0% -> 0% of each run, Pallas kernels for 2% -> 3%
where the time goes in v2:
time: 94.6 us; the launch traced here: 94.4 us
  waiting for transfers between devices  45.8 us (48%)
  starting transfers between devices  40 us (42%)
  Pallas kernels  7.46 us (8%)
  local copies, waits for them, and re-layouts  1.01 us (1%)
    ppermute x9, waiting for transfers between devices, line(): lax.ppermute(pieces[m], 'zl', LINE[m])  23.4 us
    ppermute x12, waiting for transfers between devices, over(): return [lax.ppermute(arrays[k], axis, RING[k]) for k in order]  20 us
    ppermute x12, starting transfers between devices, over(): return [lax.ppermute(arrays[k], axis, RING[k]) for k in order]  17.1 us
    ppermute x9, starting transfers between devices, line(): lax.ppermute(pieces[m], 'zl', LINE[m])  15.3 us
    pallas_call x10, Pallas kernels, run(): pl.pallas_call(kernel, out_shape=[jax.ShapeDtypeStruct(s, d) for s, d in...  7.46 us
    ppermute x1, starting transfers between devices, per_device(): other = lax.ppermute(sent, 'zh', [(0, 1), (1, 0)])  5.94 us
    ppermute x1, waiting for transfers between devices, per_device(): other = lax.ppermute(sent, 'zh', [(0, 1), (1, 0)])  2.39 us
  transfers between devices with their start and end apart: 30, of which 12 were waited for; matrix products, arithmetic and copies ran while one was open for 0% of the time, Pallas kernels for 3%

profile of v2, /device:TPU:6, one launch (start us, length us, event | category | flops | bytes accessed | tf_op | source)
XLA Modules:
  0.0 94.4 jit_solution(17535801980633537363)
XLA Ops:
  0.0 2.9 %shard_map.64 = (bf16[256,768]{1,0:T(8,128)(2,1)}, bf16[384,128]{1,0:T(8,128)(2,1)}, bf16[384,128]{1,0:T(8,128)(2,1)}, bf16[384,128]{1,0:T(8,128)(2,1)}, bf16[384,128]{1,0:T(8,128)(2,1)}) custom-call(bf16[256,768]{1,0:T(8,128)(2,1)} %bitcast.2, f32[768]{0:T(1024)} %refs_1_.2, bf16[768,768]{1,0:T(8,128)(2,1)} %refs_2_.2), custom_call_target="tpu_custom_call" | custom-call | flops 5000000000 | bytes 1000000 | tf_op jit(solution)/shard_map/pallas_call | solution.py:32
  2.9 2.0 %collective-permute-start.3 = (bf16[384,128]{1,0:T(8,128)(2,1)}, bf16[384,128]{1,0:T(8,128)(2,1)S(1)}, u32[]{:S(2)}, u32[]{:S(2)}) collective-permute-start(bf16[384,128]{1,0:T(8,128)(2,1)} %get-tuple-element.30), channel_id=1, source_target_pairs={{0,8},{8,0},{16,24},{24,16},{1,9},{9,1},{17,25},{25,17},{2,10},{10... | collective-permute-start | bytes 294920 | tf_op jit(solution)/shard_map/ppermute | solution.py:194
  4.9 3.3 %collective-permute-start.4 = (bf16[384,128]{1,0:T(8,128)(2,1)}, bf16[384,128]{1,0:T(8,128)(2,1)S(1)}, u32[]{:S(2)}, u32[]{:S(2)}) collective-permute-start(bf16[384,128]{1,0:T(8,128)(2,1)} %get-tuple-element.31), channel_id=1, source_target_pairs={{0,16},{8,24},{16,0},{24,8},{1,17},{9,25},{17,1},{25,9},{2,18},{10... | collective-permute-start | bytes 294920 | tf_op jit(solution)/shard_map/ppermute | solution.py:194
  8.2 1.0 %copy-done.4 = bf16[256,768]{1,0:T(8,128)(2,1)S(1)} copy-done((bf16[256,768]{1,0:T(8,128)(2,1)S(1)}, bf16[256,768]{1,0:T(8,128)(2,1)}, u32[]{:S(2)}) %copy-start.4) | copy-done | bytes 393240
  10.1 6.0 %collective-permute-done.4.refs_2_ = bf16[384,128]{1,0:T(8,128)(2,1)S(1)} collective-permute-done((bf16[384,128]{1,0:T(8,128)(2,1)}, bf16[384,128]{1,0:T(8,128)(2,1)S(1)}, u32[]{:S(2)}, u32[]{:S(2)}) %collective-permute-start.4) | collective-permute-done | bytes 98336 | tf_op jit(solution)/shard_map/ppermute | solution.py:194
  16.2 1.7 %collective-permute-start.6 = (bf16[384,512]{1,0:T(8,128)(2,1)S(1)}, bf16[384,512]{1,0:T(8,128)(2,1)S(1)}, u32[]{:S(2)}, u32[]{:S(2)}) collective-permute-start(bf16[384,512]{1,0:T(8,128)(2,1)S(1)} %shard_map.66.refs_4_), channel_id=1, source_target_pairs={{0,2},{2,4},{4,6},{6,0},{1,3},{3,5},{5,7},{7,1},{8,10},{10,12},{12... | collective-permute-start | bytes 1179656 | tf_op jit(solution)/shard_map/ppermute | solution.py:202
  17.9 1.7 %collective-permute-start.7 = (bf16[384,512]{1,0:T(8,128)(2,1)S(1)}, bf16[384,512]{1,0:T(8,128)(2,1)S(1)}, u32[]{:S(2)}, u32[]{:S(2)}) collective-permute-start(bf16[384,512]{1,0:T(8,128)(2,1)S(1)} %shard_map.66.refs_4_), channel_id=1, source_target_pairs={{0,6},{2,0},{4,2},{6,4},{1,7},{3,1},{5,3},{7,5},{8,14},{10,8},{12,... | collective-permute-start | bytes 1179656 | tf_op jit(solution)/shard_map/ppermute | solution.py:202
  19.5 1.7 %collective-permute-start = (bf16[768,128]{1,0:T(8,128)(2,1)S(1)}, bf16[768,128]{1,0:T(8,128)(2,1)S(1)}, u32[]{:S(2)}, u32[]{:S(2)}) collective-permute-start(bf16[768,128]{1,0:T(8,128)(2,1)S(1)} %get-tuple-element.26), channel_id=1, source_target_pairs={{0,8},{8,0},{16,24},{24,16},{1,9},{9,1},{17,25},{25,17},{2,10},{10... | collective-permute-start | bytes 589832 | tf_op jit(solution)/shard_map/ppermute | solution.py:194
  21.2 2.0 %collective-permute-start.8 = (bf16[384,512]{1,0:T(8,128)(2,1)S(1)}, bf16[384,512]{1,0:T(8,128)(2,1)S(1)}, u32[]{:S(2)}, u32[]{:S(2)}) collective-permute-start(bf16[384,512]{1,0:T(8,128)(2,1)S(1)} %shard_map.66.refs_4_), channel_id=1, source_target_pairs={{0,4},{2,6},{4,0},{6,2},{1,5},{3,7},{5,1},{7,3},{8,12},{10,14},{12... | collective-permute-start | bytes 1179656 | tf_op jit(solution)/shard_map/ppermute | solution.py:202
  23.2 1.4 %collective-permute-start.1 = (bf16[768,128]{1,0:T(8,128)(2,1)S(1)}, bf16[768,128]{1,0:T(8,128)(2,1)S(1)}, u32[]{:S(2)}, u32[]{:S(2)}) collective-permute-start(bf16[768,128]{1,0:T(8,128)(2,1)S(1)} %get-tuple-element.27), channel_id=1, source_target_pairs={{0,16},{8,24},{16,0},{24,8},{1,17},{9,25},{17,1},{25,9},{2,18},{10... | collective-permute-start | bytes 589832 | tf_op jit(solution)/shard_map/ppermute | solution.py:194
  24.6 1.9 %collective-permute-done.refs_1_ = bf16[768,128]{1,0:T(8,128)(2,1)S(1)} collective-permute-done((bf16[768,128]{1,0:T(8,128)(2,1)S(1)}, bf16[768,128]{1,0:T(8,128)(2,1)S(1)}, u32[]{:S(2)}, u32[]{:S(2)}) %collective-permute-start) | collective-permute-done | bytes 196640 | tf_op jit(solution)/shard_map/ppermute | solution.py:194
  26.5 2.5 %collective-permute-start.2 = (bf16[768,128]{1,0:T(8,128)(2,1)S(1)}, bf16[768,128]{1,0:T(8,128)(2,1)S(1)}, u32[]{:S(2)}, u32[]{:S(2)}) collective-permute-start(bf16[768,128]{1,0:T(8,128)(2,1)S(1)} %get-tuple-element.28), channel_id=1, source_target_pairs={{0,24},{8,16},{16,8},{24,0},{1,25},{9,17},{17,9},{25,1},{2,26},{10... | collective-permute-start | bytes 589832 | tf_op jit(solution)/shard_map/ppermute | solution.py:194
  29.0 9.5 %collective-permute-done.1.refs_2_ = bf16[768,128]{1,0:T(8,128)(2,1)S(1)} collective-permute-done((bf16[768,128]{1,0:T(8,128)(2,1)S(1)}, bf16[768,128]{1,0:T(8,128)(2,1)S(1)}, u32[]{:S(2)}, u32[]{:S(2)}) %collective-permute-start.1) | collective-permute-done | bytes 196640 | tf_op jit(solution)/shard_map/ppermute | solution.py:194
  40.4 2.6 %collective-permute-start.20 = (bf16[384,512]{1,0:T(8,128)(2,1)S(1)}, bf16[384,512]{1,0:T(8,128)(2,1)S(1)}, u32[]{:S(2)}, u32[]{:S(2)}) collective-permute-start(bf16[384,512]{1,0:T(8,128)(2,1)S(1)} %shard_map.69.refs_4_), channel_id=1, source_target_pairs={{0,6},{2,0},{4,2},{6,4},{1,7},{3,1},{5,3},{7,5},{8,14},{10,8},{12,... | collective-permute-start | bytes 1179656 | tf_op jit(solution)/shard_map/ppermute | solution.py:202
  42.9 1.1 %shard_map.67 = (f32[96,1024]{1,0:T(8,128)S(1)}, bf16[96,1024]{1,0:T(8,128)(2,1)S(1)}, bf16[96,1024]{1,0:T(8,128)(2,1)S(1)}, bf16[96,1024]{1,0:T(8,128)(2,1)S(1)}) custom-call(bf16[768,128]{1,0:T(8,128)(2,1)S(1)} %get-tuple-element.25.refs_0_, bf16[768,128]{1,0:T(8,128)(2,1)S(1)} %collective-permute-done.refs_1_, ...), custom_call_target="tpu_custom_call" | custom-call | flops 5000000000 | bytes 1000000 | tf_op jit(solution)/shard_map/pallas_call | solution.py:32
  44.8 1.6 %collective-permute-start.14 = (bf16[96,1024]{1,0:T(8,128)(2,1)S(1)}, bf16[96,1024]{1,0:T(8,128)(2,1)S(1)}, u32[]{:S(2)}, u32[]{:S(2)}) collective-permute-start(bf16[96,1024]{1,0:T(8,128)(2,1)S(1)} %get-tuple-element.35), channel_id=1, source_target_pairs={{0,96},{32,0},{64,32},{96,64},{1,97},{33,1},{65,33},{97,65},{2,98}... | collective-permute-start | bytes 589832 | tf_op jit(solution)/shard_map/ppermute | solution.py:202
  46.3 1.4 %collective-permute-start.15 = (bf16[96,1024]{1,0:T(8,128)(2,1)S(1)}, bf16[96,1024]{1,0:T(8,128)(2,1)S(1)}, u32[]{:S(2)}, u32[]{:S(2)}) collective-permute-start(bf16[96,1024]{1,0:T(8,128)(2,1)S(1)} %get-tuple-element.36), channel_id=1, source_target_pairs={{0,64},{32,96},{64,0},{96,32},{1,65},{33,97},{65,1},{97,33},{2,66}... | collective-permute-start | bytes 589832 | tf_op jit(solution)/shard_map/ppermute | solution.py:202
  47.7 4.3 %collective-permute-done.18.refs_5_ = bf16[384,512]{1,0:T(8,128)(2,1)S(1)} collective-permute-done((bf16[384,512]{1,0:T(8,128)(2,1)S(1)}, bf16[384,512]{1,0:T(8,128)(2,1)S(1)}, u32[]{:S(2)}, u32[]{:S(2)}) %collective-permute-start.18) | collective-permute-done | bytes 393248 | tf_op jit(solution)/shard_map/ppermute | solution.py:202
  52.6 3.7 %collective-permute-done.14.refs_2_.refs_5_ = bf16[96,1024]{1,0:T(8,128)(2,1)S(1)} collective-permute-done((bf16[96,1024]{1,0:T(8,128)(2,1)S(1)}, bf16[96,1024]{1,0:T(8,128)(2,1)S(1)}, u32[]{:S(2)}, u32[]{:S(2)}) %collective-permute-start.14) | collective-permute-done | bytes 196640 | tf_op jit(solution)/shard_map/ppermute | solution.py:202
  56.3 1.3 %collective-permute-start.25 = (bf16[384,512]{1,0:T(8,128)(2,1)S(1)}, bf16[384,512]{1,0:T(8,128)(2,1)S(1)}, u32[]{:S(2)}, u32[]{:S(2)}) collective-permute-start(bf16[384,512]{1,0:T(8,128)(2,1)S(1)} %shard_map.71), channel_id=1, source_target_pairs={{0,4},{2,6},{4,0},{6,2},{1,5},{3,7},{5,1},{7,3},{8,12},{10,14},{12... | collective-permute-start | bytes 1179656 | tf_op jit(solution)/shard_map/ppermute | solution.py:202
  57.7 5.9 %collective-permute-start.16 = (bf16[96,1024]{1,0:T(8,128)(2,1)S(1)}, bf16[96,1024]{1,0:T(8,128)(2,1)S(1)}, u32[]{:S(2)}, u32[]{:S(2)}) collective-permute-start(bf16[96,1024]{1,0:T(8,128)(2,1)S(1)} %get-tuple-element.38), channel_id=1, source_target_pairs={{0,128},{128,0},{1,129},{129,1},{2,130},{130,2},{3,131},{131,3},{4... | collective-permute-start | bytes 589832 | tf_op jit(solution)/shard_map/ppermute | solution.py:248
  63.6 3.3 %collective-permute-done.25.refs_7_ = bf16[384,512]{1,0:T(8,128)(2,1)S(1)} collective-permute-done((bf16[384,512]{1,0:T(8,128)(2,1)S(1)}, bf16[384,512]{1,0:T(8,128)(2,1)S(1)}, u32[]{:S(2)}, u32[]{:S(2)}) %collective-permute-start.25) | collective-permute-done | bytes 393248 | tf_op jit(solution)/shard_map/ppermute | solution.py:202
  67.0 2.4 %collective-permute-done.16.refs_1_ = bf16[96,1024]{1,0:T(8,128)(2,1)S(1)} collective-permute-done((bf16[96,1024]{1,0:T(8,128)(2,1)S(1)}, bf16[96,1024]{1,0:T(8,128)(2,1)S(1)}, u32[]{:S(2)}, u32[]{:S(2)}) %collective-permute-start.16) | collective-permute-done | bytes 196640 | tf_op jit(solution)/shard_map/ppermute | solution.py:248
  69.7 1.9 %collective-permute-start.22 = (bf16[96,1024]{1,0:T(8,128)(2,1)S(1)}, bf16[96,1024]{1,0:T(8,128)(2,1)S(1)}, u32[]{:S(2)}, u32[]{:S(2)}) collective-permute-start(bf16[96,1024]{1,0:T(8,128)(2,1)S(1)} %shard_map.70.refs_0_), channel_id=1, source_target_pairs={{0,32},{32,64},{64,96},{96,0},{1,33},{33,65},{65,97},{97,1},{2,34}... | collective-permute-start | bytes 589832 | tf_op jit(solution)/shard_map/ppermute | solution.py:202
  71.9 1.3 %collective-permute-start.24 = (bf16[96,1024]{1,0:T(8,128)(2,1)S(1)}, bf16[96,1024]{1,0:T(8,128)(2,1)S(1)}, u32[]{:S(2)}, u32[]{:S(2)}) collective-permute-start(bf16[96,1024]{1,0:T(8,128)(2,1)S(1)} %shard_map.70.refs_0_), channel_id=1, source_target_pairs={{0,96},{32,0},{64,32},{96,64},{1,97},{33,1},{65,33},{97,65},{2,98}... | collective-permute-start | bytes 589832 | tf_op jit(solution)/shard_map/ppermute | solution.py:202
  73.2 5.1 %collective-permute-done.22.refs_1_ = bf16[96,1024]{1,0:T(8,128)(2,1)S(1)} collective-permute-done((bf16[96,1024]{1,0:T(8,128)(2,1)S(1)}, bf16[96,1024]{1,0:T(8,128)(2,1)S(1)}, u32[]{:S(2)}, u32[]{:S(2)}) %collective-permute-start.22) | collective-permute-done | bytes 196640 | tf_op jit(solution)/shard_map/ppermute | solution.py:202
  78.3 1.7 %collective-permute-done.23.refs_2_ = bf16[96,1024]{1,0:T(8,128)(2,1)S(1)} collective-permute-done((bf16[96,1024]{1,0:T(8,128)(2,1)S(1)}, bf16[96,1024]{1,0:T(8,128)(2,1)S(1)}, u32[]{:S(2)}, u32[]{:S(2)}) %collective-permute-start.23) | collective-permute-done | bytes 196640 | tf_op jit(solution)/shard_map/ppermute | solution.py:202
  80.0 2.0 %collective-permute-done.24.refs_3_ = bf16[96,1024]{1,0:T(8,128)(2,1)S(1)} collective-permute-done((bf16[96,1024]{1,0:T(8,128)(2,1)S(1)}, bf16[96,1024]{1,0:T(8,128)(2,1)S(1)}, u32[]{:S(2)}, u32[]{:S(2)}) %collective-permute-start.24) | collective-permute-done | bytes 196640 | tf_op jit(solution)/shard_map/ppermute | solution.py:202
  83.3 2.3 %collective-permute-start.28 = (bf16[384,128]{1,0:T(8,128)(2,1)S(1)}, bf16[384,128]{1,0:T(8,128)(2,1)S(1)}, u32[]{:S(2)}, u32[]{:S(2)}) collective-permute-start(bf16[384,128]{1,0:T(8,128)(2,1)S(1)} %get-tuple-element.41), channel_id=1, source_target_pairs={{0,16},{8,24},{16,0},{24,8},{1,17},{9,25},{17,1},{25,9},{2,18},{10... | collective-permute-start | bytes 294920 | tf_op jit(solution)/shard_map/ppermute | solution.py:194
  85.7 1.5 %collective-permute-start.29 = (bf16[384,128]{1,0:T(8,128)(2,1)S(1)}, bf16[384,128]{1,0:T(8,128)(2,1)S(1)}, u32[]{:S(2)}, u32[]{:S(2)}) collective-permute-start(bf16[384,128]{1,0:T(8,128)(2,1)S(1)} %get-tuple-element.42), channel_id=1, source_target_pairs={{0,24},{8,16},{16,8},{24,0},{1,25},{9,17},{17,9},{25,1},{2,26},{10... | collective-permute-start | bytes 294920 | tf_op jit(solution)/shard_map/ppermute | solution.py:194
  87.8 5.3 %collective-permute-done.28.refs_2_ = bf16[384,128]{1,0:T(8,128)(2,1)S(1)} collective-permute-done((bf16[384,128]{1,0:T(8,128)(2,1)S(1)}, bf16[384,128]{1,0:T(8,128)(2,1)S(1)}, u32[]{:S(2)}, u32[]{:S(2)}) %collective-permute-start.28) | collective-permute-done | bytes 98336 | tf_op jit(solution)/shard_map/ppermute | solution.py:194
  93.1 1.3 %shard_map.73 = bf16[256,768]{1,0:T(8,128)(2,1)} custom-call(bf16[384,128]{1,0:T(8,128)(2,1)S(1)} %get-tuple-element.39.refs_0_, bf16[384,128]{1,0:T(8,128)(2,1)S(1)} %collective-permute-done.27.refs_1_, bf16[384,128]{1,0:T(8,128)(2,1)S(1)} %collective-permute-done.28.refs_2_, bf16[384,128]{1,0:T(8,128)(2,1)S(1)} %collective-permute-done.29.refs_3_, ...), custom_call_target="tpu_custom_call" | custom-call | flops 5000000000 | bytes 1000000 | tf_op jit(solution)/shard_map/pallas_call | solution.py:32
  (50 shorter events, 7.0 us)
Async XLA Ops:
  2.9 7.2 %collective-permute-start.3 = (bf16[384,128]{1,0:T(8,128)(2,1)}, bf16[384,128]{1,0:T(8,128)(2,1)S(1)}, u32[]{:S(2)}, u32[]{:S(2)}) collective-permute-start(bf16[384,128]{1,0:T(8,128)(2,1)} %get-tuple-element.30), channel_id=1, source_target_pairs={{0,8},{8,0},{16,24},{24,16},{1,9},{9,1},{17,25},{25,17},{2,10},{10... | collective-permute-start | bytes 294920 | tf_op jit(solution)/shard_map/ppermute | solution.py:194
  4.9 11.2 %collective-permute-start.4 = (bf16[384,128]{1,0:T(8,128)(2,1)}, bf16[384,128]{1,0:T(8,128)(2,1)S(1)}, u32[]{:S(2)}, u32[]{:S(2)}) collective-permute-start(bf16[384,128]{1,0:T(8,128)(2,1)} %get-tuple-element.31), channel_id=1, source_target_pairs={{0,16},{8,24},{16,0},{24,8},{1,17},{9,25},{17,1},{25,9},{2,18},{10... | collective-permute-start | bytes 294920 | tf_op jit(solution)/shard_map/ppermute | solution.py:194
  8.2 8.0 %collective-permute-start.5 = (bf16[384,128]{1,0:T(8,128)(2,1)}, bf16[384,128]{1,0:T(8,128)(2,1)S(1)}, u32[]{:S(2)}, u32[]{:S(2)}) collective-permute-start(bf16[384,128]{1,0:T(8,128)(2,1)} %get-tuple-element.32), channel_id=1, source_target_pairs={{0,24},{8,16},{16,8},{24,0},{1,25},{9,17},{17,9},{25,1},{2,26},{10... | collective-permute-start | bytes 294920 | tf_op jit(solution)/shard_map/ppermute | solution.py:194
  16.2 22.3 %collective-permute-start.6 = (bf16[384,512]{1,0:T(8,128)(2,1)S(1)}, bf16[384,512]{1,0:T(8,128)(2,1)S(1)}, u32[]{:S(2)}, u32[]{:S(2)}) collective-permute-start(bf16[384,512]{1,0:T(8,128)(2,1)S(1)} %shard_map.66.refs_4_), channel_id=1, source_target_pairs={{0,2},{2,4},{4,6},{6,0},{1,3},{3,5},{5,7},{7,1},{8,10},{10,12},{12... | collective-permute-start | bytes 1179656 | tf_op jit(solution)/shard_map/ppermute | solution.py:202
  17.9 21.1 %collective-permute-start.7 = (bf16[384,512]{1,0:T(8,128)(2,1)S(1)}, bf16[384,512]{1,0:T(8,128)(2,1)S(1)}, u32[]{:S(2)}, u32[]{:S(2)}) collective-permute-start(bf16[384,512]{1,0:T(8,128)(2,1)S(1)} %shard_map.66.refs_4_), channel_id=1, source_target_pairs={{0,6},{2,0},{4,2},{6,4},{1,7},{3,1},{5,3},{7,5},{8,14},{10,8},{12,... | collective-permute-start | bytes 1179656 | tf_op jit(solution)/shard_map/ppermute | solution.py:202
  19.5 6.9 %collective-permute-start = (bf16[768,128]{1,0:T(8,128)(2,1)S(1)}, bf16[768,128]{1,0:T(8,128)(2,1)S(1)}, u32[]{:S(2)}, u32[]{:S(2)}) collective-permute-start(bf16[768,128]{1,0:T(8,128)(2,1)S(1)} %get-tuple-element.26), channel_id=1, source_target_pairs={{0,8},{8,0},{16,24},{24,16},{1,9},{9,1},{17,25},{25,17},{2,10},{10... | collective-permute-start | bytes 589832 | tf_op jit(solution)/shard_map/ppermute | solution.py:194
  21.2 17.9 %collective-permute-start.8 = (bf16[384,512]{1,0:T(8,128)(2,1)S(1)}, bf16[384,512]{1,0:T(8,128)(2,1)S(1)}, u32[]{:S(2)}, u32[]{:S(2)}) collective-permute-start(bf16[384,512]{1,0:T(8,128)(2,1)S(1)} %shard_map.66.refs_4_), channel_id=1, source_target_pairs={{0,4},{2,6},{4,0},{6,2},{1,5},{3,7},{5,1},{7,3},{8,12},{10,14},{12... | collective-permute-start | bytes 1179656 | tf_op jit(solution)/shard_map/ppermute | solution.py:202
  23.2 15.3 %collective-permute-start.1 = (bf16[768,128]{1,0:T(8,128)(2,1)S(1)}, bf16[768,128]{1,0:T(8,128)(2,1)S(1)}, u32[]{:S(2)}, u32[]{:S(2)}) collective-permute-start(bf16[768,128]{1,0:T(8,128)(2,1)S(1)} %get-tuple-element.27), channel_id=1, source_target_pairs={{0,16},{8,24},{16,0},{24,8},{1,17},{9,25},{17,1},{25,9},{2,18},{10... | collective-permute-start | bytes 589832 | tf_op jit(solution)/shard_map/ppermute | solution.py:194
  26.5 13.0 %collective-permute-start.2 = (bf16[768,128]{1,0:T(8,128)(2,1)S(1)}, bf16[768,128]{1,0:T(8,128)(2,1)S(1)}, u32[]{:S(2)}, u32[]{:S(2)}) collective-permute-start(bf16[768,128]{1,0:T(8,128)(2,1)S(1)} %get-tuple-element.28), channel_id=1, source_target_pairs={{0,24},{8,16},{16,8},{24,0},{1,25},{9,17},{17,9},{25,1},{2,26},{10... | collective-permute-start | bytes 589832 | tf_op jit(solution)/shard_map/ppermute | solution.py:194
  38.5 1.9 %collective-permute-start.9 = (bf16[384,512]{1,0:T(8,128)(2,1)S(1)}, bf16[384,512]{1,0:T(8,128)(2,1)S(1)}, u32[]{:S(2)}, u32[]{:S(2)}) collective-permute-start(bf16[384,512]{1,0:T(8,128)(2,1)S(1)} %shard_map.66.refs_4_), channel_id=1, source_target_pairs={{0,1},{1,0},{2,3},{3,2},{4,5},{5,4},{6,7},{7,6},{8,9},{9,8},{10,11... | collective-permute-start | bytes 1179656 | tf_op jit(solution)/shard_map/ppermute | solution.py:198
  38.5 4.4 %collective-permute-start.10 = (bf16[384,512]{1,0:T(8,128)(2,1)S(1)}, bf16[384,512]{1,0:T(8,128)(2,1)S(1)}, u32[]{:S(2)}, u32[]{:S(2)}) collective-permute-start(bf16[384,512]{1,0:T(8,128)(2,1)S(1)} %collective-permute-done.6.refs_5_), channel_id=1, source_target_pairs={{0,1},{1,0},{2,3},{3,2},{4,5},{5,4},{6,7},{7,6},{8,9},{9,8},{10,11... | collective-permute-start | bytes 1179656 | tf_op jit(solution)/shard_map/ppermute | solution.py:198
  39.0 3.9 %collective-permute-start.11 = (bf16[384,512]{1,0:T(8,128)(2,1)S(1)}, bf16[384,512]{1,0:T(8,128)(2,1)S(1)}, u32[]{:S(2)}, u32[]{:S(2)}) collective-permute-start(bf16[384,512]{1,0:T(8,128)(2,1)S(1)} %collective-permute-done.7.refs_6_), channel_id=1, source_target_pairs={{0,1},{1,0},{2,3},{3,2},{4,5},{5,4},{6,7},{7,6},{8,9},{9,8},{10,11... | collective-permute-start | bytes 1179656 | tf_op jit(solution)/shard_map/ppermute | solution.py:198
  39.1 3.8 %collective-permute-start.12 = (bf16[384,512]{1,0:T(8,128)(2,1)S(1)}, bf16[384,512]{1,0:T(8,128)(2,1)S(1)}, u32[]{:S(2)}, u32[]{:S(2)}) collective-permute-start(bf16[384,512]{1,0:T(8,128)(2,1)S(1)} %collective-permute-done.8.refs_7_), channel_id=1, source_target_pairs={{0,1},{1,0},{2,3},{3,2},{4,5},{5,4},{6,7},{7,6},{8,9},{9,8},{10,11... | collective-permute-start | bytes 1179656 | tf_op jit(solution)/shard_map/ppermute | solution.py:198
  39.6 12.4 %collective-permute-start.18 = (bf16[384,512]{1,0:T(8,128)(2,1)S(1)}, bf16[384,512]{1,0:T(8,128)(2,1)S(1)}, u32[]{:S(2)}, u32[]{:S(2)}) collective-permute-start(bf16[384,512]{1,0:T(8,128)(2,1)S(1)} %shard_map.69.refs_4_), channel_id=1, source_target_pairs={{0,2},{2,4},{4,6},{6,0},{1,3},{3,5},{5,7},{7,1},{8,10},{10,12},{12... | collective-permute-start | bytes 1179656 | tf_op jit(solution)/shard_map/ppermute | solution.py:202
  40.4 11.6 %collective-permute-start.20 = (bf16[384,512]{1,0:T(8,128)(2,1)S(1)}, bf16[384,512]{1,0:T(8,128)(2,1)S(1)}, u32[]{:S(2)}, u32[]{:S(2)}) collective-permute-start(bf16[384,512]{1,0:T(8,128)(2,1)S(1)} %shard_map.69.refs_4_), channel_id=1, source_target_pairs={{0,6},{2,0},{4,2},{6,4},{1,7},{3,1},{5,3},{7,5},{8,14},{10,8},{12,... | collective-permute-start | bytes 1179656 | tf_op jit(solution)/shard_map/ppermute | solution.py:202
  44.1 8.5 %collective-permute-start.13 = (bf16[96,1024]{1,0:T(8,128)(2,1)S(1)}, bf16[96,1024]{1,0:T(8,128)(2,1)S(1)}, u32[]{:S(2)}, u32[]{:S(2)}) collective-permute-start(bf16[96,1024]{1,0:T(8,128)(2,1)S(1)} %get-tuple-element.34), channel_id=1, source_target_pairs={{0,32},{32,64},{64,96},{96,0},{1,33},{33,65},{65,97},{97,1},{2,34}... | collective-permute-start | bytes 589832 | tf_op jit(solution)/shard_map/ppermute | solution.py:202
  44.8 11.5 %collective-permute-start.14 = (bf16[96,1024]{1,0:T(8,128)(2,1)S(1)}, bf16[96,1024]{1,0:T(8,128)(2,1)S(1)}, u32[]{:S(2)}, u32[]{:S(2)}) collective-permute-start(bf16[96,1024]{1,0:T(8,128)(2,1)S(1)} %get-tuple-element.35), channel_id=1, source_target_pairs={{0,96},{32,0},{64,32},{96,64},{1,97},{33,1},{65,33},{97,65},{2,98}... | collective-permute-start | bytes 589832 | tf_op jit(solution)/shard_map/ppermute | solution.py:202
  46.3 9.9 %collective-permute-start.15 = (bf16[96,1024]{1,0:T(8,128)(2,1)S(1)}, bf16[96,1024]{1,0:T(8,128)(2,1)S(1)}, u32[]{:S(2)}, u32[]{:S(2)}) collective-permute-start(bf16[96,1024]{1,0:T(8,128)(2,1)S(1)} %get-tuple-element.36), channel_id=1, source_target_pairs={{0,64},{32,96},{64,0},{96,32},{1,65},{33,97},{65,1},{97,33},{2,66}... | collective-permute-start | bytes 589832 | tf_op jit(solution)/shard_map/ppermute | solution.py:202
  52.0 15.0 %collective-permute-start.17 = (bf16[384,512]{1,0:T(8,128)(2,1)S(1)}, bf16[384,512]{1,0:T(8,128)(2,1)S(1)}, u32[]{:S(2)}, u32[]{:S(2)}) collective-permute-start(bf16[384,512]{1,0:T(8,128)(2,1)S(1)} %shard_map.69.refs_4_), channel_id=1, source_target_pairs={{0,1},{1,0},{2,3},{3,2},{4,5},{5,4},{6,7},{7,6},{8,9},{9,8},{10,11... | collective-permute-start | bytes 1179656 | tf_op jit(solution)/shard_map/ppermute | solution.py:198
  52.0 15.0 %collective-permute-start.19 = (bf16[384,512]{1,0:T(8,128)(2,1)S(1)}, bf16[384,512]{1,0:T(8,128)(2,1)S(1)}, u32[]{:S(2)}, u32[]{:S(2)}) collective-permute-start(bf16[384,512]{1,0:T(8,128)(2,1)S(1)} %collective-permute-done.18.refs_5_), channel_id=1, source_target_pairs={{0,1},{1,0},{2,3},{3,2},{4,5},{5,4},{6,7},{7,6},{8,9},{9,8},{10,11... | collective-permute-start | bytes 1179656 | tf_op jit(solution)/shard_map/ppermute | solution.py:198
  52.5 14.5 %collective-permute-start.21 = (bf16[384,512]{1,0:T(8,128)(2,1)S(1)}, bf16[384,512]{1,0:T(8,128)(2,1)S(1)}, u32[]{:S(2)}, u32[]{:S(2)}) collective-permute-start(bf16[384,512]{1,0:T(8,128)(2,1)S(1)} %collective-permute-done.20.refs_6_), channel_id=1, source_target_pairs={{0,1},{1,0},{2,3},{3,2},{4,5},{5,4},{6,7},{7,6},{8,9},{9,8},{10,11... | collective-permute-start | bytes 1179656 | tf_op jit(solution)/shard_map/ppermute | solution.py:198
  56.3 10.7 %collective-permute-start.25 = (bf16[384,512]{1,0:T(8,128)(2,1)S(1)}, bf16[384,512]{1,0:T(8,128)(2,1)S(1)}, u32[]{:S(2)}, u32[]{:S(2)}) collective-permute-start(bf16[384,512]{1,0:T(8,128)(2,1)S(1)} %shard_map.71), channel_id=1, source_target_pairs={{0,4},{2,6},{4,0},{6,2},{1,5},{3,7},{5,1},{7,3},{8,12},{10,14},{12... | collective-permute-start | bytes 1179656 | tf_op jit(solution)/shard_map/ppermute | solution.py:202
  57.7 11.7 %collective-permute-start.16 = (bf16[96,1024]{1,0:T(8,128)(2,1)S(1)}, bf16[96,1024]{1,0:T(8,128)(2,1)S(1)}, u32[]{:S(2)}, u32[]{:S(2)}) collective-permute-start(bf16[96,1024]{1,0:T(8,128)(2,1)S(1)} %get-tuple-element.38), channel_id=1, source_target_pairs={{0,128},{128,0},{1,129},{129,1},{2,130},{130,2},{3,131},{131,3},{4... | collective-permute-start | bytes 589832 | tf_op jit(solution)/shard_map/ppermute | solution.py:248
  67.0 15.0 %collective-permute-start.26 = (bf16[384,512]{1,0:T(8,128)(2,1)S(1)}, bf16[384,512]{1,0:T(8,128)(2,1)S(1)}, u32[]{:S(2)}, u32[]{:S(2)}) collective-permute-start(bf16[384,512]{1,0:T(8,128)(2,1)S(1)} %collective-permute-done.25.refs_7_), channel_id=1, source_target_pairs={{0,1},{1,0},{2,3},{3,2},{4,5},{5,4},{6,7},{7,6},{8,9},{9,8},{10,11... | collective-permute-start | bytes 1179656 | tf_op jit(solution)/shard_map/ppermute | solution.py:198
  69.6 23.5 %copy-start.2 = (bf16[768,768]{1,0:T(8,128)(2,1)S(1)}, bf16[768,768]{1,0:T(8,128)(2,1)}, u32[]{:S(2)}) copy-start(bf16[768,768]{1,0:T(8,128)(2,1)} %refs_5_.1) | copy-start | bytes 3538948
  69.7 23.4 %copy-start.3 = (bf16[8,32,768]{2,1,0:T(8,128)(2,1)S(1)}, bf16[8,32,768]{2,1,0:T(8,128)(2,1)}, u32[]{:S(2)}) copy-start(bf16[8,32,768]{2,1,0:T(8,128)(2,1)} %param.6) | copy-start | bytes 1179652
  69.7 8.6 %collective-permute-start.22 = (bf16[96,1024]{1,0:T(8,128)(2,1)S(1)}, bf16[96,1024]{1,0:T(8,128)(2,1)S(1)}, u32[]{:S(2)}, u32[]{:S(2)}) collective-permute-start(bf16[96,1024]{1,0:T(8,128)(2,1)S(1)} %shard_map.70.refs_0_), channel_id=1, source_target_pairs={{0,32},{32,64},{64,96},{96,0},{1,33},{33,65},{65,97},{97,1},{2,34}... | collective-permute-start | bytes 589832 | tf_op jit(solution)/shard_map/ppermute | solution.py:202
  71.6 8.4 %collective-permute-start.23 = (bf16[96,1024]{1,0:T(8,128)(2,1)S(1)}, bf16[96,1024]{1,0:T(8,128)(2,1)S(1)}, u32[]{:S(2)}, u32[]{:S(2)}) collective-permute-start(bf16[96,1024]{1,0:T(8,128)(2,1)S(1)} %shard_map.70.refs_0_), channel_id=1, source_target_pairs={{0,64},{32,96},{64,0},{96,32},{1,65},{33,97},{65,1},{97,33},{2,66}... | collective-permute-start | bytes 589832 | tf_op jit(solution)/shard_map/ppermute | solution.py:202
  71.9 10.1 %collective-permute-start.24 = (bf16[96,1024]{1,0:T(8,128)(2,1)S(1)}, bf16[96,1024]{1,0:T(8,128)(2,1)S(1)}, u32[]{:S(2)}, u32[]{:S(2)}) collective-permute-start(bf16[96,1024]{1,0:T(8,128)(2,1)S(1)} %shard_map.70.refs_0_), channel_id=1, source_target_pairs={{0,96},{32,0},{64,32},{96,64},{1,97},{33,1},{65,33},{97,65},{2,98}... | collective-permute-start | bytes 589832 | tf_op jit(solution)/shard_map/ppermute | solution.py:202
  82.6 5.2 %collective-permute-start.27 = (bf16[384,128]{1,0:T(8,128)(2,1)S(1)}, bf16[384,128]{1,0:T(8,128)(2,1)S(1)}, u32[]{:S(2)}, u32[]{:S(2)}) collective-permute-start(bf16[384,128]{1,0:T(8,128)(2,1)S(1)} %get-tuple-element.40), channel_id=1, source_target_pairs={{0,8},{8,0},{16,24},{24,16},{1,9},{9,1},{17,25},{25,17},{2,10},{10... | collective-permute-start | bytes 294920 | tf_op jit(solution)/shard_map/ppermute | solution.py:194
  83.3 9.8 %collective-permute-start.28 = (bf16[384,128]{1,0:T(8,128)(2,1)S(1)}, bf16[384,128]{1,0:T(8,128)(2,1)S(1)}, u32[]{:S(2)}, u32[]{:S(2)}) collective-permute-start(bf16[384,128]{1,0:T(8,128)(2,1)S(1)} %get-tuple-element.41), channel_id=1, source_target_pairs={{0,16},{8,24},{16,0},{24,8},{1,17},{9,25},{17,1},{25,9},{2,18},{10... | collective-permute-start | bytes 294920 | tf_op jit(solution)/shard_map/ppermute | solution.py:194
  85.7 7.4 %collective-permute-start.29 = (bf16[384,128]{1,0:T(8,128)(2,1)S(1)}, bf16[384,128]{1,0:T(8,128)(2,1)S(1)}, u32[]{:S(2)}, u32[]{:S(2)}) collective-permute-start(bf16[384,128]{1,0:T(8,128)(2,1)S(1)} %get-tuple-element.42), channel_id=1, source_target_pairs={{0,24},{8,16},{16,8},{24,0},{1,25},{9,17},{17,9},{25,1},{2,26},{10... | collective-permute-start | bytes 294920 | tf_op jit(solution)/shard_map/ppermute | solution.py:194
  (4 other events, 24.3 us)

commit v3 on v2

--- a/solution.py
+++ b/solution.py
@@ -18,10 +18,9 @@
 VMEM = pl.BlockSpec(memory_space=pltpu.VMEM)
 FAR = pl.BlockSpec(memory_space=pltpu.HBM)
 LIMIT = 48 * 1024 * 1024
-MOST = 60 * 1024 * 1024
-
-
-def call(body, outs, scratch=(), flops=5000000000, moved=1000000, places=None, after=(), limit=LIMIT):
+
+
+def call(body, outs, scratch=(), flops=5000000000, moved=1000000, places=None, after=()):
     def run(*args):
         count = len(args)
 
@@ -35,7 +34,7 @@
             in_specs=specs + [FAR] * len(after),
             out_specs=[VMEM] * len(outs),
             scratch_shapes=list(scratch),
-            compiler_params=pltpu.CompilerParams(vmem_limit_bytes=limit),
+            compiler_params=pltpu.CompilerParams(vmem_limit_bytes=LIMIT),
             cost_estimate=pl.CostEstimate(
                 flops=flops, bytes_accessed=moved, transcendentals=0
             ),
@@ -69,7 +68,7 @@
     var = jnp.mean(off * off, axis=-1, keepdims=True)
     copies[1].wait()
     gain = gain_ref[...].reshape(1, HEADS * SIZE)
-    normed = (off / jnp.sqrt(var + 1e-05) * gain).astype(BF16)
+    normed = (off * lax.rsqrt(var + 1e-05) * gain).astype(BF16)
     normed_ref[...] = normed
     copies[2].wait()
     spread(normed, w_ref, (o0, o1, o2, o3), held)
@@ -135,6 +134,10 @@
     sent[...] = s.astype(BF16)
 
 
+def copy_kernel(old, new):
+    new[...] = old[...]
+
+
 def softmax_kernel(scale, total, other, probs):
     logits = (total[...] + other[...].astype(F32)) * scale
     top = jnp.max(logits, axis=-1, keepdims=True)
@@ -209,6 +212,7 @@
     whole = ((384, 512), BF16)
     weights = pltpu.VMEM((768, 768), BF16)
     pieces = pltpu.VMEM((4, 384, 128), BF16)
+    at_rest = [pltpu.with_memory_space_constraint(a, pltpu.HBM) for a in (flat, gain, wk)]
     normed, *keys = call(
         key_kernel,
         [((256, 768), BF16)] + [piece] * 4,
@@ -220,8 +224,7 @@
             pltpu.SemaphoreType.DMA((3,)),
         ],
         places={0: FAR, 1: FAR, 2: FAR},
-        limit=MOST,
-    )(flat, gain, wk)
+    )(*at_rest)
     keys = line(keys)
 
     def slab(parts, base, after=()):
@@ -242,7 +245,8 @@
     first = slab(pairs, 384)
     slabs = [first] + over("y", [first] * 4, (1, 3))
     swapped = other_core(slabs)
-    last = over("y", [slab(pairs, 384, got)] * 4, (2,))
+    (passed,) = call(copy_kernel, [whole], after=got)(slabs[2])
+    last = over("y", [passed] * 4, (3,))
     slabs += last + swapped + other_core(last)
     total, sent = call(sum_kernel, [((96, 1024), F32), part])(own, *got)
     other = lax.ppermute(sent, "zh", [(0, 1), (1, 0)])

time: 94.6 us -> 92.7 us (0.980)
  local copies, waits for them, and re-layouts: 1.01 us -> 0.02 us
    ppermute x12, waiting for transfers between devices: 20 us -> 18.2 us  [over(): return [lax.ppermute(arrays[k], axis, RING[k]) for k in order]]
    ppermute x1, waiting for transfers between devices: 2.39 us -> 3.55 us  [per_device(): other = lax.ppermute(sent, 'zh', [(0, 1), (1, 0)])]
    ppermute x9, waiting for transfers between devices: 23.4 us -> 24.5 us  [line(): lax.ppermute(pieces[m], 'zl', LINE[m])]
    unnamed x12 -> x8, local copies, waits for them, and re-layouts: 1.01 us -> 0.02 us
  transfers between devices with their start and end apart: 30 -> 30, of which waited for: 12 -> 14; matrix products, arithmetic and copies ran while one was open for 0% -> 0% of each run, Pallas kernels for 3% -> 3%
where the time goes in v3:
time: 92.7 us
  waiting for transfers between devices  46.4 us (50%)
  starting transfers between devices  39.4 us (43%)
  Pallas kernels  6.69 us (7%)
    ppermute x9, waiting for transfers between devices, line(): lax.ppermute(pieces[m], 'zl', LINE[m])  24.5 us
    ppermute x12, waiting for transfers between devices, over(): return [lax.ppermute(arrays[k], axis, RING[k]) for k in order]  18.2 us
    ppermute x12, starting transfers between devices, over(): return [lax.ppermute(arrays[k], axis, RING[k]) for k in order]  16.5 us
    ppermute x9, starting transfers between devices, line(): lax.ppermute(pieces[m], 'zl', LINE[m])  15.5 us
    pallas_call x10, Pallas kernels, run(): pl.pallas_call(kernel, out_shape=[jax.ShapeDtypeStruct(s, d) for s, d in...  6.69 us
    ppermute x1, starting transfers between devices, per_device(): other = lax.ppermute(sent, 'zh', [(0, 1), (1, 0)])  5.93 us
    ppermute x1, waiting for transfers between devices, per_device(): other = lax.ppermute(sent, 'zh', [(0, 1), (1, 0)])  3.55 us
  transfers between devices with their start and end apart: 30, of which 14 were waited for; matrix products, arithmetic and copies ran while one was open for 0% of the time, Pallas kernels for 3%

profile of v3, /device:TPU:6, one launch (start us, length us, event | category | flops | bytes accessed | tf_op | source)
XLA Modules:
  0.0 92.7 jit_solution(4072253429529316913)
XLA Ops:
  0.0 2.2 %shard_map.64 = (bf16[256,768]{1,0:T(8,128)(2,1)S(1)}, bf16[384,128]{1,0:T(8,128)(2,1)S(1)}, bf16[384,128]{1,0:T(8,128)(2,1)S(1)}, bf16[384,128]{1,0:T(8,128)(2,1)S(1)}, bf16[384,128]{1,0:T(8,128)(2,1)S(1)}) custom-call(bf16[256,768]{1,0:T(8,128)(2,1)} %bitcast.2, f32[768]{0:T(1024)} %refs_1_.2, bf16[768,768]{1,0:T(8,128)(2,1)} %refs_2_.2), custom_call_target="tpu_custom_call" | custom-call | flops 5000000000 | bytes 1000000 | tf_op jit(solution)/shard_map/pallas_call | solution.py:31
  2.2 2.0 %collective-permute-start.3 = (bf16[384,128]{1,0:T(8,128)(2,1)S(1)}, bf16[384,128]{1,0:T(8,128)(2,1)S(1)}, u32[]{:S(2)}, u32[]{:S(2)}) collective-permute-start(bf16[384,128]{1,0:T(8,128)(2,1)S(1)} %get-tuple-element.30), channel_id=1, source_target_pairs={{0,8},{8,0},{16,24},{24,16},{1,9},{9,1},{17,25},{25,17},{2,10},{10... | collective-permute-start | bytes 294920 | tf_op jit(solution)/shard_map/ppermute | solution.py:197
  4.2 3.3 %collective-permute-start.4 = (bf16[384,128]{1,0:T(8,128)(2,1)S(1)}, bf16[384,128]{1,0:T(8,128)(2,1)S(1)}, u32[]{:S(2)}, u32[]{:S(2)}) collective-permute-start(bf16[384,128]{1,0:T(8,128)(2,1)S(1)} %get-tuple-element.31), channel_id=1, source_target_pairs={{0,16},{8,24},{16,0},{24,8},{1,17},{9,25},{17,1},{25,9},{2,18},{10... | collective-permute-start | bytes 294920 | tf_op jit(solution)/shard_map/ppermute | solution.py:197
  8.4 6.8 %collective-permute-done.4.refs_2_ = bf16[384,128]{1,0:T(8,128)(2,1)S(1)} collective-permute-done((bf16[384,128]{1,0:T(8,128)(2,1)S(1)}, bf16[384,128]{1,0:T(8,128)(2,1)S(1)}, u32[]{:S(2)}, u32[]{:S(2)}) %collective-permute-start.4) | collective-permute-done | bytes 98336 | tf_op jit(solution)/shard_map/ppermute | solution.py:197
  15.3 1.7 %collective-permute-start.6 = (bf16[384,512]{1,0:T(8,128)(2,1)S(1)}, bf16[384,512]{1,0:T(8,128)(2,1)S(1)}, u32[]{:S(2)}, u32[]{:S(2)}) collective-permute-start(bf16[384,512]{1,0:T(8,128)(2,1)S(1)} %shard_map.66.refs_4_), channel_id=1, source_target_pairs={{0,2},{2,4},{4,6},{6,0},{1,3},{3,5},{5,7},{7,1},{8,10},{10,12},{12... | collective-permute-start | bytes 1179656 | tf_op jit(solution)/shard_map/ppermute | solution.py:205
  16.9 1.7 %collective-permute-start.7 = (bf16[384,512]{1,0:T(8,128)(2,1)S(1)}, bf16[384,512]{1,0:T(8,128)(2,1)S(1)}, u32[]{:S(2)}, u32[]{:S(2)}) collective-permute-start(bf16[384,512]{1,0:T(8,128)(2,1)S(1)} %shard_map.66.refs_4_), channel_id=1, source_target_pairs={{0,6},{2,0},{4,2},{6,4},{1,7},{3,1},{5,3},{7,5},{8,14},{10,8},{12,... | collective-permute-start | bytes 1179656 | tf_op jit(solution)/shard_map/ppermute | solution.py:205
  18.6 1.7 %collective-permute-start = (bf16[768,128]{1,0:T(8,128)(2,1)S(1)}, bf16[768,128]{1,0:T(8,128)(2,1)S(1)}, u32[]{:S(2)}, u32[]{:S(2)}) collective-permute-start(bf16[768,128]{1,0:T(8,128)(2,1)S(1)} %get-tuple-element.26), channel_id=1, source_target_pairs={{0,8},{8,0},{16,24},{24,16},{1,9},{9,1},{17,25},{25,17},{2,10},{10... | collective-permute-start | bytes 589832 | tf_op jit(solution)/shard_map/ppermute | solution.py:197
  20.3 2.0 %collective-permute-start.8 = (bf16[384,512]{1,0:T(8,128)(2,1)S(1)}, bf16[384,512]{1,0:T(8,128)(2,1)S(1)}, u32[]{:S(2)}, u32[]{:S(2)}) collective-permute-start(bf16[384,512]{1,0:T(8,128)(2,1)S(1)} %shard_map.66.refs_4_), channel_id=1, source_target_pairs={{0,4},{2,6},{4,0},{6,2},{1,5},{3,7},{5,1},{7,3},{8,12},{10,14},{12... | collective-permute-start | bytes 1179656 | tf_op jit(solution)/shard_map/ppermute | solution.py:205
  22.2 1.4 %collective-permute-start.1 = (bf16[768,128]{1,0:T(8,128)(2,1)S(1)}, bf16[768,128]{1,0:T(8,128)(2,1)S(1)}, u32[]{:S(2)}, u32[]{:S(2)}) collective-permute-start(bf16[768,128]{1,0:T(8,128)(2,1)S(1)} %get-tuple-element.27), channel_id=1, source_target_pairs={{0,16},{8,24},{16,0},{24,8},{1,17},{9,25},{17,1},{25,9},{2,18},{10... | collective-permute-start | bytes 589832 | tf_op jit(solution)/shard_map/ppermute | solution.py:197
  23.6 1.9 %collective-permute-done.refs_1_ = bf16[768,128]{1,0:T(8,128)(2,1)S(1)} collective-permute-done((bf16[768,128]{1,0:T(8,128)(2,1)S(1)}, bf16[768,128]{1,0:T(8,128)(2,1)S(1)}, u32[]{:S(2)}, u32[]{:S(2)}) %collective-permute-start) | collective-permute-done | bytes 196640 | tf_op jit(solution)/shard_map/ppermute | solution.py:197
  25.6 2.5 %collective-permute-start.2 = (bf16[768,128]{1,0:T(8,128)(2,1)S(1)}, bf16[768,128]{1,0:T(8,128)(2,1)S(1)}, u32[]{:S(2)}, u32[]{:S(2)}) collective-permute-start(bf16[768,128]{1,0:T(8,128)(2,1)S(1)} %get-tuple-element.28), channel_id=1, source_target_pairs={{0,24},{8,16},{16,8},{24,0},{1,25},{9,17},{17,9},{25,1},{2,26},{10... | collective-permute-start | bytes 589832 | tf_op jit(solution)/shard_map/ppermute | solution.py:197
  28.1 9.5 %collective-permute-done.1.refs_2_ = bf16[768,128]{1,0:T(8,128)(2,1)S(1)} collective-permute-done((bf16[768,128]{1,0:T(8,128)(2,1)S(1)}, bf16[768,128]{1,0:T(8,128)(2,1)S(1)}, u32[]{:S(2)}, u32[]{:S(2)}) %collective-permute-start.1) | collective-permute-done | bytes 196640 | tf_op jit(solution)/shard_map/ppermute | solution.py:197
  38.6 1.4 %collective-permute-start.20 = (bf16[384,512]{1,0:T(8,128)(2,1)S(1)}, bf16[384,512]{1,0:T(8,128)(2,1)S(1)}, u32[]{:S(2)}, u32[]{:S(2)}) collective-permute-start(bf16[384,512]{1,0:T(8,128)(2,1)S(1)} %shard_map.69.refs_4_), channel_id=1, source_target_pairs={{0,6},{2,0},{4,2},{6,4},{1,7},{3,1},{5,3},{7,5},{8,14},{10,8},{12,... | collective-permute-start | bytes 1179656 | tf_op jit(solution)/shard_map/ppermute | solution.py:205
  42.8 1.5 %collective-permute-start.14 = (bf16[96,1024]{1,0:T(8,128)(2,1)S(1)}, bf16[96,1024]{1,0:T(8,128)(2,1)S(1)}, u32[]{:S(2)}, u32[]{:S(2)}) collective-permute-start(bf16[96,1024]{1,0:T(8,128)(2,1)S(1)} %get-tuple-element.35), channel_id=1, source_target_pairs={{0,96},{32,0},{64,32},{96,64},{1,97},{33,1},{65,33},{97,65},{2,98}... | collective-permute-start | bytes 589832 | tf_op jit(solution)/shard_map/ppermute | solution.py:205
  44.4 1.4 %collective-permute-start.15 = (bf16[96,1024]{1,0:T(8,128)(2,1)S(1)}, bf16[96,1024]{1,0:T(8,128)(2,1)S(1)}, u32[]{:S(2)}, u32[]{:S(2)}) collective-permute-start(bf16[96,1024]{1,0:T(8,128)(2,1)S(1)} %get-tuple-element.36), channel_id=1, source_target_pairs={{0,64},{32,96},{64,0},{96,32},{1,65},{33,97},{65,1},{97,33},{2,66}... | collective-permute-start | bytes 589832 | tf_op jit(solution)/shard_map/ppermute | solution.py:205
  45.8 4.1 %collective-permute-done.20.refs_0_.refs_6_ = bf16[384,512]{1,0:T(8,128)(2,1)S(1)} collective-permute-done((bf16[384,512]{1,0:T(8,128)(2,1)S(1)}, bf16[384,512]{1,0:T(8,128)(2,1)S(1)}, u32[]{:S(2)}, u32[]{:S(2)}) %collective-permute-start.20) | collective-permute-done | bytes 393248 | tf_op jit(solution)/shard_map/ppermute | solution.py:205
  49.8 2.2 %collective-permute-done.18.refs_5_ = bf16[384,512]{1,0:T(8,128)(2,1)S(1)} collective-permute-done((bf16[384,512]{1,0:T(8,128)(2,1)S(1)}, bf16[384,512]{1,0:T(8,128)(2,1)S(1)}, u32[]{:S(2)}, u32[]{:S(2)}) %collective-permute-start.18) | collective-permute-done | bytes 393248 | tf_op jit(solution)/shard_map/ppermute | solution.py:205
  52.6 2.3 %collective-permute-done.14.refs_2_ = bf16[96,1024]{1,0:T(8,128)(2,1)S(1)} collective-permute-done((bf16[96,1024]{1,0:T(8,128)(2,1)S(1)}, bf16[96,1024]{1,0:T(8,128)(2,1)S(1)}, u32[]{:S(2)}, u32[]{:S(2)}) %collective-permute-start.14) | collective-permute-done | bytes 196640 | tf_op jit(solution)/shard_map/ppermute | solution.py:205
  54.9 1.8 %collective-permute-start.25 = (bf16[384,512]{1,0:T(8,128)(2,1)S(1)}, bf16[384,512]{1,0:T(8,128)(2,1)S(1)}, u32[]{:S(2)}, u32[]{:S(2)}) collective-permute-start(bf16[384,512]{1,0:T(8,128)(2,1)S(1)} %shard_map.71), channel_id=1, source_target_pairs={{0,6},{2,0},{4,2},{6,4},{1,7},{3,1},{5,3},{7,5},{8,14},{10,8},{12,... | collective-permute-start | bytes 1179656 | tf_op jit(solution)/shard_map/ppermute | solution.py:205
  56.8 5.9 %collective-permute-start.16 = (bf16[96,1024]{1,0:T(8,128)(2,1)S(1)}, bf16[96,1024]{1,0:T(8,128)(2,1)S(1)}, u32[]{:S(2)}, u32[]{:S(2)}) collective-permute-start(bf16[96,1024]{1,0:T(8,128)(2,1)S(1)} %get-tuple-element.38), channel_id=1, source_target_pairs={{0,128},{128,0},{1,129},{129,1},{2,130},{130,2},{3,131},{131,3},{4... | collective-permute-start | bytes 589832 | tf_op jit(solution)/shard_map/ppermute | solution.py:252
  62.8 2.0 %collective-permute-done.25.refs_7_ = bf16[384,512]{1,0:T(8,128)(2,1)S(1)} collective-permute-done((bf16[384,512]{1,0:T(8,128)(2,1)S(1)}, bf16[384,512]{1,0:T(8,128)(2,1)S(1)}, u32[]{:S(2)}, u32[]{:S(2)}) %collective-permute-start.25) | collective-permute-done | bytes 393248 | tf_op jit(solution)/shard_map/ppermute | solution.py:205
  64.8 3.5 %collective-permute-done.16.refs_1_ = bf16[96,1024]{1,0:T(8,128)(2,1)S(1)} collective-permute-done((bf16[96,1024]{1,0:T(8,128)(2,1)S(1)}, bf16[96,1024]{1,0:T(8,128)(2,1)S(1)}, u32[]{:S(2)}, u32[]{:S(2)}) %collective-permute-start.16) | collective-permute-done | bytes 196640 | tf_op jit(solution)/shard_map/ppermute | solution.py:252
  68.6 1.3 %collective-permute-start.22 = (bf16[96,1024]{1,0:T(8,128)(2,1)S(1)}, bf16[96,1024]{1,0:T(8,128)(2,1)S(1)}, u32[]{:S(2)}, u32[]{:S(2)}) collective-permute-start(bf16[96,1024]{1,0:T(8,128)(2,1)S(1)} %shard_map.70.refs_0_), channel_id=1, source_target_pairs={{0,32},{32,64},{64,96},{96,0},{1,33},{33,65},{65,97},{97,1},{2,34}... | collective-permute-start | bytes 589832 | tf_op jit(solution)/shard_map/ppermute | solution.py:205
  71.0 1.2 %collective-permute-start.24 = (bf16[96,1024]{1,0:T(8,128)(2,1)S(1)}, bf16[96,1024]{1,0:T(8,128)(2,1)S(1)}, u32[]{:S(2)}, u32[]{:S(2)}) collective-permute-start(bf16[96,1024]{1,0:T(8,128)(2,1)S(1)} %shard_map.70.refs_0_), channel_id=1, source_target_pairs={{0,96},{32,0},{64,32},{96,64},{1,97},{33,1},{65,33},{97,65},{2,98}... | collective-permute-start | bytes 589832 | tf_op jit(solution)/shard_map/ppermute | solution.py:205
  72.2 3.8 %collective-permute-done.22.refs_1_ = bf16[96,1024]{1,0:T(8,128)(2,1)S(1)} collective-permute-done((bf16[96,1024]{1,0:T(8,128)(2,1)S(1)}, bf16[96,1024]{1,0:T(8,128)(2,1)S(1)}, u32[]{:S(2)}, u32[]{:S(2)}) %collective-permute-start.22) | collective-permute-done | bytes 196640 | tf_op jit(solution)/shard_map/ppermute | solution.py:205
  76.0 1.7 %collective-permute-done.23.refs_2_ = bf16[96,1024]{1,0:T(8,128)(2,1)S(1)} collective-permute-done((bf16[96,1024]{1,0:T(8,128)(2,1)S(1)}, bf16[96,1024]{1,0:T(8,128)(2,1)S(1)}, u32[]{:S(2)}, u32[]{:S(2)}) %collective-permute-start.23) | collective-permute-done | bytes 196640 | tf_op jit(solution)/shard_map/ppermute | solution.py:205
  77.8 2.0 %collective-permute-done.24.refs_3_ = bf16[96,1024]{1,0:T(8,128)(2,1)S(1)} collective-permute-done((bf16[96,1024]{1,0:T(8,128)(2,1)S(1)}, bf16[96,1024]{1,0:T(8,128)(2,1)S(1)}, u32[]{:S(2)}, u32[]{:S(2)}) %collective-permute-start.24) | collective-permute-done | bytes 196640 | tf_op jit(solution)/shard_map/ppermute | solution.py:205
  80.4 2.2 %collective-permute-start.27 = (bf16[384,128]{1,0:T(8,128)(2,1)S(1)}, bf16[384,128]{1,0:T(8,128)(2,1)S(1)}, u32[]{:S(2)}, u32[]{:S(2)}) collective-permute-start(bf16[384,128]{1,0:T(8,128)(2,1)S(1)} %get-tuple-element.40), channel_id=1, source_target_pairs={{0,8},{8,0},{16,24},{24,16},{1,9},{9,1},{17,25},{25,17},{2,10},{10... | collective-permute-start | bytes 294920 | tf_op jit(solution)/shard_map/ppermute | solution.py:197
  83.4 1.6 %collective-permute-start.29 = (bf16[384,128]{1,0:T(8,128)(2,1)S(1)}, bf16[384,128]{1,0:T(8,128)(2,1)S(1)}, u32[]{:S(2)}, u32[]{:S(2)}) collective-permute-start(bf16[384,128]{1,0:T(8,128)(2,1)S(1)} %get-tuple-element.42), channel_id=1, source_target_pairs={{0,24},{8,16},{16,8},{24,0},{1,25},{9,17},{17,9},{25,1},{2,26},{10... | collective-permute-start | bytes 294920 | tf_op jit(solution)/shard_map/ppermute | solution.py:197
  85.0 2.4 %collective-permute-done.27.refs_1_ = bf16[384,128]{1,0:T(8,128)(2,1)S(1)} collective-permute-done((bf16[384,128]{1,0:T(8,128)(2,1)S(1)}, bf16[384,128]{1,0:T(8,128)(2,1)S(1)}, u32[]{:S(2)}, u32[]{:S(2)}) %collective-permute-start.27) | collective-permute-done | bytes 98336 | tf_op jit(solution)/shard_map/ppermute | solution.py:197
  87.4 3.9 %collective-permute-done.28.refs_2_ = bf16[384,128]{1,0:T(8,128)(2,1)S(1)} collective-permute-done((bf16[384,128]{1,0:T(8,128)(2,1)S(1)}, bf16[384,128]{1,0:T(8,128)(2,1)S(1)}, u32[]{:S(2)}, u32[]{:S(2)}) %collective-permute-start.28) | collective-permute-done | bytes 98336 | tf_op jit(solution)/shard_map/ppermute | solution.py:197
  91.3 1.3 %shard_map.73 = bf16[256,768]{1,0:T(8,128)(2,1)} custom-call(bf16[384,128]{1,0:T(8,128)(2,1)S(1)} %get-tuple-element.39.refs_0_, bf16[384,128]{1,0:T(8,128)(2,1)S(1)} %collective-permute-done.27.refs_1_, bf16[384,128]{1,0:T(8,128)(2,1)S(1)} %collective-permute-done.28.refs_2_, bf16[384,128]{1,0:T(8,128)(2,1)S(1)} %collective-permute-done.29.refs_3_, ...), custom_call_target="tpu_custom_call" | custom-call | flops 5000000000 | bytes 1000000 | tf_op jit(solution)/shard_map/pallas_call | solution.py:31
  (46 shorter events, 8.4 us)
Async XLA Ops:
  2.2 6.2 %collective-permute-start.3 = (bf16[384,128]{1,0:T(8,128)(2,1)S(1)}, bf16[384,128]{1,0:T(8,128)(2,1)S(1)}, u32[]{:S(2)}, u32[]{:S(2)}) collective-permute-start(bf16[384,128]{1,0:T(8,128)(2,1)S(1)} %get-tuple-element.30), channel_id=1, source_target_pairs={{0,8},{8,0},{16,24},{24,16},{1,9},{9,1},{17,25},{25,17},{2,10},{10... | collective-permute-start | bytes 294920 | tf_op jit(solution)/shard_map/ppermute | solution.py:197
  4.2 11.0 %collective-permute-start.4 = (bf16[384,128]{1,0:T(8,128)(2,1)S(1)}, bf16[384,128]{1,0:T(8,128)(2,1)S(1)}, u32[]{:S(2)}, u32[]{:S(2)}) collective-permute-start(bf16[384,128]{1,0:T(8,128)(2,1)S(1)} %get-tuple-element.31), channel_id=1, source_target_pairs={{0,16},{8,24},{16,0},{24,8},{1,17},{9,25},{17,1},{25,9},{2,18},{10... | collective-permute-start | bytes 294920 | tf_op jit(solution)/shard_map/ppermute | solution.py:197
  7.5 7.7 %collective-permute-start.5 = (bf16[384,128]{1,0:T(8,128)(2,1)S(1)}, bf16[384,128]{1,0:T(8,128)(2,1)S(1)}, u32[]{:S(2)}, u32[]{:S(2)}) collective-permute-start(bf16[384,128]{1,0:T(8,128)(2,1)S(1)} %get-tuple-element.32), channel_id=1, source_target_pairs={{0,24},{8,16},{16,8},{24,0},{1,25},{9,17},{17,9},{25,1},{2,26},{10... | collective-permute-start | bytes 294920 | tf_op jit(solution)/shard_map/ppermute | solution.py:197
  15.3 22.3 %collective-permute-start.6 = (bf16[384,512]{1,0:T(8,128)(2,1)S(1)}, bf16[384,512]{1,0:T(8,128)(2,1)S(1)}, u32[]{:S(2)}, u32[]{:S(2)}) collective-permute-start(bf16[384,512]{1,0:T(8,128)(2,1)S(1)} %shard_map.66.refs_4_), channel_id=1, source_target_pairs={{0,2},{2,4},{4,6},{6,0},{1,3},{3,5},{5,7},{7,1},{8,10},{10,12},{12... | collective-permute-start | bytes 1179656 | tf_op jit(solution)/shard_map/ppermute | solution.py:205
  16.9 21.1 %collective-permute-start.7 = (bf16[384,512]{1,0:T(8,128)(2,1)S(1)}, bf16[384,512]{1,0:T(8,128)(2,1)S(1)}, u32[]{:S(2)}, u32[]{:S(2)}) collective-permute-start(bf16[384,512]{1,0:T(8,128)(2,1)S(1)} %shard_map.66.refs_4_), channel_id=1, source_target_pairs={{0,6},{2,0},{4,2},{6,4},{1,7},{3,1},{5,3},{7,5},{8,14},{10,8},{12,... | collective-permute-start | bytes 1179656 | tf_op jit(solution)/shard_map/ppermute | solution.py:205
  18.6 6.9 %collective-permute-start = (bf16[768,128]{1,0:T(8,128)(2,1)S(1)}, bf16[768,128]{1,0:T(8,128)(2,1)S(1)}, u32[]{:S(2)}, u32[]{:S(2)}) collective-permute-start(bf16[768,128]{1,0:T(8,128)(2,1)S(1)} %get-tuple-element.26), channel_id=1, source_target_pairs={{0,8},{8,0},{16,24},{24,16},{1,9},{9,1},{17,25},{25,17},{2,10},{10... | collective-permute-start | bytes 589832 | tf_op jit(solution)/shard_map/ppermute | solution.py:197
  20.3 17.9 %collective-permute-start.8 = (bf16[384,512]{1,0:T(8,128)(2,1)S(1)}, bf16[384,512]{1,0:T(8,128)(2,1)S(1)}, u32[]{:S(2)}, u32[]{:S(2)}) collective-permute-start(bf16[384,512]{1,0:T(8,128)(2,1)S(1)} %shard_map.66.refs_4_), channel_id=1, source_target_pairs={{0,4},{2,6},{4,0},{6,2},{1,5},{3,7},{5,1},{7,3},{8,12},{10,14},{12... | collective-permute-start | bytes 1179656 | tf_op jit(solution)/shard_map/ppermute | solution.py:205
  22.2 15.3 %collective-permute-start.1 = (bf16[768,128]{1,0:T(8,128)(2,1)S(1)}, bf16[768,128]{1,0:T(8,128)(2,1)S(1)}, u32[]{:S(2)}, u32[]{:S(2)}) collective-permute-start(bf16[768,128]{1,0:T(8,128)(2,1)S(1)} %get-tuple-element.27), channel_id=1, source_target_pairs={{0,16},{8,24},{16,0},{24,8},{1,17},{9,25},{17,1},{25,9},{2,18},{10... | collective-permute-start | bytes 589832 | tf_op jit(solution)/shard_map/ppermute | solution.py:197
  25.6 13.0 %collective-permute-start.2 = (bf16[768,128]{1,0:T(8,128)(2,1)S(1)}, bf16[768,128]{1,0:T(8,128)(2,1)S(1)}, u32[]{:S(2)}, u32[]{:S(2)}) collective-permute-start(bf16[768,128]{1,0:T(8,128)(2,1)S(1)} %get-tuple-element.28), channel_id=1, source_target_pairs={{0,24},{8,16},{16,8},{24,0},{1,25},{9,17},{17,9},{25,1},{2,26},{10... | collective-permute-start | bytes 589832 | tf_op jit(solution)/shard_map/ppermute | solution.py:197
  37.5 2.5 %collective-permute-start.9 = (bf16[384,512]{1,0:T(8,128)(2,1)S(1)}, bf16[384,512]{1,0:T(8,128)(2,1)S(1)}, u32[]{:S(2)}, u32[]{:S(2)}) collective-permute-start(bf16[384,512]{1,0:T(8,128)(2,1)S(1)} %shard_map.66.refs_4_), channel_id=1, source_target_pairs={{0,1},{1,0},{2,3},{3,2},{4,5},{5,4},{6,7},{7,6},{8,9},{9,8},{10,11... | collective-permute-start | bytes 1179656 | tf_op jit(solution)/shard_map/ppermute | solution.py:201
  37.5 3.2 %collective-permute-start.10 = (bf16[384,512]{1,0:T(8,128)(2,1)S(1)}, bf16[384,512]{1,0:T(8,128)(2,1)S(1)}, u32[]{:S(2)}, u32[]{:S(2)}) collective-permute-start(bf16[384,512]{1,0:T(8,128)(2,1)S(1)} %collective-permute-done.6.refs_5_), channel_id=1, source_target_pairs={{0,1},{1,0},{2,3},{3,2},{4,5},{5,4},{6,7},{7,6},{8,9},{9,8},{10,11... | collective-permute-start | bytes 1179656 | tf_op jit(solution)/shard_map/ppermute | solution.py:201
  38.1 2.7 %collective-permute-start.11 = (bf16[384,512]{1,0:T(8,128)(2,1)S(1)}, bf16[384,512]{1,0:T(8,128)(2,1)S(1)}, u32[]{:S(2)}, u32[]{:S(2)}) collective-permute-start(bf16[384,512]{1,0:T(8,128)(2,1)S(1)} %collective-permute-done.7.refs_6_), channel_id=1, source_target_pairs={{0,1},{1,0},{2,3},{3,2},{4,5},{5,4},{6,7},{7,6},{8,9},{9,8},{10,11... | collective-permute-start | bytes 1179656 | tf_op jit(solution)/shard_map/ppermute | solution.py:201
  38.2 2.8 %collective-permute-start.12 = (bf16[384,512]{1,0:T(8,128)(2,1)S(1)}, bf16[384,512]{1,0:T(8,128)(2,1)S(1)}, u32[]{:S(2)}, u32[]{:S(2)}) collective-permute-start(bf16[384,512]{1,0:T(8,128)(2,1)S(1)} %collective-permute-done.8.refs_7_), channel_id=1, source_target_pairs={{0,1},{1,0},{2,3},{3,2},{4,5},{5,4},{6,7},{7,6},{8,9},{9,8},{10,11... | collective-permute-start | bytes 1179656 | tf_op jit(solution)/shard_map/ppermute | solution.py:201
  38.6 11.2 %collective-permute-start.20 = (bf16[384,512]{1,0:T(8,128)(2,1)S(1)}, bf16[384,512]{1,0:T(8,128)(2,1)S(1)}, u32[]{:S(2)}, u32[]{:S(2)}) collective-permute-start(bf16[384,512]{1,0:T(8,128)(2,1)S(1)} %shard_map.69.refs_4_), channel_id=1, source_target_pairs={{0,6},{2,0},{4,2},{6,4},{1,7},{3,1},{5,3},{7,5},{8,14},{10,8},{12,... | collective-permute-start | bytes 1179656 | tf_op jit(solution)/shard_map/ppermute | solution.py:205
  40.0 12.0 %collective-permute-start.18 = (bf16[384,512]{1,0:T(8,128)(2,1)S(1)}, bf16[384,512]{1,0:T(8,128)(2,1)S(1)}, u32[]{:S(2)}, u32[]{:S(2)}) collective-permute-start(bf16[384,512]{1,0:T(8,128)(2,1)S(1)} %shard_map.69.refs_4_), channel_id=1, source_target_pairs={{0,2},{2,4},{4,6},{6,0},{1,3},{3,5},{5,7},{7,1},{8,10},{10,12},{12... | collective-permute-start | bytes 1179656 | tf_op jit(solution)/shard_map/ppermute | solution.py:205
  42.1 10.0 %collective-permute-start.13 = (bf16[96,1024]{1,0:T(8,128)(2,1)S(1)}, bf16[96,1024]{1,0:T(8,128)(2,1)S(1)}, u32[]{:S(2)}, u32[]{:S(2)}) collective-permute-start(bf16[96,1024]{1,0:T(8,128)(2,1)S(1)} %get-tuple-element.34), channel_id=1, source_target_pairs={{0,32},{32,64},{64,96},{96,0},{1,33},{33,65},{65,97},{97,1},{2,34}... | collective-permute-start | bytes 589832 | tf_op jit(solution)/shard_map/ppermute | solution.py:205
  42.8 12.1 %collective-permute-start.14 = (bf16[96,1024]{1,0:T(8,128)(2,1)S(1)}, bf16[96,1024]{1,0:T(8,128)(2,1)S(1)}, u32[]{:S(2)}, u32[]{:S(2)}) collective-permute-start(bf16[96,1024]{1,0:T(8,128)(2,1)S(1)} %get-tuple-element.35), channel_id=1, source_target_pairs={{0,96},{32,0},{64,32},{96,64},{1,97},{33,1},{65,33},{97,65},{2,98}... | collective-permute-start | bytes 589832 | tf_op jit(solution)/shard_map/ppermute | solution.py:205
  44.4 10.5 %collective-permute-start.15 = (bf16[96,1024]{1,0:T(8,128)(2,1)S(1)}, bf16[96,1024]{1,0:T(8,128)(2,1)S(1)}, u32[]{:S(2)}, u32[]{:S(2)}) collective-permute-start(bf16[96,1024]{1,0:T(8,128)(2,1)S(1)} %get-tuple-element.36), channel_id=1, source_target_pairs={{0,64},{32,96},{64,0},{96,32},{1,65},{33,97},{65,1},{97,33},{2,66}... | collective-permute-start | bytes 589832 | tf_op jit(solution)/shard_map/ppermute | solution.py:205
  49.8 14.9 %collective-permute-start.17 = (bf16[384,512]{1,0:T(8,128)(2,1)S(1)}, bf16[384,512]{1,0:T(8,128)(2,1)S(1)}, u32[]{:S(2)}, u32[]{:S(2)}) collective-permute-start(bf16[384,512]{1,0:T(8,128)(2,1)S(1)} %shard_map.69.refs_4_), channel_id=1, source_target_pairs={{0,1},{1,0},{2,3},{3,2},{4,5},{5,4},{6,7},{7,6},{8,9},{9,8},{10,11... | collective-permute-start | bytes 1179656 | tf_op jit(solution)/shard_map/ppermute | solution.py:201
  52.0 12.7 %collective-permute-start.21 = (bf16[384,512]{1,0:T(8,128)(2,1)S(1)}, bf16[384,512]{1,0:T(8,128)(2,1)S(1)}, u32[]{:S(2)}, u32[]{:S(2)}) collective-permute-start(bf16[384,512]{1,0:T(8,128)(2,1)S(1)} %collective-permute-done.20.refs_0_.refs_6_), channel_id=1, source_target_pairs={{0,1},{1,0},{2,3},{3,2},{4,5},{5,4},{6,7},{7,6},{8,9},{9,8},{10,11... | collective-permute-start | bytes 1179656 | tf_op jit(solution)/shard_map/ppermute | solution.py:201
  52.1 12.7 %collective-permute-start.19 = (bf16[384,512]{1,0:T(8,128)(2,1)S(1)}, bf16[384,512]{1,0:T(8,128)(2,1)S(1)}, u32[]{:S(2)}, u32[]{:S(2)}) collective-permute-start(bf16[384,512]{1,0:T(8,128)(2,1)S(1)} %collective-permute-done.18.refs_5_), channel_id=1, source_target_pairs={{0,1},{1,0},{2,3},{3,2},{4,5},{5,4},{6,7},{7,6},{8,9},{9,8},{10,11... | collective-permute-start | bytes 1179656 | tf_op jit(solution)/shard_map/ppermute | solution.py:201
  54.9 9.8 %collective-permute-start.25 = (bf16[384,512]{1,0:T(8,128)(2,1)S(1)}, bf16[384,512]{1,0:T(8,128)(2,1)S(1)}, u32[]{:S(2)}, u32[]{:S(2)}) collective-permute-start(bf16[384,512]{1,0:T(8,128)(2,1)S(1)} %shard_map.71), channel_id=1, source_target_pairs={{0,6},{2,0},{4,2},{6,4},{1,7},{3,1},{5,3},{7,5},{8,14},{10,8},{12,... | collective-permute-start | bytes 1179656 | tf_op jit(solution)/shard_map/ppermute | solution.py:205
  56.8 11.5 %collective-permute-start.16 = (bf16[96,1024]{1,0:T(8,128)(2,1)S(1)}, bf16[96,1024]{1,0:T(8,128)(2,1)S(1)}, u32[]{:S(2)}, u32[]{:S(2)}) collective-permute-start(bf16[96,1024]{1,0:T(8,128)(2,1)S(1)} %get-tuple-element.38), channel_id=1, source_target_pairs={{0,128},{128,0},{1,129},{129,1},{2,130},{130,2},{3,131},{131,3},{4... | collective-permute-start | bytes 589832 | tf_op jit(solution)/shard_map/ppermute | solution.py:252
  64.8 14.9 %collective-permute-start.26 = (bf16[384,512]{1,0:T(8,128)(2,1)S(1)}, bf16[384,512]{1,0:T(8,128)(2,1)S(1)}, u32[]{:S(2)}, u32[]{:S(2)}) collective-permute-start(bf16[384,512]{1,0:T(8,128)(2,1)S(1)} %collective-permute-done.25.refs_7_), channel_id=1, source_target_pairs={{0,1},{1,0},{2,3},{3,2},{4,5},{5,4},{6,7},{7,6},{8,9},{9,8},{10,11... | collective-permute-start | bytes 1179656 | tf_op jit(solution)/shard_map/ppermute | solution.py:201
  68.6 22.7 %copy-start.2 = (bf16[768,768]{1,0:T(8,128)(2,1)S(1)}, bf16[768,768]{1,0:T(8,128)(2,1)}, u32[]{:S(2)}) copy-start(bf16[768,768]{1,0:T(8,128)(2,1)} %refs_5_.1) | copy-start | bytes 3538948
  68.6 22.7 %copy-start.3 = (bf16[8,32,768]{2,1,0:T(8,128)(2,1)S(1)}, bf16[8,32,768]{2,1,0:T(8,128)(2,1)}, u32[]{:S(2)}) copy-start(bf16[8,32,768]{2,1,0:T(8,128)(2,1)} %param.6) | copy-start | bytes 1179652
  68.6 7.4 %collective-permute-start.22 = (bf16[96,1024]{1,0:T(8,128)(2,1)S(1)}, bf16[96,1024]{1,0:T(8,128)(2,1)S(1)}, u32[]{:S(2)}, u32[]{:S(2)}) collective-permute-start(bf16[96,1024]{1,0:T(8,128)(2,1)S(1)} %shard_map.70.refs_0_), channel_id=1, source_target_pairs={{0,32},{32,64},{64,96},{96,0},{1,33},{33,65},{65,97},{97,1},{2,34}... | collective-permute-start | bytes 589832 | tf_op jit(solution)/shard_map/ppermute | solution.py:205
  69.9 7.9 %collective-permute-start.23 = (bf16[96,1024]{1,0:T(8,128)(2,1)S(1)}, bf16[96,1024]{1,0:T(8,128)(2,1)S(1)}, u32[]{:S(2)}, u32[]{:S(2)}) collective-permute-start(bf16[96,1024]{1,0:T(8,128)(2,1)S(1)} %shard_map.70.refs_0_), channel_id=1, source_target_pairs={{0,64},{32,96},{64,0},{96,32},{1,65},{33,97},{65,1},{97,33},{2,66}... | collective-permute-start | bytes 589832 | tf_op jit(solution)/shard_map/ppermute | solution.py:205
  71.0 8.7 %collective-permute-start.24 = (bf16[96,1024]{1,0:T(8,128)(2,1)S(1)}, bf16[96,1024]{1,0:T(8,128)(2,1)S(1)}, u32[]{:S(2)}, u32[]{:S(2)}) collective-permute-start(bf16[96,1024]{1,0:T(8,128)(2,1)S(1)} %shard_map.70.refs_0_), channel_id=1, source_target_pairs={{0,96},{32,0},{64,32},{96,64},{1,97},{33,1},{65,33},{97,65},{2,98}... | collective-permute-start | bytes 589832 | tf_op jit(solution)/shard_map/ppermute | solution.py:205
  80.4 7.0 %collective-permute-start.27 = (bf16[384,128]{1,0:T(8,128)(2,1)S(1)}, bf16[384,128]{1,0:T(8,128)(2,1)S(1)}, u32[]{:S(2)}, u32[]{:S(2)}) collective-permute-start(bf16[384,128]{1,0:T(8,128)(2,1)S(1)} %get-tuple-element.40), channel_id=1, source_target_pairs={{0,8},{8,0},{16,24},{24,16},{1,9},{9,1},{17,25},{25,17},{2,10},{10... | collective-permute-start | bytes 294920 | tf_op jit(solution)/shard_map/ppermute | solution.py:197
  82.6 8.7 %collective-permute-start.28 = (bf16[384,128]{1,0:T(8,128)(2,1)S(1)}, bf16[384,128]{1,0:T(8,128)(2,1)S(1)}, u32[]{:S(2)}, u32[]{:S(2)}) collective-permute-start(bf16[384,128]{1,0:T(8,128)(2,1)S(1)} %get-tuple-element.41), channel_id=1, source_target_pairs={{0,16},{8,24},{16,0},{24,8},{1,17},{9,25},{17,1},{25,9},{2,18},{10... | collective-permute-start | bytes 294920 | tf_op jit(solution)/shard_map/ppermute | solution.py:197
  83.4 7.9 %collective-permute-start.29 = (bf16[384,128]{1,0:T(8,128)(2,1)S(1)}, bf16[384,128]{1,0:T(8,128)(2,1)S(1)}, u32[]{:S(2)}, u32[]{:S(2)}) collective-permute-start(bf16[384,128]{1,0:T(8,128)(2,1)S(1)} %get-tuple-element.42), channel_id=1, source_target_pairs={{0,24},{8,16},{16,8},{24,0},{1,25},{9,17},{17,9},{25,1},{2,26},{10... | collective-permute-start | bytes 294920 | tf_op jit(solution)/shard_map/ppermute | solution.py:197
  (2 other events, 15.0 us)

commit v4 on v3

--- a/solution.py
+++ b/solution.py
@@ -44,12 +44,12 @@
 
 
 def pack(full, store):
-    parts = full.reshape(4, 2, 32, HEADS * SIZE)
+    parts = full.astype(BF16).reshape(4, 2, 32, HEADS * SIZE)
     even, odd = parts[:, 0].reshape(128, -1), parts[:, 1].reshape(128, -1)
     for n in range(HEADS // 2):
         a, b = even[:, n * 128 : n * 128 + 128], odd[:, n * 128 : n * 128 + 128]
-        store(2 * n, jnp.concatenate([a[:, :64], b[:, :64]], axis=1).astype(BF16))
-        store(2 * n + 1, jnp.concatenate([a[:, 64:], b[:, 64:]], axis=1).astype(BF16))
+        store(2 * n, jnp.concatenate([a[:, :64], b[:, :64]], axis=1))
+        store(2 * n + 1, jnp.concatenate([a[:, 64:], b[:, 64:]], axis=1))
 
 
 def key_kernel(x_far, gain_far, w_far, normed_ref, o0, o1, o2, o3, held, x_ref, gain_ref, w_ref, sems):
@@ -178,12 +178,12 @@
         held[jnp.bitwise_xor(me, m)] = piece[...]
 
     def block(h):
-        return held[h // OWN, (h % OWN) * 128 : (h % OWN) * 128 + 128, :].astype(F32)
+        return held[h // OWN, (h % OWN) * 128 : (h % OWN) * 128 + 128, :]
 
     for n in range(HEADS // 2):
         a, b = block(2 * n), block(2 * n + 1)
-        even = jnp.concatenate([a[:, :64], b[:, :64]], axis=1).astype(BF16)
-        odd = jnp.concatenate([a[:, 64:], b[:, 64:]], axis=1).astype(BF16)
+        even = jnp.concatenate([a[:, :64], b[:, :64]], axis=1)
+        odd = jnp.concatenate([a[:, 64:], b[:, 64:]], axis=1)
         for sp in range(4):
             rows = slice(sp * 32, sp * 32 + 32)
             cols = slice(n * 128, n * 128 + 128)
@@ -193,8 +193,9 @@
     out[...] = (x_ref[...].astype(F32) + mixed).astype(BF16)
 
 
-def line(pieces):
-    return (pieces[0], *(lax.ppermute(pieces[m], "zl", LINE[m]) for m in (1, 2, 3)))
+def line(pieces, order=(1, 2, 3)):
+    got = {m: lax.ppermute(pieces[m], "zl", LINE[m]) for m in order}
+    return (pieces[0], got[1], got[2], got[3])
 
 
 def other_core(slabs):
@@ -225,7 +226,7 @@
         ],
         places={0: FAR, 1: FAR, 2: FAR},
     )(*at_rest)
-    keys = line(keys)
+    keys = line(keys, (3, 2, 1))
 
     def slab(parts, base, after=()):
         return call(functools.partial(slab_kernel, base), [whole], after=after)(*parts)[0]
@@ -254,7 +255,8 @@
     (probs,) = call(functools.partial(softmax_kernel, scale), [part], after=swapped)(
         total, other
     )
-    probs = [probs] + over("x", [probs] * 4, (1, 2, 3))
+    near, back, far = over("x", [probs] * 4, (1, 3, 2))
+    probs = [probs, near, far, back]
     context = call(
         context_kernel, [piece] * 4, [pltpu.VMEM((OWN, 4, 32, 1024), BF16)]
     )(*probs, *slabs)

time: 92.7 us -> 92.5 us (level)
  no operation moved by 1% of the time
where the time goes in v4:
time: 92.5 us
  waiting for transfers between devices  46.1 us (50%)
  starting transfers between devices  39.5 us (43%)
  Pallas kernels  6.7 us (7%)
    ppermute x9, waiting for transfers between devices, line(): got = {m: lax.ppermute(pieces[m], 'zl', LINE[m]) for m in order}  24.3 us
    ppermute x12, waiting for transfers between devices, over(): return [lax.ppermute(arrays[k], axis, RING[k]) for k in order]  18.1 us
    ppermute x12, starting transfers between devices, over(): return [lax.ppermute(arrays[k], axis, RING[k]) for k in order]  16.6 us
    ppermute x9, starting transfers between devices, line(): got = {m: lax.ppermute(pieces[m], 'zl', LINE[m]) for m in order}  15.5 us
    pallas_call x10, Pallas kernels, run(): pl.pallas_call(kernel, out_shape=[jax.ShapeDtypeStruct(s, d) for s, d in...  6.7 us
    ppermute x1, starting transfers between devices, per_device(): other = lax.ppermute(sent, 'zh', [(0, 1), (1, 0)])  5.92 us
    ppermute x1, waiting for transfers between devices, per_device(): other = lax.ppermute(sent, 'zh', [(0, 1), (1, 0)])  3.53 us
  transfers between devices with their start and end apart: 30, of which 14 were waited for; matrix products, arithmetic and copies ran while one was open for 0% of the time, Pallas kernels for 3%

profile of v4, /device:TPU:6, one launch (start us, length us, event | category | flops | bytes accessed | tf_op | source)
XLA Modules:
  0.0 92.5 jit_solution(6553241307171995868)
XLA Ops:
  0.0 2.2 %shard_map.64 = (bf16[256,768]{1,0:T(8,128)(2,1)S(1)}, bf16[384,128]{1,0:T(8,128)(2,1)S(1)}, bf16[384,128]{1,0:T(8,128)(2,1)S(1)}, bf16[384,128]{1,0:T(8,128)(2,1)S(1)}, bf16[384,128]{1,0:T(8,128)(2,1)S(1)}) custom-call(bf16[256,768]{1,0:T(8,128)(2,1)} %bitcast.2, f32[768]{0:T(1024)} %refs_1_.2, bf16[768,768]{1,0:T(8,128)(2,1)} %refs_2_.2), custom_call_target="tpu_custom_call" | custom-call | flops 5000000000 | bytes 1000000 | tf_op jit(solution)/shard_map/pallas_call | solution.py:31
  2.2 2.0 %collective-permute-start.3 = (bf16[384,128]{1,0:T(8,128)(2,1)S(1)}, bf16[384,128]{1,0:T(8,128)(2,1)S(1)}, u32[]{:S(2)}, u32[]{:S(2)}) collective-permute-start(bf16[384,128]{1,0:T(8,128)(2,1)S(1)} %get-tuple-element.30), channel_id=1, source_target_pairs={{0,8},{8,0},{16,24},{24,16},{1,9},{9,1},{17,25},{25,17},{2,10},{10... | collective-permute-start | bytes 294920 | tf_op jit(solution)/shard_map/ppermute | solution.py:197
  4.2 3.3 %collective-permute-start.4 = (bf16[384,128]{1,0:T(8,128)(2,1)S(1)}, bf16[384,128]{1,0:T(8,128)(2,1)S(1)}, u32[]{:S(2)}, u32[]{:S(2)}) collective-permute-start(bf16[384,128]{1,0:T(8,128)(2,1)S(1)} %get-tuple-element.31), channel_id=1, source_target_pairs={{0,16},{8,24},{16,0},{24,8},{1,17},{9,25},{17,1},{25,9},{2,18},{10... | collective-permute-start | bytes 294920 | tf_op jit(solution)/shard_map/ppermute | solution.py:197
  8.4 6.8 %collective-permute-done.4.refs_2_ = bf16[384,128]{1,0:T(8,128)(2,1)S(1)} collective-permute-done((bf16[384,128]{1,0:T(8,128)(2,1)S(1)}, bf16[384,128]{1,0:T(8,128)(2,1)S(1)}, u32[]{:S(2)}, u32[]{:S(2)}) %collective-permute-start.4) | collective-permute-done | bytes 98336 | tf_op jit(solution)/shard_map/ppermute | solution.py:197
  15.3 1.7 %collective-permute-start.6 = (bf16[384,512]{1,0:T(8,128)(2,1)S(1)}, bf16[384,512]{1,0:T(8,128)(2,1)S(1)}, u32[]{:S(2)}, u32[]{:S(2)}) collective-permute-start(bf16[384,512]{1,0:T(8,128)(2,1)S(1)} %shard_map.66.refs_4_), channel_id=1, source_target_pairs={{0,2},{2,4},{4,6},{6,0},{1,3},{3,5},{5,7},{7,1},{8,10},{10,12},{12... | collective-permute-start | bytes 1179656 | tf_op jit(solution)/shard_map/ppermute | solution.py:206
  17.0 1.7 %collective-permute-start.7 = (bf16[384,512]{1,0:T(8,128)(2,1)S(1)}, bf16[384,512]{1,0:T(8,128)(2,1)S(1)}, u32[]{:S(2)}, u32[]{:S(2)}) collective-permute-start(bf16[384,512]{1,0:T(8,128)(2,1)S(1)} %shard_map.66.refs_4_), channel_id=1, source_target_pairs={{0,6},{2,0},{4,2},{6,4},{1,7},{3,1},{5,3},{7,5},{8,14},{10,8},{12,... | collective-permute-start | bytes 1179656 | tf_op jit(solution)/shard_map/ppermute | solution.py:206
  18.6 1.6 %collective-permute-start = (bf16[768,128]{1,0:T(8,128)(2,1)S(1)}, bf16[768,128]{1,0:T(8,128)(2,1)S(1)}, u32[]{:S(2)}, u32[]{:S(2)}) collective-permute-start(bf16[768,128]{1,0:T(8,128)(2,1)S(1)} %get-tuple-element.26), channel_id=1, source_target_pairs={{0,8},{8,0},{16,24},{24,16},{1,9},{9,1},{17,25},{25,17},{2,10},{10... | collective-permute-start | bytes 589832 | tf_op jit(solution)/shard_map/ppermute | solution.py:197
  20.3 2.0 %collective-permute-start.8 = (bf16[384,512]{1,0:T(8,128)(2,1)S(1)}, bf16[384,512]{1,0:T(8,128)(2,1)S(1)}, u32[]{:S(2)}, u32[]{:S(2)}) collective-permute-start(bf16[384,512]{1,0:T(8,128)(2,1)S(1)} %shard_map.66.refs_4_), channel_id=1, source_target_pairs={{0,4},{2,6},{4,0},{6,2},{1,5},{3,7},{5,1},{7,3},{8,12},{10,14},{12... | collective-permute-start | bytes 1179656 | tf_op jit(solution)/shard_map/ppermute | solution.py:206
  22.2 1.4 %collective-permute-start.1 = (bf16[768,128]{1,0:T(8,128)(2,1)S(1)}, bf16[768,128]{1,0:T(8,128)(2,1)S(1)}, u32[]{:S(2)}, u32[]{:S(2)}) collective-permute-start(bf16[768,128]{1,0:T(8,128)(2,1)S(1)} %get-tuple-element.27), channel_id=1, source_target_pairs={{0,16},{8,24},{16,0},{24,8},{1,17},{9,25},{17,1},{25,9},{2,18},{10... | collective-permute-start | bytes 589832 | tf_op jit(solution)/shard_map/ppermute | solution.py:197
  23.7 1.9 %collective-permute-done.refs_1_ = bf16[768,128]{1,0:T(8,128)(2,1)S(1)} collective-permute-done((bf16[768,128]{1,0:T(8,128)(2,1)S(1)}, bf16[768,128]{1,0:T(8,128)(2,1)S(1)}, u32[]{:S(2)}, u32[]{:S(2)}) %collective-permute-start) | collective-permute-done | bytes 196640 | tf_op jit(solution)/shard_map/ppermute | solution.py:197
  25.6 2.5 %collective-permute-start.2 = (bf16[768,128]{1,0:T(8,128)(2,1)S(1)}, bf16[768,128]{1,0:T(8,128)(2,1)S(1)}, u32[]{:S(2)}, u32[]{:S(2)}) collective-permute-start(bf16[768,128]{1,0:T(8,128)(2,1)S(1)} %get-tuple-element.28), channel_id=1, source_target_pairs={{0,24},{8,16},{16,8},{24,0},{1,25},{9,17},{17,9},{25,1},{2,26},{10... | collective-permute-start | bytes 589832 | tf_op jit(solution)/shard_map/ppermute | solution.py:197
  28.1 9.5 %collective-permute-done.1.refs_2_ = bf16[768,128]{1,0:T(8,128)(2,1)S(1)} collective-permute-done((bf16[768,128]{1,0:T(8,128)(2,1)S(1)}, bf16[768,128]{1,0:T(8,128)(2,1)S(1)}, u32[]{:S(2)}, u32[]{:S(2)}) %collective-permute-start.1) | collective-permute-done | bytes 196640 | tf_op jit(solution)/shard_map/ppermute | solution.py:197
  38.7 1.4 %collective-permute-start.20 = (bf16[384,512]{1,0:T(8,128)(2,1)S(1)}, bf16[384,512]{1,0:T(8,128)(2,1)S(1)}, u32[]{:S(2)}, u32[]{:S(2)}) collective-permute-start(bf16[384,512]{1,0:T(8,128)(2,1)S(1)} %shard_map.69.refs_4_), channel_id=1, source_target_pairs={{0,6},{2,0},{4,2},{6,4},{1,7},{3,1},{5,3},{7,5},{8,14},{10,8},{12,... | collective-permute-start | bytes 1179656 | tf_op jit(solution)/shard_map/ppermute | solution.py:206
  42.8 1.5 %collective-permute-start.14 = (bf16[96,1024]{1,0:T(8,128)(2,1)S(1)}, bf16[96,1024]{1,0:T(8,128)(2,1)S(1)}, u32[]{:S(2)}, u32[]{:S(2)}) collective-permute-start(bf16[96,1024]{1,0:T(8,128)(2,1)S(1)} %get-tuple-element.35), channel_id=1, source_target_pairs={{0,96},{32,0},{64,32},{96,64},{1,97},{33,1},{65,33},{97,65},{2,98}... | collective-permute-start | bytes 589832 | tf_op jit(solution)/shard_map/ppermute | solution.py:206
  44.4 1.4 %collective-permute-start.15 = (bf16[96,1024]{1,0:T(8,128)(2,1)S(1)}, bf16[96,1024]{1,0:T(8,128)(2,1)S(1)}, u32[]{:S(2)}, u32[]{:S(2)}) collective-permute-start(bf16[96,1024]{1,0:T(8,128)(2,1)S(1)} %get-tuple-element.36), channel_id=1, source_target_pairs={{0,64},{32,96},{64,0},{96,32},{1,65},{33,97},{65,1},{97,33},{2,66}... | collective-permute-start | bytes 589832 | tf_op jit(solution)/shard_map/ppermute | solution.py:206
  45.8 4.1 %collective-permute-done.20.refs_0_.refs_6_ = bf16[384,512]{1,0:T(8,128)(2,1)S(1)} collective-permute-done((bf16[384,512]{1,0:T(8,128)(2,1)S(1)}, bf16[384,512]{1,0:T(8,128)(2,1)S(1)}, u32[]{:S(2)}, u32[]{:S(2)}) %collective-permute-start.20) | collective-permute-done | bytes 393248 | tf_op jit(solution)/shard_map/ppermute | solution.py:206
  49.8 2.2 %collective-permute-done.18.refs_5_ = bf16[384,512]{1,0:T(8,128)(2,1)S(1)} collective-permute-done((bf16[384,512]{1,0:T(8,128)(2,1)S(1)}, bf16[384,512]{1,0:T(8,128)(2,1)S(1)}, u32[]{:S(2)}, u32[]{:S(2)}) %collective-permute-start.18) | collective-permute-done | bytes 393248 | tf_op jit(solution)/shard_map/ppermute | solution.py:206
  52.6 2.3 %collective-permute-done.14.refs_2_ = bf16[96,1024]{1,0:T(8,128)(2,1)S(1)} collective-permute-done((bf16[96,1024]{1,0:T(8,128)(2,1)S(1)}, bf16[96,1024]{1,0:T(8,128)(2,1)S(1)}, u32[]{:S(2)}, u32[]{:S(2)}) %collective-permute-start.14) | collective-permute-done | bytes 196640 | tf_op jit(solution)/shard_map/ppermute | solution.py:206
  54.9 1.8 %collective-permute-start.25 = (bf16[384,512]{1,0:T(8,128)(2,1)S(1)}, bf16[384,512]{1,0:T(8,128)(2,1)S(1)}, u32[]{:S(2)}, u32[]{:S(2)}) collective-permute-start(bf16[384,512]{1,0:T(8,128)(2,1)S(1)} %shard_map.71), channel_id=1, source_target_pairs={{0,6},{2,0},{4,2},{6,4},{1,7},{3,1},{5,3},{7,5},{8,14},{10,8},{12,... | collective-permute-start | bytes 1179656 | tf_op jit(solution)/shard_map/ppermute | solution.py:206
  56.8 5.9 %collective-permute-start.16 = (bf16[96,1024]{1,0:T(8,128)(2,1)S(1)}, bf16[96,1024]{1,0:T(8,128)(2,1)S(1)}, u32[]{:S(2)}, u32[]{:S(2)}) collective-permute-start(bf16[96,1024]{1,0:T(8,128)(2,1)S(1)} %get-tuple-element.38), channel_id=1, source_target_pairs={{0,128},{128,0},{1,129},{129,1},{2,130},{130,2},{3,131},{131,3},{4... | collective-permute-start | bytes 589832 | tf_op jit(solution)/shard_map/ppermute | solution.py:253
  62.7 2.0 %collective-permute-done.25.refs_7_ = bf16[384,512]{1,0:T(8,128)(2,1)S(1)} collective-permute-done((bf16[384,512]{1,0:T(8,128)(2,1)S(1)}, bf16[384,512]{1,0:T(8,128)(2,1)S(1)}, u32[]{:S(2)}, u32[]{:S(2)}) %collective-permute-start.25) | collective-permute-done | bytes 393248 | tf_op jit(solution)/shard_map/ppermute | solution.py:206
  64.8 3.5 %collective-permute-done.16.refs_1_ = bf16[96,1024]{1,0:T(8,128)(2,1)S(1)} collective-permute-done((bf16[96,1024]{1,0:T(8,128)(2,1)S(1)}, bf16[96,1024]{1,0:T(8,128)(2,1)S(1)}, u32[]{:S(2)}, u32[]{:S(2)}) %collective-permute-start.16) | collective-permute-done | bytes 196640 | tf_op jit(solution)/shard_map/ppermute | solution.py:253
  68.6 1.3 %collective-permute-start.22 = (bf16[96,1024]{1,0:T(8,128)(2,1)S(1)}, bf16[96,1024]{1,0:T(8,128)(2,1)S(1)}, u32[]{:S(2)}, u32[]{:S(2)}) collective-permute-start(bf16[96,1024]{1,0:T(8,128)(2,1)S(1)} %shard_map.70.refs_0_), channel_id=1, source_target_pairs={{0,32},{32,64},{64,96},{96,0},{1,33},{33,65},{65,97},{97,1},{2,34}... | collective-permute-start | bytes 589832 | tf_op jit(solution)/shard_map/ppermute | solution.py:206
  71.0 1.3 %collective-permute-start.24 = (bf16[96,1024]{1,0:T(8,128)(2,1)S(1)}, bf16[96,1024]{1,0:T(8,128)(2,1)S(1)}, u32[]{:S(2)}, u32[]{:S(2)}) collective-permute-start(bf16[96,1024]{1,0:T(8,128)(2,1)S(1)} %shard_map.70.refs_0_), channel_id=1, source_target_pairs={{0,96},{32,0},{64,32},{96,64},{1,97},{33,1},{65,33},{97,65},{2,98}... | collective-permute-start | bytes 589832 | tf_op jit(solution)/shard_map/ppermute | solution.py:206
  72.3 3.7 %collective-permute-done.22.refs_1_ = bf16[96,1024]{1,0:T(8,128)(2,1)S(1)} collective-permute-done((bf16[96,1024]{1,0:T(8,128)(2,1)S(1)}, bf16[96,1024]{1,0:T(8,128)(2,1)S(1)}, u32[]{:S(2)}, u32[]{:S(2)}) %collective-permute-start.22) | collective-permute-done | bytes 196640 | tf_op jit(solution)/shard_map/ppermute | solution.py:206
  76.1 1.7 %collective-permute-done.23.refs_2_ = bf16[96,1024]{1,0:T(8,128)(2,1)S(1)} collective-permute-done((bf16[96,1024]{1,0:T(8,128)(2,1)S(1)}, bf16[96,1024]{1,0:T(8,128)(2,1)S(1)}, u32[]{:S(2)}, u32[]{:S(2)}) %collective-permute-start.23) | collective-permute-done | bytes 196640 | tf_op jit(solution)/shard_map/ppermute | solution.py:206
  77.8 2.0 %collective-permute-done.24.refs_3_ = bf16[96,1024]{1,0:T(8,128)(2,1)S(1)} collective-permute-done((bf16[96,1024]{1,0:T(8,128)(2,1)S(1)}, bf16[96,1024]{1,0:T(8,128)(2,1)S(1)}, u32[]{:S(2)}, u32[]{:S(2)}) %collective-permute-start.24) | collective-permute-done | bytes 196640 | tf_op jit(solution)/shard_map/ppermute | solution.py:206
  80.4 2.2 %collective-permute-start.27 = (bf16[384,128]{1,0:T(8,128)(2,1)S(1)}, bf16[384,128]{1,0:T(8,128)(2,1)S(1)}, u32[]{:S(2)}, u32[]{:S(2)}) collective-permute-start(bf16[384,128]{1,0:T(8,128)(2,1)S(1)} %get-tuple-element.40), channel_id=1, source_target_pairs={{0,8},{8,0},{16,24},{24,16},{1,9},{9,1},{17,25},{25,17},{2,10},{10... | collective-permute-start | bytes 294920 | tf_op jit(solution)/shard_map/ppermute | solution.py:197
  83.4 1.6 %collective-permute-start.29 = (bf16[384,128]{1,0:T(8,128)(2,1)S(1)}, bf16[384,128]{1,0:T(8,128)(2,1)S(1)}, u32[]{:S(2)}, u32[]{:S(2)}) collective-permute-start(bf16[384,128]{1,0:T(8,128)(2,1)S(1)} %get-tuple-element.42), channel_id=1, source_target_pairs={{0,24},{8,16},{16,8},{24,0},{1,25},{9,17},{17,9},{25,1},{2,26},{10... | collective-permute-start | bytes 294920 | tf_op jit(solution)/shard_map/ppermute | solution.py:197
  85.0 2.4 %collective-permute-done.27.refs_1_ = bf16[384,128]{1,0:T(8,128)(2,1)S(1)} collective-permute-done((bf16[384,128]{1,0:T(8,128)(2,1)S(1)}, bf16[384,128]{1,0:T(8,128)(2,1)S(1)}, u32[]{:S(2)}, u32[]{:S(2)}) %collective-permute-start.27) | collective-permute-done | bytes 98336 | tf_op jit(solution)/shard_map/ppermute | solution.py:197
  87.4 3.7 %collective-permute-done.28.refs_2_ = bf16[384,128]{1,0:T(8,128)(2,1)S(1)} collective-permute-done((bf16[384,128]{1,0:T(8,128)(2,1)S(1)}, bf16[384,128]{1,0:T(8,128)(2,1)S(1)}, u32[]{:S(2)}, u32[]{:S(2)}) %collective-permute-start.28) | collective-permute-done | bytes 98336 | tf_op jit(solution)/shard_map/ppermute | solution.py:197
  91.1 1.3 %shard_map.73 = bf16[256,768]{1,0:T(8,128)(2,1)} custom-call(bf16[384,128]{1,0:T(8,128)(2,1)S(1)} %get-tuple-element.39.refs_0_, bf16[384,128]{1,0:T(8,128)(2,1)S(1)} %collective-permute-done.27.refs_1_, bf16[384,128]{1,0:T(8,128)(2,1)S(1)} %collective-permute-done.28.refs_2_, bf16[384,128]{1,0:T(8,128)(2,1)S(1)} %collective-permute-done.29.refs_3_, ...), custom_call_target="tpu_custom_call" | custom-call | flops 5000000000 | bytes 1000000 | tf_op jit(solution)/shard_map/pallas_call | solution.py:31
  (46 shorter events, 8.4 us)
Async XLA Ops:
  2.2 6.2 %collective-permute-start.3 = (bf16[384,128]{1,0:T(8,128)(2,1)S(1)}, bf16[384,128]{1,0:T(8,128)(2,1)S(1)}, u32[]{:S(2)}, u32[]{:S(2)}) collective-permute-start(bf16[384,128]{1,0:T(8,128)(2,1)S(1)} %get-tuple-element.30), channel_id=1, source_target_pairs={{0,8},{8,0},{16,24},{24,16},{1,9},{9,1},{17,25},{25,17},{2,10},{10... | collective-permute-start | bytes 294920 | tf_op jit(solution)/shard_map/ppermute | solution.py:197
  4.2 11.0 %collective-permute-start.4 = (bf16[384,128]{1,0:T(8,128)(2,1)S(1)}, bf16[384,128]{1,0:T(8,128)(2,1)S(1)}, u32[]{:S(2)}, u32[]{:S(2)}) collective-permute-start(bf16[384,128]{1,0:T(8,128)(2,1)S(1)} %get-tuple-element.31), channel_id=1, source_target_pairs={{0,16},{8,24},{16,0},{24,8},{1,17},{9,25},{17,1},{25,9},{2,18},{10... | collective-permute-start | bytes 294920 | tf_op jit(solution)/shard_map/ppermute | solution.py:197
  7.5 7.7 %collective-permute-start.5 = (bf16[384,128]{1,0:T(8,128)(2,1)S(1)}, bf16[384,128]{1,0:T(8,128)(2,1)S(1)}, u32[]{:S(2)}, u32[]{:S(2)}) collective-permute-start(bf16[384,128]{1,0:T(8,128)(2,1)S(1)} %get-tuple-element.32), channel_id=1, source_target_pairs={{0,24},{8,16},{16,8},{24,0},{1,25},{9,17},{17,9},{25,1},{2,26},{10... | collective-permute-start | bytes 294920 | tf_op jit(solution)/shard_map/ppermute | solution.py:197
  15.3 22.3 %collective-permute-start.6 = (bf16[384,512]{1,0:T(8,128)(2,1)S(1)}, bf16[384,512]{1,0:T(8,128)(2,1)S(1)}, u32[]{:S(2)}, u32[]{:S(2)}) collective-permute-start(bf16[384,512]{1,0:T(8,128)(2,1)S(1)} %shard_map.66.refs_4_), channel_id=1, source_target_pairs={{0,2},{2,4},{4,6},{6,0},{1,3},{3,5},{5,7},{7,1},{8,10},{10,12},{12... | collective-permute-start | bytes 1179656 | tf_op jit(solution)/shard_map/ppermute | solution.py:206
  17.0 21.1 %collective-permute-start.7 = (bf16[384,512]{1,0:T(8,128)(2,1)S(1)}, bf16[384,512]{1,0:T(8,128)(2,1)S(1)}, u32[]{:S(2)}, u32[]{:S(2)}) collective-permute-start(bf16[384,512]{1,0:T(8,128)(2,1)S(1)} %shard_map.66.refs_4_), channel_id=1, source_target_pairs={{0,6},{2,0},{4,2},{6,4},{1,7},{3,1},{5,3},{7,5},{8,14},{10,8},{12,... | collective-permute-start | bytes 1179656 | tf_op jit(solution)/shard_map/ppermute | solution.py:206
  18.6 6.9 %collective-permute-start = (bf16[768,128]{1,0:T(8,128)(2,1)S(1)}, bf16[768,128]{1,0:T(8,128)(2,1)S(1)}, u32[]{:S(2)}, u32[]{:S(2)}) collective-permute-start(bf16[768,128]{1,0:T(8,128)(2,1)S(1)} %get-tuple-element.26), channel_id=1, source_target_pairs={{0,8},{8,0},{16,24},{24,16},{1,9},{9,1},{17,25},{25,17},{2,10},{10... | collective-permute-start | bytes 589832 | tf_op jit(solution)/shard_map/ppermute | solution.py:197
  20.3 17.9 %collective-permute-start.8 = (bf16[384,512]{1,0:T(8,128)(2,1)S(1)}, bf16[384,512]{1,0:T(8,128)(2,1)S(1)}, u32[]{:S(2)}, u32[]{:S(2)}) collective-permute-start(bf16[384,512]{1,0:T(8,128)(2,1)S(1)} %shard_map.66.refs_4_), channel_id=1, source_target_pairs={{0,4},{2,6},{4,0},{6,2},{1,5},{3,7},{5,1},{7,3},{8,12},{10,14},{12... | collective-permute-start | bytes 1179656 | tf_op jit(solution)/shard_map/ppermute | solution.py:206
  22.2 15.3 %collective-permute-start.1 = (bf16[768,128]{1,0:T(8,128)(2,1)S(1)}, bf16[768,128]{1,0:T(8,128)(2,1)S(1)}, u32[]{:S(2)}, u32[]{:S(2)}) collective-permute-start(bf16[768,128]{1,0:T(8,128)(2,1)S(1)} %get-tuple-element.27), channel_id=1, source_target_pairs={{0,16},{8,24},{16,0},{24,8},{1,17},{9,25},{17,1},{25,9},{2,18},{10... | collective-permute-start | bytes 589832 | tf_op jit(solution)/shard_map/ppermute | solution.py:197
  25.6 13.0 %collective-permute-start.2 = (bf16[768,128]{1,0:T(8,128)(2,1)S(1)}, bf16[768,128]{1,0:T(8,128)(2,1)S(1)}, u32[]{:S(2)}, u32[]{:S(2)}) collective-permute-start(bf16[768,128]{1,0:T(8,128)(2,1)S(1)} %get-tuple-element.28), channel_id=1, source_target_pairs={{0,24},{8,16},{16,8},{24,0},{1,25},{9,17},{17,9},{25,1},{2,26},{10... | collective-permute-start | bytes 589832 | tf_op jit(solution)/shard_map/ppermute | solution.py:197
  37.5 2.5 %collective-permute-start.9 = (bf16[384,512]{1,0:T(8,128)(2,1)S(1)}, bf16[384,512]{1,0:T(8,128)(2,1)S(1)}, u32[]{:S(2)}, u32[]{:S(2)}) collective-permute-start(bf16[384,512]{1,0:T(8,128)(2,1)S(1)} %shard_map.66.refs_4_), channel_id=1, source_target_pairs={{0,1},{1,0},{2,3},{3,2},{4,5},{5,4},{6,7},{7,6},{8,9},{9,8},{10,11... | collective-permute-start | bytes 1179656 | tf_op jit(solution)/shard_map/ppermute | solution.py:202
  37.6 3.2 %collective-permute-start.10 = (bf16[384,512]{1,0:T(8,128)(2,1)S(1)}, bf16[384,512]{1,0:T(8,128)(2,1)S(1)}, u32[]{:S(2)}, u32[]{:S(2)}) collective-permute-start(bf16[384,512]{1,0:T(8,128)(2,1)S(1)} %collective-permute-done.6.refs_5_), channel_id=1, source_target_pairs={{0,1},{1,0},{2,3},{3,2},{4,5},{5,4},{6,7},{7,6},{8,9},{9,8},{10,11... | collective-permute-start | bytes 1179656 | tf_op jit(solution)/shard_map/ppermute | solution.py:202
  38.1 2.7 %collective-permute-start.11 = (bf16[384,512]{1,0:T(8,128)(2,1)S(1)}, bf16[384,512]{1,0:T(8,128)(2,1)S(1)}, u32[]{:S(2)}, u32[]{:S(2)}) collective-permute-start(bf16[384,512]{1,0:T(8,128)(2,1)S(1)} %collective-permute-done.7.refs_6_), channel_id=1, source_target_pairs={{0,1},{1,0},{2,3},{3,2},{4,5},{5,4},{6,7},{7,6},{8,9},{9,8},{10,11... | collective-permute-start | bytes 1179656 | tf_op jit(solution)/shard_map/ppermute | solution.py:202
  38.2 2.8 %collective-permute-start.12 = (bf16[384,512]{1,0:T(8,128)(2,1)S(1)}, bf16[384,512]{1,0:T(8,128)(2,1)S(1)}, u32[]{:S(2)}, u32[]{:S(2)}) collective-permute-start(bf16[384,512]{1,0:T(8,128)(2,1)S(1)} %collective-permute-done.8.refs_7_), channel_id=1, source_target_pairs={{0,1},{1,0},{2,3},{3,2},{4,5},{5,4},{6,7},{7,6},{8,9},{9,8},{10,11... | collective-permute-start | bytes 1179656 | tf_op jit(solution)/shard_map/ppermute | solution.py:202
  38.7 11.2 %collective-permute-start.20 = (bf16[384,512]{1,0:T(8,128)(2,1)S(1)}, bf16[384,512]{1,0:T(8,128)(2,1)S(1)}, u32[]{:S(2)}, u32[]{:S(2)}) collective-permute-start(bf16[384,512]{1,0:T(8,128)(2,1)S(1)} %shard_map.69.refs_4_), channel_id=1, source_target_pairs={{0,6},{2,0},{4,2},{6,4},{1,7},{3,1},{5,3},{7,5},{8,14},{10,8},{12,... | collective-permute-start | bytes 1179656 | tf_op jit(solution)/shard_map/ppermute | solution.py:206
  40.0 12.0 %collective-permute-start.18 = (bf16[384,512]{1,0:T(8,128)(2,1)S(1)}, bf16[384,512]{1,0:T(8,128)(2,1)S(1)}, u32[]{:S(2)}, u32[]{:S(2)}) collective-permute-start(bf16[384,512]{1,0:T(8,128)(2,1)S(1)} %shard_map.69.refs_4_), channel_id=1, source_target_pairs={{0,2},{2,4},{4,6},{6,0},{1,3},{3,5},{5,7},{7,1},{8,10},{10,12},{12... | collective-permute-start | bytes 1179656 | tf_op jit(solution)/shard_map/ppermute | solution.py:206
  42.1 10.0 %collective-permute-start.13 = (bf16[96,1024]{1,0:T(8,128)(2,1)S(1)}, bf16[96,1024]{1,0:T(8,128)(2,1)S(1)}, u32[]{:S(2)}, u32[]{:S(2)}) collective-permute-start(bf16[96,1024]{1,0:T(8,128)(2,1)S(1)} %get-tuple-element.34), channel_id=1, source_target_pairs={{0,32},{32,64},{64,96},{96,0},{1,33},{33,65},{65,97},{97,1},{2,34}... | collective-permute-start | bytes 589832 | tf_op jit(solution)/shard_map/ppermute | solution.py:206
  42.8 12.1 %collective-permute-start.14 = (bf16[96,1024]{1,0:T(8,128)(2,1)S(1)}, bf16[96,1024]{1,0:T(8,128)(2,1)S(1)}, u32[]{:S(2)}, u32[]{:S(2)}) collective-permute-start(bf16[96,1024]{1,0:T(8,128)(2,1)S(1)} %get-tuple-element.35), channel_id=1, source_target_pairs={{0,96},{32,0},{64,32},{96,64},{1,97},{33,1},{65,33},{97,65},{2,98}... | collective-permute-start | bytes 589832 | tf_op jit(solution)/shard_map/ppermute | solution.py:206
  44.4 10.5 %collective-permute-start.15 = (bf16[96,1024]{1,0:T(8,128)(2,1)S(1)}, bf16[96,1024]{1,0:T(8,128)(2,1)S(1)}, u32[]{:S(2)}, u32[]{:S(2)}) collective-permute-start(bf16[96,1024]{1,0:T(8,128)(2,1)S(1)} %get-tuple-element.36), channel_id=1, source_target_pairs={{0,64},{32,96},{64,0},{96,32},{1,65},{33,97},{65,1},{97,33},{2,66}... | collective-permute-start | bytes 589832 | tf_op jit(solution)/shard_map/ppermute | solution.py:206
  49.8 14.9 %collective-permute-start.17 = (bf16[384,512]{1,0:T(8,128)(2,1)S(1)}, bf16[384,512]{1,0:T(8,128)(2,1)S(1)}, u32[]{:S(2)}, u32[]{:S(2)}) collective-permute-start(bf16[384,512]{1,0:T(8,128)(2,1)S(1)} %shard_map.69.refs_4_), channel_id=1, source_target_pairs={{0,1},{1,0},{2,3},{3,2},{4,5},{5,4},{6,7},{7,6},{8,9},{9,8},{10,11... | collective-permute-start | bytes 1179656 | tf_op jit(solution)/shard_map/ppermute | solution.py:202
  52.1 12.7 %collective-permute-start.21 = (bf16[384,512]{1,0:T(8,128)(2,1)S(1)}, bf16[384,512]{1,0:T(8,128)(2,1)S(1)}, u32[]{:S(2)}, u32[]{:S(2)}) collective-permute-start(bf16[384,512]{1,0:T(8,128)(2,1)S(1)} %collective-permute-done.20.refs_0_.refs_6_), channel_id=1, source_target_pairs={{0,1},{1,0},{2,3},{3,2},{4,5},{5,4},{6,7},{7,6},{8,9},{9,8},{10,11... | collective-permute-start | bytes 1179656 | tf_op jit(solution)/shard_map/ppermute | solution.py:202
  52.1 12.7 %collective-permute-start.19 = (bf16[384,512]{1,0:T(8,128)(2,1)S(1)}, bf16[384,512]{1,0:T(8,128)(2,1)S(1)}, u32[]{:S(2)}, u32[]{:S(2)}) collective-permute-start(bf16[384,512]{1,0:T(8,128)(2,1)S(1)} %collective-permute-done.18.refs_5_), channel_id=1, source_target_pairs={{0,1},{1,0},{2,3},{3,2},{4,5},{5,4},{6,7},{7,6},{8,9},{9,8},{10,11... | collective-permute-start | bytes 1179656 | tf_op jit(solution)/shard_map/ppermute | solution.py:202
  54.9 9.8 %collective-permute-start.25 = (bf16[384,512]{1,0:T(8,128)(2,1)S(1)}, bf16[384,512]{1,0:T(8,128)(2,1)S(1)}, u32[]{:S(2)}, u32[]{:S(2)}) collective-permute-start(bf16[384,512]{1,0:T(8,128)(2,1)S(1)} %shard_map.71), channel_id=1, source_target_pairs={{0,6},{2,0},{4,2},{6,4},{1,7},{3,1},{5,3},{7,5},{8,14},{10,8},{12,... | collective-permute-start | bytes 1179656 | tf_op jit(solution)/shard_map/ppermute | solution.py:206
  56.8 11.5 %collective-permute-start.16 = (bf16[96,1024]{1,0:T(8,128)(2,1)S(1)}, bf16[96,1024]{1,0:T(8,128)(2,1)S(1)}, u32[]{:S(2)}, u32[]{:S(2)}) collective-permute-start(bf16[96,1024]{1,0:T(8,128)(2,1)S(1)} %get-tuple-element.38), channel_id=1, source_target_pairs={{0,128},{128,0},{1,129},{129,1},{2,130},{130,2},{3,131},{131,3},{4... | collective-permute-start | bytes 589832 | tf_op jit(solution)/shard_map/ppermute | solution.py:253
  64.8 14.9 %collective-permute-start.26 = (bf16[384,512]{1,0:T(8,128)(2,1)S(1)}, bf16[384,512]{1,0:T(8,128)(2,1)S(1)}, u32[]{:S(2)}, u32[]{:S(2)}) collective-permute-start(bf16[384,512]{1,0:T(8,128)(2,1)S(1)} %collective-permute-done.25.refs_7_), channel_id=1, source_target_pairs={{0,1},{1,0},{2,3},{3,2},{4,5},{5,4},{6,7},{7,6},{8,9},{9,8},{10,11... | collective-permute-start | bytes 1179656 | tf_op jit(solution)/shard_map/ppermute | solution.py:202
  68.6 22.5 %copy-start.2 = (bf16[768,768]{1,0:T(8,128)(2,1)S(1)}, bf16[768,768]{1,0:T(8,128)(2,1)}, u32[]{:S(2)}) copy-start(bf16[768,768]{1,0:T(8,128)(2,1)} %refs_5_.1) | copy-start | bytes 3538948
  68.6 22.5 %copy-start.3 = (bf16[8,32,768]{2,1,0:T(8,128)(2,1)S(1)}, bf16[8,32,768]{2,1,0:T(8,128)(2,1)}, u32[]{:S(2)}) copy-start(bf16[8,32,768]{2,1,0:T(8,128)(2,1)} %param.6) | copy-start | bytes 1179652
  68.6 7.4 %collective-permute-start.22 = (bf16[96,1024]{1,0:T(8,128)(2,1)S(1)}, bf16[96,1024]{1,0:T(8,128)(2,1)S(1)}, u32[]{:S(2)}, u32[]{:S(2)}) collective-permute-start(bf16[96,1024]{1,0:T(8,128)(2,1)S(1)} %shard_map.70.refs_0_), channel_id=1, source_target_pairs={{0,32},{32,64},{64,96},{96,0},{1,33},{33,65},{65,97},{97,1},{2,34}... | collective-permute-start | bytes 589832 | tf_op jit(solution)/shard_map/ppermute | solution.py:206
  69.9 7.9 %collective-permute-start.23 = (bf16[96,1024]{1,0:T(8,128)(2,1)S(1)}, bf16[96,1024]{1,0:T(8,128)(2,1)S(1)}, u32[]{:S(2)}, u32[]{:S(2)}) collective-permute-start(bf16[96,1024]{1,0:T(8,128)(2,1)S(1)} %shard_map.70.refs_0_), channel_id=1, source_target_pairs={{0,64},{32,96},{64,0},{96,32},{1,65},{33,97},{65,1},{97,33},{2,66}... | collective-permute-start | bytes 589832 | tf_op jit(solution)/shard_map/ppermute | solution.py:206
  71.0 8.7 %collective-permute-start.24 = (bf16[96,1024]{1,0:T(8,128)(2,1)S(1)}, bf16[96,1024]{1,0:T(8,128)(2,1)S(1)}, u32[]{:S(2)}, u32[]{:S(2)}) collective-permute-start(bf16[96,1024]{1,0:T(8,128)(2,1)S(1)} %shard_map.70.refs_0_), channel_id=1, source_target_pairs={{0,96},{32,0},{64,32},{96,64},{1,97},{33,1},{65,33},{97,65},{2,98}... | collective-permute-start | bytes 589832 | tf_op jit(solution)/shard_map/ppermute | solution.py:206
  80.4 7.0 %collective-permute-start.27 = (bf16[384,128]{1,0:T(8,128)(2,1)S(1)}, bf16[384,128]{1,0:T(8,128)(2,1)S(1)}, u32[]{:S(2)}, u32[]{:S(2)}) collective-permute-start(bf16[384,128]{1,0:T(8,128)(2,1)S(1)} %get-tuple-element.40), channel_id=1, source_target_pairs={{0,8},{8,0},{16,24},{24,16},{1,9},{9,1},{17,25},{25,17},{2,10},{10... | collective-permute-start | bytes 294920 | tf_op jit(solution)/shard_map/ppermute | solution.py:197
  82.6 8.5 %collective-permute-start.28 = (bf16[384,128]{1,0:T(8,128)(2,1)S(1)}, bf16[384,128]{1,0:T(8,128)(2,1)S(1)}, u32[]{:S(2)}, u32[]{:S(2)}) collective-permute-start(bf16[384,128]{1,0:T(8,128)(2,1)S(1)} %get-tuple-element.41), channel_id=1, source_target_pairs={{0,16},{8,24},{16,0},{24,8},{1,17},{9,25},{17,1},{25,9},{2,18},{10... | collective-permute-start | bytes 294920 | tf_op jit(solution)/shard_map/ppermute | solution.py:197
  83.4 7.7 %collective-permute-start.29 = (bf16[384,128]{1,0:T(8,128)(2,1)S(1)}, bf16[384,128]{1,0:T(8,128)(2,1)S(1)}, u32[]{:S(2)}, u32[]{:S(2)}) collective-permute-start(bf16[384,128]{1,0:T(8,128)(2,1)S(1)} %get-tuple-element.42), channel_id=1, source_target_pairs={{0,24},{8,16},{16,8},{24,0},{1,25},{9,17},{17,9},{25,1},{2,26},{10... | collective-permute-start | bytes 294920 | tf_op jit(solution)/shard_map/ppermute | solution.py:197
  (2 other events, 15.0 us)

commit v5 on v4

--- a/solution.py
+++ b/solution.py
@@ -262,7 +262,7 @@
     )(*probs, *slabs)
     (out,) = call(
         out_kernel, [((256, 768), BF16)], [pieces, pltpu.VMEM((256, 768), BF16)]
-    )(*line(context), flat, wf)
+    )(*line(context, (2, 3, 1)), flat, wf)
     return out.reshape(8, 32, 768)
 
 

time: 92.5 us -> 92.5 us (level)
  no operation moved by 1% of the time
where the time goes in v5:
time: 92.5 us
  waiting for transfers between devices  46.1 us (50%)
  starting transfers between devices  39.5 us (43%)
  Pallas kernels  6.7 us (7%)
    ppermute x9, waiting for transfers between devices, line(): got = {m: lax.ppermute(pieces[m], 'zl', LINE[m]) for m in order}  24.3 us
    ppermute x12, waiting for transfers between devices, over(): return [lax.ppermute(arrays[k], axis, RING[k]) for k in order]  18.1 us
    ppermute x12, starting transfers between devices, over(): return [lax.ppermute(arrays[k], axis, RING[k]) for k in order]  16.6 us
    ppermute x9, starting transfers between devices, line(): got = {m: lax.ppermute(pieces[m], 'zl', LINE[m]) for m in order}  15.5 us
    pallas_call x10, Pallas kernels, run(): pl.pallas_call(kernel, out_shape=[jax.ShapeDtypeStruct(s, d) for s, d in...  6.7 us
    ppermute x1, starting transfers between devices, per_device(): other = lax.ppermute(sent, 'zh', [(0, 1), (1, 0)])  5.92 us
    ppermute x1, waiting for transfers between devices, per_device(): other = lax.ppermute(sent, 'zh', [(0, 1), (1, 0)])  3.53 us
  transfers between devices with their start and end apart: 30, of which 14 were waited for; matrix products, arithmetic and copies ran while one was open for 0% of the time, Pallas kernels for 3%

profile of v5, /device:TPU:6, one launch (start us, length us, event | category | flops | bytes accessed | tf_op | source)
XLA Modules:
  0.0 92.5 jit_solution(6553241307171995868)
XLA Ops:
  0.0 2.2 %shard_map.64 = (bf16[256,768]{1,0:T(8,128)(2,1)S(1)}, bf16[384,128]{1,0:T(8,128)(2,1)S(1)}, bf16[384,128]{1,0:T(8,128)(2,1)S(1)}, bf16[384,128]{1,0:T(8,128)(2,1)S(1)}, bf16[384,128]{1,0:T(8,128)(2,1)S(1)}) custom-call(bf16[256,768]{1,0:T(8,128)(2,1)} %bitcast.2, f32[768]{0:T(1024)} %refs_1_.2, bf16[768,768]{1,0:T(8,128)(2,1)} %refs_2_.2), custom_call_target="tpu_custom_call" | custom-call | flops 5000000000 | bytes 1000000 | tf_op jit(solution)/shard_map/pallas_call | solution.py:31
  2.2 2.0 %collective-permute-start.3 = (bf16[384,128]{1,0:T(8,128)(2,1)S(1)}, bf16[384,128]{1,0:T(8,128)(2,1)S(1)}, u32[]{:S(2)}, u32[]{:S(2)}) collective-permute-start(bf16[384,128]{1,0:T(8,128)(2,1)S(1)} %get-tuple-element.30), channel_id=1, source_target_pairs={{0,8},{8,0},{16,24},{24,16},{1,9},{9,1},{17,25},{25,17},{2,10},{10... | collective-permute-start | bytes 294920 | tf_op jit(solution)/shard_map/ppermute | solution.py:197
  4.2 3.3 %collective-permute-start.4 = (bf16[384,128]{1,0:T(8,128)(2,1)S(1)}, bf16[384,128]{1,0:T(8,128)(2,1)S(1)}, u32[]{:S(2)}, u32[]{:S(2)}) collective-permute-start(bf16[384,128]{1,0:T(8,128)(2,1)S(1)} %get-tuple-element.31), channel_id=1, source_target_pairs={{0,16},{8,24},{16,0},{24,8},{1,17},{9,25},{17,1},{25,9},{2,18},{10... | collective-permute-start | bytes 294920 | tf_op jit(solution)/shard_map/ppermute | solution.py:197
  8.4 6.8 %collective-permute-done.4.refs_2_ = bf16[384,128]{1,0:T(8,128)(2,1)S(1)} collective-permute-done((bf16[384,128]{1,0:T(8,128)(2,1)S(1)}, bf16[384,128]{1,0:T(8,128)(2,1)S(1)}, u32[]{:S(2)}, u32[]{:S(2)}) %collective-permute-start.4) | collective-permute-done | bytes 98336 | tf_op jit(solution)/shard_map/ppermute | solution.py:197
  15.3 1.7 %collective-permute-start.6 = (bf16[384,512]{1,0:T(8,128)(2,1)S(1)}, bf16[384,512]{1,0:T(8,128)(2,1)S(1)}, u32[]{:S(2)}, u32[]{:S(2)}) collective-permute-start(bf16[384,512]{1,0:T(8,128)(2,1)S(1)} %shard_map.66.refs_4_), channel_id=1, source_target_pairs={{0,2},{2,4},{4,6},{6,0},{1,3},{3,5},{5,7},{7,1},{8,10},{10,12},{12... | collective-permute-start | bytes 1179656 | tf_op jit(solution)/shard_map/ppermute | solution.py:206
  17.0 1.7 %collective-permute-start.7 = (bf16[384,512]{1,0:T(8,128)(2,1)S(1)}, bf16[384,512]{1,0:T(8,128)(2,1)S(1)}, u32[]{:S(2)}, u32[]{:S(2)}) collective-permute-start(bf16[384,512]{1,0:T(8,128)(2,1)S(1)} %shard_map.66.refs_4_), channel_id=1, source_target_pairs={{0,6},{2,0},{4,2},{6,4},{1,7},{3,1},{5,3},{7,5},{8,14},{10,8},{12,... | collective-permute-start | bytes 1179656 | tf_op jit(solution)/shard_map/ppermute | solution.py:206
  18.6 1.6 %collective-permute-start = (bf16[768,128]{1,0:T(8,128)(2,1)S(1)}, bf16[768,128]{1,0:T(8,128)(2,1)S(1)}, u32[]{:S(2)}, u32[]{:S(2)}) collective-permute-start(bf16[768,128]{1,0:T(8,128)(2,1)S(1)} %get-tuple-element.26), channel_id=1, source_target_pairs={{0,8},{8,0},{16,24},{24,16},{1,9},{9,1},{17,25},{25,17},{2,10},{10... | collective-permute-start | bytes 589832 | tf_op jit(solution)/shard_map/ppermute | solution.py:197
  20.3 2.0 %collective-permute-start.8 = (bf16[384,512]{1,0:T(8,128)(2,1)S(1)}, bf16[384,512]{1,0:T(8,128)(2,1)S(1)}, u32[]{:S(2)}, u32[]{:S(2)}) collective-permute-start(bf16[384,512]{1,0:T(8,128)(2,1)S(1)} %shard_map.66.refs_4_), channel_id=1, source_target_pairs={{0,4},{2,6},{4,0},{6,2},{1,5},{3,7},{5,1},{7,3},{8,12},{10,14},{12... | collective-permute-start | bytes 1179656 | tf_op jit(solution)/shard_map/ppermute | solution.py:206
  22.2 1.4 %collective-permute-start.1 = (bf16[768,128]{1,0:T(8,128)(2,1)S(1)}, bf16[768,128]{1,0:T(8,128)(2,1)S(1)}, u32[]{:S(2)}, u32[]{:S(2)}) collective-permute-start(bf16[768,128]{1,0:T(8,128)(2,1)S(1)} %get-tuple-element.27), channel_id=1, source_target_pairs={{0,16},{8,24},{16,0},{24,8},{1,17},{9,25},{17,1},{25,9},{2,18},{10... | collective-permute-start | bytes 589832 | tf_op jit(solution)/shard_map/ppermute | solution.py:197
  23.7 1.9 %collective-permute-done.refs_1_ = bf16[768,128]{1,0:T(8,128)(2,1)S(1)} collective-permute-done((bf16[768,128]{1,0:T(8,128)(2,1)S(1)}, bf16[768,128]{1,0:T(8,128)(2,1)S(1)}, u32[]{:S(2)}, u32[]{:S(2)}) %collective-permute-start) | collective-permute-done | bytes 196640 | tf_op jit(solution)/shard_map/ppermute | solution.py:197
  25.6 2.5 %collective-permute-start.2 = (bf16[768,128]{1,0:T(8,128)(2,1)S(1)}, bf16[768,128]{1,0:T(8,128)(2,1)S(1)}, u32[]{:S(2)}, u32[]{:S(2)}) collective-permute-start(bf16[768,128]{1,0:T(8,128)(2,1)S(1)} %get-tuple-element.28), channel_id=1, source_target_pairs={{0,24},{8,16},{16,8},{24,0},{1,25},{9,17},{17,9},{25,1},{2,26},{10... | collective-permute-start | bytes 589832 | tf_op jit(solution)/shard_map/ppermute | solution.py:197
  28.1 9.5 %collective-permute-done.1.refs_2_ = bf16[768,128]{1,0:T(8,128)(2,1)S(1)} collective-permute-done((bf16[768,128]{1,0:T(8,128)(2,1)S(1)}, bf16[768,128]{1,0:T(8,128)(2,1)S(1)}, u32[]{:S(2)}, u32[]{:S(2)}) %collective-permute-start.1) | collective-permute-done | bytes 196640 | tf_op jit(solution)/shard_map/ppermute | solution.py:197
  38.7 1.4 %collective-permute-start.20 = (bf16[384,512]{1,0:T(8,128)(2,1)S(1)}, bf16[384,512]{1,0:T(8,128)(2,1)S(1)}, u32[]{:S(2)}, u32[]{:S(2)}) collective-permute-start(bf16[384,512]{1,0:T(8,128)(2,1)S(1)} %shard_map.69.refs_4_), channel_id=1, source_target_pairs={{0,6},{2,0},{4,2},{6,4},{1,7},{3,1},{5,3},{7,5},{8,14},{10,8},{12,... | collective-permute-start | bytes 1179656 | tf_op jit(solution)/shard_map/ppermute | solution.py:206
  42.8 1.5 %collective-permute-start.14 = (bf16[96,1024]{1,0:T(8,128)(2,1)S(1)}, bf16[96,1024]{1,0:T(8,128)(2,1)S(1)}, u32[]{:S(2)}, u32[]{:S(2)}) collective-permute-start(bf16[96,1024]{1,0:T(8,128)(2,1)S(1)} %get-tuple-element.35), channel_id=1, source_target_pairs={{0,96},{32,0},{64,32},{96,64},{1,97},{33,1},{65,33},{97,65},{2,98}... | collective-permute-start | bytes 589832 | tf_op jit(solution)/shard_map/ppermute | solution.py:206
  44.4 1.4 %collective-permute-start.15 = (bf16[96,1024]{1,0:T(8,128)(2,1)S(1)}, bf16[96,1024]{1,0:T(8,128)(2,1)S(1)}, u32[]{:S(2)}, u32[]{:S(2)}) collective-permute-start(bf16[96,1024]{1,0:T(8,128)(2,1)S(1)} %get-tuple-element.36), channel_id=1, source_target_pairs={{0,64},{32,96},{64,0},{96,32},{1,65},{33,97},{65,1},{97,33},{2,66}... | collective-permute-start | bytes 589832 | tf_op jit(solution)/shard_map/ppermute | solution.py:206
  45.8 4.1 %collective-permute-done.20.refs_0_.refs_6_ = bf16[384,512]{1,0:T(8,128)(2,1)S(1)} collective-permute-done((bf16[384,512]{1,0:T(8,128)(2,1)S(1)}, bf16[384,512]{1,0:T(8,128)(2,1)S(1)}, u32[]{:S(2)}, u32[]{:S(2)}) %collective-permute-start.20) | collective-permute-done | bytes 393248 | tf_op jit(solution)/shard_map/ppermute | solution.py:206
  49.8 2.2 %collective-permute-done.18.refs_5_ = bf16[384,512]{1,0:T(8,128)(2,1)S(1)} collective-permute-done((bf16[384,512]{1,0:T(8,128)(2,1)S(1)}, bf16[384,512]{1,0:T(8,128)(2,1)S(1)}, u32[]{:S(2)}, u32[]{:S(2)}) %collective-permute-start.18) | collective-permute-done | bytes 393248 | tf_op jit(solution)/shard_map/ppermute | solution.py:206
  52.6 2.3 %collective-permute-done.14.refs_2_ = bf16[96,1024]{1,0:T(8,128)(2,1)S(1)} collective-permute-done((bf16[96,1024]{1,0:T(8,128)(2,1)S(1)}, bf16[96,1024]{1,0:T(8,128)(2,1)S(1)}, u32[]{:S(2)}, u32[]{:S(2)}) %collective-permute-start.14) | collective-permute-done | bytes 196640 | tf_op jit(solution)/shard_map/ppermute | solution.py:206
  54.9 1.8 %collective-permute-start.25 = (bf16[384,512]{1,0:T(8,128)(2,1)S(1)}, bf16[384,512]{1,0:T(8,128)(2,1)S(1)}, u32[]{:S(2)}, u32[]{:S(2)}) collective-permute-start(bf16[384,512]{1,0:T(8,128)(2,1)S(1)} %shard_map.71), channel_id=1, source_target_pairs={{0,6},{2,0},{4,2},{6,4},{1,7},{3,1},{5,3},{7,5},{8,14},{10,8},{12,... | collective-permute-start | bytes 1179656 | tf_op jit(solution)/shard_map/ppermute | solution.py:206
  56.8 5.9 %collective-permute-start.16 = (bf16[96,1024]{1,0:T(8,128)(2,1)S(1)}, bf16[96,1024]{1,0:T(8,128)(2,1)S(1)}, u32[]{:S(2)}, u32[]{:S(2)}) collective-permute-start(bf16[96,1024]{1,0:T(8,128)(2,1)S(1)} %get-tuple-element.38), channel_id=1, source_target_pairs={{0,128},{128,0},{1,129},{129,1},{2,130},{130,2},{3,131},{131,3},{4... | collective-permute-start | bytes 589832 | tf_op jit(solution)/shard_map/ppermute | solution.py:253
  62.7 2.0 %collective-permute-done.25.refs_7_ = bf16[384,512]{1,0:T(8,128)(2,1)S(1)} collective-permute-done((bf16[384,512]{1,0:T(8,128)(2,1)S(1)}, bf16[384,512]{1,0:T(8,128)(2,1)S(1)}, u32[]{:S(2)}, u32[]{:S(2)}) %collective-permute-start.25) | collective-permute-done | bytes 393248 | tf_op jit(solution)/shard_map/ppermute | solution.py:206
  64.8 3.5 %collective-permute-done.16.refs_1_ = bf16[96,1024]{1,0:T(8,128)(2,1)S(1)} collective-permute-done((bf16[96,1024]{1,0:T(8,128)(2,1)S(1)}, bf16[96,1024]{1,0:T(8,128)(2,1)S(1)}, u32[]{:S(2)}, u32[]{:S(2)}) %collective-permute-start.16) | collective-permute-done | bytes 196640 | tf_op jit(solution)/shard_map/ppermute | solution.py:253
  68.6 1.3 %collective-permute-start.22 = (bf16[96,1024]{1,0:T(8,128)(2,1)S(1)}, bf16[96,1024]{1,0:T(8,128)(2,1)S(1)}, u32[]{:S(2)}, u32[]{:S(2)}) collective-permute-start(bf16[96,1024]{1,0:T(8,128)(2,1)S(1)} %shard_map.70.refs_0_), channel_id=1, source_target_pairs={{0,32},{32,64},{64,96},{96,0},{1,33},{33,65},{65,97},{97,1},{2,34}... | collective-permute-start | bytes 589832 | tf_op jit(solution)/shard_map/ppermute | solution.py:206
  71.0 1.3 %collective-permute-start.24 = (bf16[96,1024]{1,0:T(8,128)(2,1)S(1)}, bf16[96,1024]{1,0:T(8,128)(2,1)S(1)}, u32[]{:S(2)}, u32[]{:S(2)}) collective-permute-start(bf16[96,1024]{1,0:T(8,128)(2,1)S(1)} %shard_map.70.refs_0_), channel_id=1, source_target_pairs={{0,96},{32,0},{64,32},{96,64},{1,97},{33,1},{65,33},{97,65},{2,98}... | collective-permute-start | bytes 589832 | tf_op jit(solution)/shard_map/ppermute | solution.py:206
  72.3 3.7 %collective-permute-done.22.refs_1_ = bf16[96,1024]{1,0:T(8,128)(2,1)S(1)} collective-permute-done((bf16[96,1024]{1,0:T(8,128)(2,1)S(1)}, bf16[96,1024]{1,0:T(8,128)(2,1)S(1)}, u32[]{:S(2)}, u32[]{:S(2)}) %collective-permute-start.22) | collective-permute-done | bytes 196640 | tf_op jit(solution)/shard_map/ppermute | solution.py:206
  76.1 1.7 %collective-permute-done.23.refs_2_ = bf16[96,1024]{1,0:T(8,128)(2,1)S(1)} collective-permute-done((bf16[96,1024]{1,0:T(8,128)(2,1)S(1)}, bf16[96,1024]{1,0:T(8,128)(2,1)S(1)}, u32[]{:S(2)}, u32[]{:S(2)}) %collective-permute-start.23) | collective-permute-done | bytes 196640 | tf_op jit(solution)/shard_map/ppermute | solution.py:206
  77.8 2.0 %collective-permute-done.24.refs_3_ = bf16[96,1024]{1,0:T(8,128)(2,1)S(1)} collective-permute-done((bf16[96,1024]{1,0:T(8,128)(2,1)S(1)}, bf16[96,1024]{1,0:T(8,128)(2,1)S(1)}, u32[]{:S(2)}, u32[]{:S(2)}) %collective-permute-start.24) | collective-permute-done | bytes 196640 | tf_op jit(solution)/shard_map/ppermute | solution.py:206
  80.4 2.2 %collective-permute-start.27 = (bf16[384,128]{1,0:T(8,128)(2,1)S(1)}, bf16[384,128]{1,0:T(8,128)(2,1)S(1)}, u32[]{:S(2)}, u32[]{:S(2)}) collective-permute-start(bf16[384,128]{1,0:T(8,128)(2,1)S(1)} %get-tuple-element.40), channel_id=1, source_target_pairs={{0,8},{8,0},{16,24},{24,16},{1,9},{9,1},{17,25},{25,17},{2,10},{10... | collective-permute-start | bytes 294920 | tf_op jit(solution)/shard_map/ppermute | solution.py:197
  83.4 1.6 %collective-permute-start.29 = (bf16[384,128]{1,0:T(8,128)(2,1)S(1)}, bf16[384,128]{1,0:T(8,128)(2,1)S(1)}, u32[]{:S(2)}, u32[]{:S(2)}) collective-permute-start(bf16[384,128]{1,0:T(8,128)(2,1)S(1)} %get-tuple-element.42), channel_id=1, source_target_pairs={{0,24},{8,16},{16,8},{24,0},{1,25},{9,17},{17,9},{25,1},{2,26},{10... | collective-permute-start | bytes 294920 | tf_op jit(solution)/shard_map/ppermute | solution.py:197
  85.0 2.4 %collective-permute-done.27.refs_1_ = bf16[384,128]{1,0:T(8,128)(2,1)S(1)} collective-permute-done((bf16[384,128]{1,0:T(8,128)(2,1)S(1)}, bf16[384,128]{1,0:T(8,128)(2,1)S(1)}, u32[]{:S(2)}, u32[]{:S(2)}) %collective-permute-start.27) | collective-permute-done | bytes 98336 | tf_op jit(solution)/shard_map/ppermute | solution.py:197
  87.4 3.7 %collective-permute-done.28.refs_2_ = bf16[384,128]{1,0:T(8,128)(2,1)S(1)} collective-permute-done((bf16[384,128]{1,0:T(8,128)(2,1)S(1)}, bf16[384,128]{1,0:T(8,128)(2,1)S(1)}, u32[]{:S(2)}, u32[]{:S(2)}) %collective-permute-start.28) | collective-permute-done | bytes 98336 | tf_op jit(solution)/shard_map/ppermute | solution.py:197
  91.1 1.3 %shard_map.73 = bf16[256,768]{1,0:T(8,128)(2,1)} custom-call(bf16[384,128]{1,0:T(8,128)(2,1)S(1)} %get-tuple-element.39.refs_0_, bf16[384,128]{1,0:T(8,128)(2,1)S(1)} %collective-permute-done.27.refs_1_, bf16[384,128]{1,0:T(8,128)(2,1)S(1)} %collective-permute-done.28.refs_2_, bf16[384,128]{1,0:T(8,128)(2,1)S(1)} %collective-permute-done.29.refs_3_, ...), custom_call_target="tpu_custom_call" | custom-call | flops 5000000000 | bytes 1000000 | tf_op jit(solution)/shard_map/pallas_call | solution.py:31
  (46 shorter events, 8.4 us)
Async XLA Ops:
  2.2 6.2 %collective-permute-start.3 = (bf16[384,128]{1,0:T(8,128)(2,1)S(1)}, bf16[384,128]{1,0:T(8,128)(2,1)S(1)}, u32[]{:S(2)}, u32[]{:S(2)}) collective-permute-start(bf16[384,128]{1,0:T(8,128)(2,1)S(1)} %get-tuple-element.30), channel_id=1, source_target_pairs={{0,8},{8,0},{16,24},{24,16},{1,9},{9,1},{17,25},{25,17},{2,10},{10... | collective-permute-start | bytes 294920 | tf_op jit(solution)/shard_map/ppermute | solution.py:197
  4.2 11.0 %collective-permute-start.4 = (bf16[384,128]{1,0:T(8,128)(2,1)S(1)}, bf16[384,128]{1,0:T(8,128)(2,1)S(1)}, u32[]{:S(2)}, u32[]{:S(2)}) collective-permute-start(bf16[384,128]{1,0:T(8,128)(2,1)S(1)} %get-tuple-element.31), channel_id=1, source_target_pairs={{0,16},{8,24},{16,0},{24,8},{1,17},{9,25},{17,1},{25,9},{2,18},{10... | collective-permute-start | bytes 294920 | tf_op jit(solution)/shard_map/ppermute | solution.py:197
  7.5 7.7 %collective-permute-start.5 = (bf16[384,128]{1,0:T(8,128)(2,1)S(1)}, bf16[384,128]{1,0:T(8,128)(2,1)S(1)}, u32[]{:S(2)}, u32[]{:S(2)}) collective-permute-start(bf16[384,128]{1,0:T(8,128)(2,1)S(1)} %get-tuple-element.32), channel_id=1, source_target_pairs={{0,24},{8,16},{16,8},{24,0},{1,25},{9,17},{17,9},{25,1},{2,26},{10... | collective-permute-start | bytes 294920 | tf_op jit(solution)/shard_map/ppermute | solution.py:197
  15.3 22.3 %collective-permute-start.6 = (bf16[384,512]{1,0:T(8,128)(2,1)S(1)}, bf16[384,512]{1,0:T(8,128)(2,1)S(1)}, u32[]{:S(2)}, u32[]{:S(2)}) collective-permute-start(bf16[384,512]{1,0:T(8,128)(2,1)S(1)} %shard_map.66.refs_4_), channel_id=1, source_target_pairs={{0,2},{2,4},{4,6},{6,0},{1,3},{3,5},{5,7},{7,1},{8,10},{10,12},{12... | collective-permute-start | bytes 1179656 | tf_op jit(solution)/shard_map/ppermute | solution.py:206
  17.0 21.1 %collective-permute-start.7 = (bf16[384,512]{1,0:T(8,128)(2,1)S(1)}, bf16[384,512]{1,0:T(8,128)(2,1)S(1)}, u32[]{:S(2)}, u32[]{:S(2)}) collective-permute-start(bf16[384,512]{1,0:T(8,128)(2,1)S(1)} %shard_map.66.refs_4_), channel_id=1, source_target_pairs={{0,6},{2,0},{4,2},{6,4},{1,7},{3,1},{5,3},{7,5},{8,14},{10,8},{12,... | collective-permute-start | bytes 1179656 | tf_op jit(solution)/shard_map/ppermute | solution.py:206
  18.6 6.9 %collective-permute-start = (bf16[768,128]{1,0:T(8,128)(2,1)S(1)}, bf16[768,128]{1,0:T(8,128)(2,1)S(1)}, u32[]{:S(2)}, u32[]{:S(2)}) collective-permute-start(bf16[768,128]{1,0:T(8,128)(2,1)S(1)} %get-tuple-element.26), channel_id=1, source_target_pairs={{0,8},{8,0},{16,24},{24,16},{1,9},{9,1},{17,25},{25,17},{2,10},{10... | collective-permute-start | bytes 589832 | tf_op jit(solution)/shard_map/ppermute | solution.py:197
  20.3 17.9 %collective-permute-start.8 = (bf16[384,512]{1,0:T(8,128)(2,1)S(1)}, bf16[384,512]{1,0:T(8,128)(2,1)S(1)}, u32[]{:S(2)}, u32[]{:S(2)}) collective-permute-start(bf16[384,512]{1,0:T(8,128)(2,1)S(1)} %shard_map.66.refs_4_), channel_id=1, source_target_pairs={{0,4},{2,6},{4,0},{6,2},{1,5},{3,7},{5,1},{7,3},{8,12},{10,14},{12... | collective-permute-start | bytes 1179656 | tf_op jit(solution)/shard_map/ppermute | solution.py:206
  22.2 15.3 %collective-permute-start.1 = (bf16[768,128]{1,0:T(8,128)(2,1)S(1)}, bf16[768,128]{1,0:T(8,128)(2,1)S(1)}, u32[]{:S(2)}, u32[]{:S(2)}) collective-permute-start(bf16[768,128]{1,0:T(8,128)(2,1)S(1)} %get-tuple-element.27), channel_id=1, source_target_pairs={{0,16},{8,24},{16,0},{24,8},{1,17},{9,25},{17,1},{25,9},{2,18},{10... | collective-permute-start | bytes 589832 | tf_op jit(solution)/shard_map/ppermute | solution.py:197
  25.6 13.0 %collective-permute-start.2 = (bf16[768,128]{1,0:T(8,128)(2,1)S(1)}, bf16[768,128]{1,0:T(8,128)(2,1)S(1)}, u32[]{:S(2)}, u32[]{:S(2)}) collective-permute-start(bf16[768,128]{1,0:T(8,128)(2,1)S(1)} %get-tuple-element.28), channel_id=1, source_target_pairs={{0,24},{8,16},{16,8},{24,0},{1,25},{9,17},{17,9},{25,1},{2,26},{10... | collective-permute-start | bytes 589832 | tf_op jit(solution)/shard_map/ppermute | solution.py:197
  37.5 2.5 %collective-permute-start.9 = (bf16[384,512]{1,0:T(8,128)(2,1)S(1)}, bf16[384,512]{1,0:T(8,128)(2,1)S(1)}, u32[]{:S(2)}, u32[]{:S(2)}) collective-permute-start(bf16[384,512]{1,0:T(8,128)(2,1)S(1)} %shard_map.66.refs_4_), channel_id=1, source_target_pairs={{0,1},{1,0},{2,3},{3,2},{4,5},{5,4},{6,7},{7,6},{8,9},{9,8},{10,11... | collective-permute-start | bytes 1179656 | tf_op jit(solution)/shard_map/ppermute | solution.py:202
  37.6 3.2 %collective-permute-start.10 = (bf16[384,512]{1,0:T(8,128)(2,1)S(1)}, bf16[384,512]{1,0:T(8,128)(2,1)S(1)}, u32[]{:S(2)}, u32[]{:S(2)}) collective-permute-start(bf16[384,512]{1,0:T(8,128)(2,1)S(1)} %collective-permute-done.6.refs_5_), channel_id=1, source_target_pairs={{0,1},{1,0},{2,3},{3,2},{4,5},{5,4},{6,7},{7,6},{8,9},{9,8},{10,11... | collective-permute-start | bytes 1179656 | tf_op jit(solution)/shard_map/ppermute | solution.py:202
  38.1 2.7 %collective-permute-start.11 = (bf16[384,512]{1,0:T(8,128)(2,1)S(1)}, bf16[384,512]{1,0:T(8,128)(2,1)S(1)}, u32[]{:S(2)}, u32[]{:S(2)}) collective-permute-start(bf16[384,512]{1,0:T(8,128)(2,1)S(1)} %collective-permute-done.7.refs_6_), channel_id=1, source_target_pairs={{0,1},{1,0},{2,3},{3,2},{4,5},{5,4},{6,7},{7,6},{8,9},{9,8},{10,11... | collective-permute-start | bytes 1179656 | tf_op jit(solution)/shard_map/ppermute | solution.py:202
  38.2 2.8 %collective-permute-start.12 = (bf16[384,512]{1,0:T(8,128)(2,1)S(1)}, bf16[384,512]{1,0:T(8,128)(2,1)S(1)}, u32[]{:S(2)}, u32[]{:S(2)}) collective-permute-start(bf16[384,512]{1,0:T(8,128)(2,1)S(1)} %collective-permute-done.8.refs_7_), channel_id=1, source_target_pairs={{0,1},{1,0},{2,3},{3,2},{4,5},{5,4},{6,7},{7,6},{8,9},{9,8},{10,11... | collective-permute-start | bytes 1179656 | tf_op jit(solution)/shard_map/ppermute | solution.py:202
  38.7 11.2 %collective-permute-start.20 = (bf16[384,512]{1,0:T(8,128)(2,1)S(1)}, bf16[384,512]{1,0:T(8,128)(2,1)S(1)}, u32[]{:S(2)}, u32[]{:S(2)}) collective-permute-start(bf16[384,512]{1,0:T(8,128)(2,1)S(1)} %shard_map.69.refs_4_), channel_id=1, source_target_pairs={{0,6},{2,0},{4,2},{6,4},{1,7},{3,1},{5,3},{7,5},{8,14},{10,8},{12,... | collective-permute-start | bytes 1179656 | tf_op jit(solution)/shard_map/ppermute | solution.py:206
  40.0 12.0 %collective-permute-start.18 = (bf16[384,512]{1,0:T(8,128)(2,1)S(1)}, bf16[384,512]{1,0:T(8,128)(2,1)S(1)}, u32[]{:S(2)}, u32[]{:S(2)}) collective-permute-start(bf16[384,512]{1,0:T(8,128)(2,1)S(1)} %shard_map.69.refs_4_), channel_id=1, source_target_pairs={{0,2},{2,4},{4,6},{6,0},{1,3},{3,5},{5,7},{7,1},{8,10},{10,12},{12... | collective-permute-start | bytes 1179656 | tf_op jit(solution)/shard_map/ppermute | solution.py:206
  42.1 10.0 %collective-permute-start.13 = (bf16[96,1024]{1,0:T(8,128)(2,1)S(1)}, bf16[96,1024]{1,0:T(8,128)(2,1)S(1)}, u32[]{:S(2)}, u32[]{:S(2)}) collective-permute-start(bf16[96,1024]{1,0:T(8,128)(2,1)S(1)} %get-tuple-element.34), channel_id=1, source_target_pairs={{0,32},{32,64},{64,96},{96,0},{1,33},{33,65},{65,97},{97,1},{2,34}... | collective-permute-start | bytes 589832 | tf_op jit(solution)/shard_map/ppermute | solution.py:206
  42.8 12.1 %collective-permute-start.14 = (bf16[96,1024]{1,0:T(8,128)(2,1)S(1)}, bf16[96,1024]{1,0:T(8,128)(2,1)S(1)}, u32[]{:S(2)}, u32[]{:S(2)}) collective-permute-start(bf16[96,1024]{1,0:T(8,128)(2,1)S(1)} %get-tuple-element.35), channel_id=1, source_target_pairs={{0,96},{32,0},{64,32},{96,64},{1,97},{33,1},{65,33},{97,65},{2,98}... | collective-permute-start | bytes 589832 | tf_op jit(solution)/shard_map/ppermute | solution.py:206
  44.4 10.5 %collective-permute-start.15 = (bf16[96,1024]{1,0:T(8,128)(2,1)S(1)}, bf16[96,1024]{1,0:T(8,128)(2,1)S(1)}, u32[]{:S(2)}, u32[]{:S(2)}) collective-permute-start(bf16[96,1024]{1,0:T(8,128)(2,1)S(1)} %get-tuple-element.36), channel_id=1, source_target_pairs={{0,64},{32,96},{64,0},{96,32},{1,65},{33,97},{65,1},{97,33},{2,66}... | collective-permute-start | bytes 589832 | tf_op jit(solution)/shard_map/ppermute | solution.py:206
  49.8 14.9 %collective-permute-start.17 = (bf16[384,512]{1,0:T(8,128)(2,1)S(1)}, bf16[384,512]{1,0:T(8,128)(2,1)S(1)}, u32[]{:S(2)}, u32[]{:S(2)}) collective-permute-start(bf16[384,512]{1,0:T(8,128)(2,1)S(1)} %shard_map.69.refs_4_), channel_id=1, source_target_pairs={{0,1},{1,0},{2,3},{3,2},{4,5},{5,4},{6,7},{7,6},{8,9},{9,8},{10,11... | collective-permute-start | bytes 1179656 | tf_op jit(solution)/shard_map/ppermute | solution.py:202
  52.1 12.7 %collective-permute-start.21 = (bf16[384,512]{1,0:T(8,128)(2,1)S(1)}, bf16[384,512]{1,0:T(8,128)(2,1)S(1)}, u32[]{:S(2)}, u32[]{:S(2)}) collective-permute-start(bf16[384,512]{1,0:T(8,128)(2,1)S(1)} %collective-permute-done.20.refs_0_.refs_6_), channel_id=1, source_target_pairs={{0,1},{1,0},{2,3},{3,2},{4,5},{5,4},{6,7},{7,6},{8,9},{9,8},{10,11... | collective-permute-start | bytes 1179656 | tf_op jit(solution)/shard_map/ppermute | solution.py:202
  52.1 12.7 %collective-permute-start.19 = (bf16[384,512]{1,0:T(8,128)(2,1)S(1)}, bf16[384,512]{1,0:T(8,128)(2,1)S(1)}, u32[]{:S(2)}, u32[]{:S(2)}) collective-permute-start(bf16[384,512]{1,0:T(8,128)(2,1)S(1)} %collective-permute-done.18.refs_5_), channel_id=1, source_target_pairs={{0,1},{1,0},{2,3},{3,2},{4,5},{5,4},{6,7},{7,6},{8,9},{9,8},{10,11... | collective-permute-start | bytes 1179656 | tf_op jit(solution)/shard_map/ppermute | solution.py:202
  54.9 9.8 %collective-permute-start.25 = (bf16[384,512]{1,0:T(8,128)(2,1)S(1)}, bf16[384,512]{1,0:T(8,128)(2,1)S(1)}, u32[]{:S(2)}, u32[]{:S(2)}) collective-permute-start(bf16[384,512]{1,0:T(8,128)(2,1)S(1)} %shard_map.71), channel_id=1, source_target_pairs={{0,6},{2,0},{4,2},{6,4},{1,7},{3,1},{5,3},{7,5},{8,14},{10,8},{12,... | collective-permute-start | bytes 1179656 | tf_op jit(solution)/shard_map/ppermute | solution.py:206
  56.8 11.5 %collective-permute-start.16 = (bf16[96,1024]{1,0:T(8,128)(2,1)S(1)}, bf16[96,1024]{1,0:T(8,128)(2,1)S(1)}, u32[]{:S(2)}, u32[]{:S(2)}) collective-permute-start(bf16[96,1024]{1,0:T(8,128)(2,1)S(1)} %get-tuple-element.38), channel_id=1, source_target_pairs={{0,128},{128,0},{1,129},{129,1},{2,130},{130,2},{3,131},{131,3},{4... | collective-permute-start | bytes 589832 | tf_op jit(solution)/shard_map/ppermute | solution.py:253
  64.8 14.9 %collective-permute-start.26 = (bf16[384,512]{1,0:T(8,128)(2,1)S(1)}, bf16[384,512]{1,0:T(8,128)(2,1)S(1)}, u32[]{:S(2)}, u32[]{:S(2)}) collective-permute-start(bf16[384,512]{1,0:T(8,128)(2,1)S(1)} %collective-permute-done.25.refs_7_), channel_id=1, source_target_pairs={{0,1},{1,0},{2,3},{3,2},{4,5},{5,4},{6,7},{7,6},{8,9},{9,8},{10,11... | collective-permute-start | bytes 1179656 | tf_op jit(solution)/shard_map/ppermute | solution.py:202
  68.6 22.5 %copy-start.2 = (bf16[768,768]{1,0:T(8,128)(2,1)S(1)}, bf16[768,768]{1,0:T(8,128)(2,1)}, u32[]{:S(2)}) copy-start(bf16[768,768]{1,0:T(8,128)(2,1)} %refs_5_.1) | copy-start | bytes 3538948
  68.6 22.5 %copy-start.3 = (bf16[8,32,768]{2,1,0:T(8,128)(2,1)S(1)}, bf16[8,32,768]{2,1,0:T(8,128)(2,1)}, u32[]{:S(2)}) copy-start(bf16[8,32,768]{2,1,0:T(8,128)(2,1)} %param.6) | copy-start | bytes 1179652
  68.6 7.4 %collective-permute-start.22 = (bf16[96,1024]{1,0:T(8,128)(2,1)S(1)}, bf16[96,1024]{1,0:T(8,128)(2,1)S(1)}, u32[]{:S(2)}, u32[]{:S(2)}) collective-permute-start(bf16[96,1024]{1,0:T(8,128)(2,1)S(1)} %shard_map.70.refs_0_), channel_id=1, source_target_pairs={{0,32},{32,64},{64,96},{96,0},{1,33},{33,65},{65,97},{97,1},{2,34}... | collective-permute-start | bytes 589832 | tf_op jit(solution)/shard_map/ppermute | solution.py:206
  69.9 7.9 %collective-permute-start.23 = (bf16[96,1024]{1,0:T(8,128)(2,1)S(1)}, bf16[96,1024]{1,0:T(8,128)(2,1)S(1)}, u32[]{:S(2)}, u32[]{:S(2)}) collective-permute-start(bf16[96,1024]{1,0:T(8,128)(2,1)S(1)} %shard_map.70.refs_0_), channel_id=1, source_target_pairs={{0,64},{32,96},{64,0},{96,32},{1,65},{33,97},{65,1},{97,33},{2,66}... | collective-permute-start | bytes 589832 | tf_op jit(solution)/shard_map/ppermute | solution.py:206
  71.0 8.7 %collective-permute-start.24 = (bf16[96,1024]{1,0:T(8,128)(2,1)S(1)}, bf16[96,1024]{1,0:T(8,128)(2,1)S(1)}, u32[]{:S(2)}, u32[]{:S(2)}) collective-permute-start(bf16[96,1024]{1,0:T(8,128)(2,1)S(1)} %shard_map.70.refs_0_), channel_id=1, source_target_pairs={{0,96},{32,0},{64,32},{96,64},{1,97},{33,1},{65,33},{97,65},{2,98}... | collective-permute-start | bytes 589832 | tf_op jit(solution)/shard_map/ppermute | solution.py:206
  80.4 7.0 %collective-permute-start.27 = (bf16[384,128]{1,0:T(8,128)(2,1)S(1)}, bf16[384,128]{1,0:T(8,128)(2,1)S(1)}, u32[]{:S(2)}, u32[]{:S(2)}) collective-permute-start(bf16[384,128]{1,0:T(8,128)(2,1)S(1)} %get-tuple-element.40), channel_id=1, source_target_pairs={{0,8},{8,0},{16,24},{24,16},{1,9},{9,1},{17,25},{25,17},{2,10},{10... | collective-permute-start | bytes 294920 | tf_op jit(solution)/shard_map/ppermute | solution.py:197
  82.6 8.5 %collective-permute-start.28 = (bf16[384,128]{1,0:T(8,128)(2,1)S(1)}, bf16[384,128]{1,0:T(8,128)(2,1)S(1)}, u32[]{:S(2)}, u32[]{:S(2)}) collective-permute-start(bf16[384,128]{1,0:T(8,128)(2,1)S(1)} %get-tuple-element.41), channel_id=1, source_target_pairs={{0,16},{8,24},{16,0},{24,8},{1,17},{9,25},{17,1},{25,9},{2,18},{10... | collective-permute-start | bytes 294920 | tf_op jit(solution)/shard_map/ppermute | solution.py:197
  83.4 7.7 %collective-permute-start.29 = (bf16[384,128]{1,0:T(8,128)(2,1)S(1)}, bf16[384,128]{1,0:T(8,128)(2,1)S(1)}, u32[]{:S(2)}, u32[]{:S(2)}) collective-permute-start(bf16[384,128]{1,0:T(8,128)(2,1)S(1)} %get-tuple-element.42), channel_id=1, source_target_pairs={{0,24},{8,16},{16,8},{24,0},{1,25},{9,17},{17,9},{25,1},{2,26},{10... | collective-permute-start | bytes 294920 | tf_op jit(solution)/shard_map/ppermute | solution.py:197
  (2 other events, 15.0 us)
